TPU v7x, 32 devices: a whole 2x2x4 slice. The times are simulated.
32 devices in a mesh: ep: 16 (over z, x, core), tp: 2 (over y).
Axes of the slice: x: 2, y: 2, z: 4, core: 2. Of those that a mesh axis runs over, the one named last changes fastest.
Arguments:
- tokens: bfloat16 [8192, 1280], P(('ep', 'tp')), may hold values from -6 to 6
- cotangent: bfloat16 [8192, 1280], P(('ep', 'tp')), may hold values from -6 to 6
- segments: int32 [32, 256], P(('ep', 'tp')), may hold values from 0 to 3, never falling along the last dimension, each value on 1 to 128 neighbouring positions
- routes: int32 [8192, 7], P(('ep', 'tp')), may hold values from 0 to 15, all different within a row; in each aligned block of 256 rows (0 to 255, 256 to 511, ...) at most 128 rows name the same one
- gates: float32 [8192, 7], P(('ep', 'tp')), may hold values from 0.2 to 0.8
- qkv_weight: float32 [1280, 3840], P(('ep', 'tp')), may hold values from -0.15625 to 0.15625
- qkv_first: float32 [1280, 3840], P(('ep', 'tp')), may hold values from -0.00018310547 to 0.00018310547
- qkv_second: float32 [1280, 3840], P(('ep', 'tp')), may hold values from 3.5783887e-09 to 1.4178521e-08
- out_weight: float32 [1280, 1280], P(('ep', 'tp')), may hold values from -1 to 1
- out_first: float32 [1280, 1280], P(('ep', 'tp')), may hold values from -0.00018310547 to 0.00018310547
- out_second: float32 [1280, 1280], P(('ep', 'tp')), may hold values from 4.4561066e-10 to 1.7554359e-09
- shared_in: float32 [1280, 1792], P(('ep', 'tp')), may hold values from -0.15625 to 0.15625
- shared_in_first: float32 [1280, 1792], P(('ep', 'tp')), may hold values from -0.00018310547 to 0.00018310547
- shared_in_second: float32 [1280, 1792], P(('ep', 'tp')), may hold values from 3.5783887e-09 to 1.4178521e-08
- shared_out: float32 [896, 1280], P(('ep', 'tp')), may hold values from -0.1875 to 0.1875
- shared_out_first: float32 [896, 1280], P(('ep', 'tp')), may hold values from -0.00018310547 to 0.00018310547
- shared_out_second: float32 [896, 1280], P(('ep', 'tp')), may hold values from 7.1567774e-10 to 2.8357041e-09
- expert_in: float32 [16, 2, 896, 1280], P('ep', None, 'tp'), may hold values from -0.15625 to 0.15625
- expert_in_first: float32 [16, 2, 896, 1280], P('ep', None, 'tp'), may hold values from -5.340576e-05 to 5.340576e-05
- expert_in_second: float32 [16, 2, 896, 1280], P('ep', None, 'tp'), may hold values from 3.13109e-10 to 1.2406206e-09
- expert_out: float32 [16, 896, 1280], P('ep', 'tp'), may hold values from -0.6781754 to 0.6781754
- expert_out_first: float32 [16, 896, 1280], P('ep', 'tp'), may hold values from -5.340576e-05 to 5.340576e-05
- expert_out_second: float32 [16, 896, 1280], P('ep', 'tp'), may hold values from 3.13109e-10 to 1.2406206e-09
- norm_gains: float32 [2, 1280], P(None, ('ep', 'tp')), may hold values from 0.36 to 2.82
- gains_first: float32 [2, 1280], P(None, ('ep', 'tp')), may hold values from -0.0008544922 to 0.0008544922
- gains_second: float32 [2, 1280], P(None, ('ep', 'tp')), may hold values from 8.7771795e-08 to 3.5783887e-07
Outputs:
- block_out: bfloat16 [8192, 1280], P(('ep', 'tp'))
- tokens_grad: float32 [8192, 1280], P(('ep', 'tp'))
- grad_norm: float32 [], replicated
- qkv_new: float32 [1280, 3840], P(('ep', 'tp'))
- qkv_first_new: float32 [1280, 3840], P(('ep', 'tp'))
- qkv_second_new: float32 [1280, 3840], P(('ep', 'tp'))
- qkv_copy: bfloat16 [1280, 3840], P(('ep', 'tp'))
- out_new: float32 [1280, 1280], P(('ep', 'tp'))
- out_first_new: float32 [1280, 1280], P(('ep', 'tp'))
- out_second_new: float32 [1280, 1280], P(('ep', 'tp'))
- out_copy: bfloat16 [1280, 1280], P(('ep', 'tp'))
- shared_in_new: float32 [1280, 1792], P(('ep', 'tp'))
- shared_in_first_new: float32 [1280, 1792], P(('ep', 'tp'))
- shared_in_second_new: float32 [1280, 1792], P(('ep', 'tp'))
- shared_in_copy: bfloat16 [1280, 1792], P(('ep', 'tp'))
- shared_out_new: float32 [896, 1280], P(('ep', 'tp'))
- shared_out_first_new: float32 [896, 1280], P(('ep', 'tp'))
- shared_out_second_new: float32 [896, 1280], P(('ep', 'tp'))
- shared_out_copy: bfloat16 [896, 1280], P(('ep', 'tp'))
- expert_in_new: float32 [16, 2, 896, 1280], P('ep', None, 'tp')
- expert_in_first_new: float32 [16, 2, 896, 1280], P('ep', None, 'tp')
- expert_in_second_new: float32 [16, 2, 896, 1280], P('ep', None, 'tp')
- expert_in_copy: bfloat16 [16, 2, 896, 1280], P('ep', None, 'tp')
- expert_out_new: float32 [16, 896, 1280], P('ep', 'tp')
- expert_out_first_new: float32 [16, 896, 1280], P('ep', 'tp')
- expert_out_second_new: float32 [16, 896, 1280], P('ep', 'tp')
- expert_out_copy: bfloat16 [16, 896, 1280], P('ep', 'tp')
- gains_new: float32 [2, 1280], P(None, ('ep', 'tp'))
- gains_first_new: float32 [2, 1280], P(None, ('ep', 'tp'))
- gains_second_new: float32 [2, 1280], P(None, ('ep', 'tp'))
- gains_copy: bfloat16 [2, 1280], P(None, ('ep', 'tp'))
Inputs may be any that keep to these rules, and one draw needn't show every extreme that they name: `routes`: each row names 7 different experts; among the 256 rows of one device no expert is named more than 128 times, a bound that some block reaches. `segments`: along each row the document number never falls; each document holds 1 to 128 tokens, one exactly 128.
All inputs are finite; a program needn't handle non-finite values.
Results may differ from a plain program's by a relative error of at most 0.017.
The roundings to bfloat16 on the way count: a program that leaves them out, or rounds other values in their place, can miss the bound.
Values may be sent and summed in bfloat16 or wider, within the bound.
A program may use at most 384 MiB of HBM per device.

v0:
```python
import jax
import jax.numpy as jnp
from jax import lax
from jax.sharding import PartitionSpec as P

HEADS = 10
HDIM = 128
FF = 896
TOPK = 7
STEP = 10


NEG_BIG = -1000000000.0
NORM_EPS = 1e-06
ROPE_BASE = 10000.0
CLIP_LEVEL = 1.0
BETA_ONE = 0.9
BETA_TWO = 0.95
ADAM_EPS = 1e-08
WEIGHT_DECAY = 0.1
MATRIX_RATE = 0.05
GAIN_RATE = 0.5


def rope_tables(length):
    places = jnp.arange(length, dtype=jnp.float32)
    frequencies = ROPE_BASE ** (-jnp.arange(HDIM // 2, dtype=jnp.float32) * (2.0 / HDIM))
    angles = places[:, None] * frequencies[None, :]
    return (jnp.cos(angles)[:, None, :], jnp.sin(angles)[:, None, :])


def rotate(values, cosine, sine_table):
    middle = values.shape[-1] // 2
    former = values[..., :middle]
    latter = values[..., middle:]
    return jnp.concatenate(
        [former * cosine - latter * sine_table, latter * cosine + former * sine_table], axis=-1
    )


def unrotate(values, cosine, sine_table):
    middle = values.shape[-1] // 2
    former = values[..., :middle]
    latter = values[..., middle:]
    return jnp.concatenate(
        [former * cosine + latter * sine_table, latter * cosine - former * sine_table], axis=-1
    )


def norm_back(grad_normed, unit_values, factor, gain_values):
    grad_unit = grad_normed * gain_values
    gain_grad = jnp.sum(grad_normed * unit_values, axis=0)
    passed = factor * (
        grad_unit - unit_values * jnp.mean(grad_unit * unit_values, axis=-1, keepdims=True)
    )
    return (passed, gain_grad)


def swiglu_back(grad_act, gate_pre, up_pre):
    sigmoid_gate = jax.nn.sigmoid(gate_pre)
    grad_up = grad_act * gate_pre * sigmoid_gate
    grad_gate = grad_act * up_pre * sigmoid_gate * (1.0 + gate_pre * (1.0 - sigmoid_gate))
    return (grad_gate.astype(jnp.bfloat16), grad_up.astype(jnp.bfloat16))


def adam_update(weight, gradient, first, second, clip_scale, rate, decay):
    clipped = gradient * clip_scale
    first_new = BETA_ONE * first + (1.0 - BETA_ONE) * clipped
    second_new = BETA_TWO * second + (1.0 - BETA_TWO) * clipped * clipped
    corr_one = 1.0 - BETA_ONE**STEP
    corr_two = 1.0 - BETA_TWO**STEP
    stepped = first_new / corr_one / (jnp.sqrt(second_new / corr_two) + ADAM_EPS)
    weight_new = weight - rate * (stepped + decay * weight)
    return (weight_new, first_new, second_new, weight_new.astype(jnp.bfloat16))


def per_device(
    tokens,
    cotangent,
    segments,
    routes,
    gates,
    qkv_weight,
    qkv_first,
    qkv_second,
    out_weight,
    out_first,
    out_second,
    shared_in,
    shared_in_first,
    shared_in_second,
    shared_out,
    shared_out_first,
    shared_out_second,
    expert_in,
    expert_in_first,
    expert_in_second,
    expert_out,
    expert_out_first,
    expert_out_second,
    norm_gains,
    gains_first,
    gains_second,
):
    tok_count = tokens.shape[0]
    width = tokens.shape[1]
    ep_count = lax.axis_size("ep")
    capacity = tok_count * 8 // ep_count
    slot_total = ep_count * capacity
    pair_count = tok_count * TOPK
    gathered = (
        lax.all_gather(qkv_weight.astype(jnp.bfloat16), ("ep", "tp"), axis=0, tiled=True),
        lax.all_gather(out_weight.astype(jnp.bfloat16), ("ep", "tp"), axis=0, tiled=True),
        lax.all_gather(shared_in.astype(jnp.bfloat16), ("ep", "tp"), axis=0, tiled=True),
        lax.all_gather(shared_out.astype(jnp.bfloat16), ("ep", "tp"), axis=0, tiled=True),
        lax.all_gather(norm_gains.astype(jnp.bfloat16), ("ep", "tp"), axis=1, tiled=True),
    )
    qkv_low, out_low, shin_low, shout_low, gains_low = gathered
    gain_one = gains_low[0].astype(jnp.float32)
    gain_two = gains_low[1].astype(jnp.float32)
    experts_low = (expert_in.astype(jnp.bfloat16), expert_out.astype(jnp.bfloat16))
    in_low = experts_low[0][0]
    ex_out_low = experts_low[1][0]
    tok_float = tokens.astype(jnp.float32)
    factor_one = lax.rsqrt(jnp.mean(tok_float * tok_float, axis=-1, keepdims=True) + NORM_EPS)
    unit_one = tok_float * factor_one
    normed_one = (unit_one * gain_one).astype(jnp.bfloat16)
    projected = jnp.dot(normed_one, qkv_low, preferred_element_type=jnp.float32).reshape(
        tok_count, 3, HEADS, HDIM
    )
    cosine, sine_table = rope_tables(tok_count)
    queries = rotate(projected[:, 0], cosine, sine_table).astype(jnp.bfloat16)
    keys_low = rotate(projected[:, 1], cosine, sine_table).astype(jnp.bfloat16)
    values_low = projected[:, 2].astype(jnp.bfloat16)
    places = jnp.arange(tok_count)
    segment_row = segments[0]
    allowed = (places[:, None] >= places[None, :]) & (segment_row[:, None] == segment_row[None, :])
    score_scale = HDIM ** (-0.5)

    def masked_scores():
        raw = (
            jnp.einsum("shw,thw->hst", queries, keys_low, preferred_element_type=jnp.float32)
            * score_scale
        )
        return jnp.where(allowed[None], raw, NEG_BIG)

    scores = masked_scores()
    highest = jnp.max(scores, axis=-1, keepdims=True)
    log_total = highest + jnp.log(jnp.sum(jnp.exp(scores - highest), axis=-1, keepdims=True))
    probs_low = jnp.exp(scores - log_total).astype(jnp.bfloat16)
    attended = (
        jnp.einsum("hst,thw->shw", probs_low, values_low, preferred_element_type=jnp.float32)
        .reshape(tok_count, width)
        .astype(jnp.bfloat16)
    )
    hidden = tok_float + jnp.dot(attended, out_low, preferred_element_type=jnp.float32)
    factor_two = lax.rsqrt(jnp.mean(hidden * hidden, axis=-1, keepdims=True) + NORM_EPS)
    unit_two = hidden * factor_two
    normed_two = (unit_two * gain_two).astype(jnp.bfloat16)
    shared_pre = jnp.dot(normed_two, shin_low, preferred_element_type=jnp.float32)
    shared_act = (jax.nn.silu(shared_pre[:, :FF]) * shared_pre[:, FF:]).astype(jnp.bfloat16)
    shared_res = jnp.dot(shared_act, shout_low, preferred_element_type=jnp.float32)
    flat_routes = routes.reshape(pair_count)
    onehot = (flat_routes[:, None] == jnp.arange(ep_count, dtype=jnp.int32)[None, :]).astype(
        jnp.int32
    )
    slot_rank = jnp.sum((jnp.cumsum(onehot, axis=0) - onehot) * onehot, axis=1)
    positions = flat_routes * capacity + slot_rank
    slot_owner = (
        jnp.zeros((slot_total,), jnp.int32)
        .at[positions]
        .set(jnp.arange(pair_count, dtype=jnp.int32) + 1)
    )
    filled = (slot_owner > 0)[:, None]
    pair_index = jnp.maximum(slot_owner - 1, 0)
    token_index = pair_index // TOPK
    zero_low = jnp.zeros((), jnp.bfloat16)
    send_rows = jnp.where(filled, normed_two[token_index], zero_low).reshape(
        1, ep_count, capacity, width
    )
    arrived = lax.all_to_all(send_rows, "ep", split_axis=1, concat_axis=1, tiled=True)
    expert_rows = lax.all_gather(arrived, "tp", axis=0, tiled=True).reshape(-1, width)
    pre_both = jnp.einsum("rd,kfd->krf", expert_rows, in_low, preferred_element_type=jnp.float32)
    gate_pre = pre_both[0]
    up_pre = pre_both[1]
    expert_act = (jax.nn.silu(gate_pre) * up_pre).astype(jnp.bfloat16)
    piece = expert_act
    expert_result = lax.psum_scatter(
        jnp.dot(piece, ex_out_low, preferred_element_type=jnp.float32).astype(jnp.bfloat16),
        "tp",
        scatter_dimension=0,
        tiled=True,
    )
    returned = lax.all_to_all(
        expert_result.reshape(1, ep_count, capacity, width),
        "ep",
        split_axis=1,
        concat_axis=1,
        tiled=True,
    )
    pair_rows = returned.reshape(slot_total, width)[positions].reshape(tok_count, TOPK, width)
    routed = jnp.einsum("tk,tkd->td", gates, pair_rows, preferred_element_type=jnp.float32)
    block_out = (hidden + shared_res + routed).astype(jnp.bfloat16)
    grad_top = cotangent.astype(jnp.float32)
    flat_gates = gates.reshape(pair_count)
    slot_grad = jnp.where(
        filled,
        (flat_gates[pair_index][:, None] * grad_top[token_index]).astype(jnp.bfloat16),
        zero_low,
    )
    grad_arrived = lax.all_to_all(
        slot_grad.reshape(1, ep_count, capacity, width),
        "ep",
        split_axis=1,
        concat_axis=1,
        tiled=True,
    )
    grad_rows = lax.all_gather(grad_arrived, "tp", axis=0, tiled=True).reshape(-1, width)
    grad_act = jnp.einsum("rd,fd->rf", grad_rows, ex_out_low, preferred_element_type=jnp.float32)
    out_grad_expert = jnp.einsum(
        "rf,rd->fd", expert_act, grad_rows, preferred_element_type=jnp.float32
    )
    grad_gate, grad_up = swiglu_back(grad_act, gate_pre, up_pre)
    grad_pre = jnp.stack([grad_gate, grad_up])
    in_grad_expert = jnp.einsum(
        "krf,rd->kfd", grad_pre, expert_rows, preferred_element_type=jnp.float32
    )
    piece = grad_pre
    input_rows = lax.psum_scatter(
        jnp.einsum("krf,kfd->rd", piece, in_low, preferred_element_type=jnp.float32).astype(
            jnp.bfloat16
        ),
        "tp",
        scatter_dimension=0,
        tiled=True,
    )
    expert_grads = (in_grad_expert[None], out_grad_expert[None])
    input_back = lax.all_to_all(
        input_rows.reshape(1, ep_count, capacity, width),
        "ep",
        split_axis=1,
        concat_axis=1,
        tiled=True,
    )
    routed_grad = jnp.sum(
        input_back.reshape(slot_total, width)[positions].reshape(tok_count, TOPK, width),
        axis=1,
        dtype=jnp.float32,
    )
    grad_low = grad_top.astype(jnp.bfloat16)
    shout_grad = jnp.einsum("tf,td->fd", shared_act, grad_low, preferred_element_type=jnp.float32)
    grad_shared_act = jnp.einsum(
        "td,fd->tf", grad_low, shout_low, preferred_element_type=jnp.float32
    )
    grad_sh_gate, grad_sh_up = swiglu_back(grad_shared_act, shared_pre[:, :FF], shared_pre[:, FF:])
    grad_shared_pre = jnp.concatenate([grad_sh_gate, grad_sh_up], axis=1)
    shin_grad = jnp.einsum(
        "td,tf->df", normed_two, grad_shared_pre, preferred_element_type=jnp.float32
    )
    grad_normed_two = routed_grad + jnp.einsum(
        "tf,df->td", grad_shared_pre, shin_low, preferred_element_type=jnp.float32
    )
    passed_two, gain_two_grad = norm_back(grad_normed_two, unit_two, factor_two, gain_two)
    grad_hidden = grad_top + passed_two
    grad_branch = grad_hidden.astype(jnp.bfloat16)
    out_grad = jnp.einsum("td,te->de", attended, grad_branch, preferred_element_type=jnp.float32)
    grad_attended = (
        jnp.einsum("te,de->td", grad_branch, out_low, preferred_element_type=jnp.float32)
        .astype(jnp.bfloat16)
        .reshape(tok_count, HEADS, HDIM)
    )
    probabilities = jnp.exp(masked_scores() - log_total)
    grad_probs = jnp.einsum(
        "shw,thw->hst", grad_attended, values_low, preferred_element_type=jnp.float32
    )
    grad_values = jnp.einsum(
        "hst,shw->thw",
        probabilities.astype(jnp.bfloat16),
        grad_attended,
        preferred_element_type=jnp.float32,
    )
    row_dot = jnp.sum(probabilities * grad_probs, axis=-1, keepdims=True)
    grad_scores = (probabilities * (grad_probs - row_dot)).astype(jnp.bfloat16)
    grad_queries = (
        jnp.einsum("hst,thw->shw", grad_scores, keys_low, preferred_element_type=jnp.float32)
        * score_scale
    )
    grad_keys = (
        jnp.einsum("hst,shw->thw", grad_scores, queries, preferred_element_type=jnp.float32)
        * score_scale
    )
    grad_proj = jnp.stack(
        [
            unrotate(grad_queries, cosine, sine_table),
            unrotate(grad_keys, cosine, sine_table),
            grad_values,
        ],
        axis=1,
    )
    grad_proj = grad_proj.reshape(tok_count, 3 * width).astype(jnp.bfloat16)
    qkv_grad = jnp.einsum("td,te->de", normed_one, grad_proj, preferred_element_type=jnp.float32)
    grad_normed_one = jnp.einsum(
        "te,de->td", grad_proj, qkv_low, preferred_element_type=jnp.float32
    )
    passed_one, gain_one_grad = norm_back(grad_normed_one, unit_one, factor_one, gain_one)
    tokens_grad = grad_hidden + passed_one
    gains_grad = jnp.stack([gain_one_grad, gain_two_grad])
    dense_grads = (
        lax.psum_scatter(qkv_grad, ("ep", "tp"), scatter_dimension=0, tiled=True),
        lax.psum_scatter(out_grad, ("ep", "tp"), scatter_dimension=0, tiled=True),
        lax.psum_scatter(shin_grad, ("ep", "tp"), scatter_dimension=0, tiled=True),
        lax.psum_scatter(shout_grad, ("ep", "tp"), scatter_dimension=0, tiled=True),
        lax.psum_scatter(gains_grad, ("ep", "tp"), scatter_dimension=1, tiled=True),
    )
    qkv_part, out_part, shin_part, shout_part, gains_part = dense_grads
    exin_part, exout_part = expert_grads
    squares = (
        jnp.sum(qkv_part * qkv_part) + jnp.sum(out_part * out_part) + jnp.sum(shin_part * shin_part)
    )
    squares = squares + jnp.sum(shout_part * shout_part) + jnp.sum(exin_part * exin_part)
    squares = squares + jnp.sum(exout_part * exout_part) + jnp.sum(gains_part * gains_part)
    grad_norm = jnp.sqrt(lax.psum(squares, ("ep", "tp")))
    clip_scale = jnp.minimum(1.0, CLIP_LEVEL / (grad_norm + 1e-06))
    qkv_new, qkv_first_new, qkv_second_new, qkv_copy = adam_update(
        qkv_weight, qkv_part, qkv_first, qkv_second, clip_scale, MATRIX_RATE, WEIGHT_DECAY
    )
    out_new, out_first_new, out_second_new, out_copy = adam_update(
        out_weight, out_part, out_first, out_second, clip_scale, MATRIX_RATE, WEIGHT_DECAY
    )
    shin_new, shin_first_new, shin_second_new, shin_copy = adam_update(
        shared_in,
        shin_part,
        shared_in_first,
        shared_in_second,
        clip_scale,
        MATRIX_RATE,
        WEIGHT_DECAY,
    )
    shout_new, shout_first_new, shout_second_new, shout_copy = adam_update(
        shared_out,
        shout_part,
        shared_out_first,
        shared_out_second,
        clip_scale,
        MATRIX_RATE,
        WEIGHT_DECAY,
    )
    exin_new, exin_first_new, exin_second_new, exin_copy = adam_update(
        expert_in,
        exin_part,
        expert_in_first,
        expert_in_second,
        clip_scale,
        MATRIX_RATE,
        WEIGHT_DECAY,
    )
    exout_new, exout_first_new, exout_second_new, exout_copy = adam_update(
        expert_out,
        exout_part,
        expert_out_first,
        expert_out_second,
        clip_scale,
        MATRIX_RATE,
        WEIGHT_DECAY,
    )
    gains_new, gains_first_new, gains_second_new, gains_copy = adam_update(
        norm_gains, gains_part, gains_first, gains_second, clip_scale, GAIN_RATE, 0.0
    )
    return (
        block_out,
        tokens_grad,
        grad_norm,
        qkv_new,
        qkv_first_new,
        qkv_second_new,
        qkv_copy,
        out_new,
        out_first_new,
        out_second_new,
        out_copy,
        shin_new,
        shin_first_new,
        shin_second_new,
        shin_copy,
        shout_new,
        shout_first_new,
        shout_second_new,
        shout_copy,
        exin_new,
        exin_first_new,
        exin_second_new,
        exin_copy,
        exout_new,
        exout_first_new,
        exout_second_new,
        exout_copy,
        gains_new,
        gains_first_new,
        gains_second_new,
        gains_copy,
    )


def solution(mesh):
    placed = (
        P(("ep", "tp"), None),
        P(("ep", "tp"), None),
        P(("ep", "tp"), None),
        P(("ep", "tp"), None),
        P(("ep", "tp"), None),
        P(("ep", "tp"), None),
        P(("ep", "tp"), None),
        P(("ep", "tp"), None),
        P(("ep", "tp"), None),
        P(("ep", "tp"), None),
        P(("ep", "tp"), None),
        P(("ep", "tp"), None),
        P(("ep", "tp"), None),
        P(("ep", "tp"), None),
        P(("ep", "tp"), None),
        P(("ep", "tp"), None),
        P(("ep", "tp"), None),
        P("ep", None, "tp", None),
        P("ep", None, "tp", None),
        P("ep", None, "tp", None),
        P("ep", "tp", None),
        P("ep", "tp", None),
        P("ep", "tp", None),
        P(None, ("ep", "tp")),
        P(None, ("ep", "tp")),
        P(None, ("ep", "tp")),
    )
    return jax.shard_map(
        per_device,
        mesh=mesh,
        in_specs=placed,
        out_specs=(
            P(("ep", "tp"), None),
            P(("ep", "tp"), None),
            P(),
            P(("ep", "tp"), None),
            P(("ep", "tp"), None),
            P(("ep", "tp"), None),
            P(("ep", "tp"), None),
            P(("ep", "tp"), None),
            P(("ep", "tp"), None),
            P(("ep", "tp"), None),
            P(("ep", "tp"), None),
            P(("ep", "tp"), None),
            P(("ep", "tp"), None),
            P(("ep", "tp"), None),
            P(("ep", "tp"), None),
            P(("ep", "tp"), None),
            P(("ep", "tp"), None),
            P(("ep", "tp"), None),
            P(("ep", "tp"), None),
            P("ep", None, "tp", None),
            P("ep", None, "tp", None),
            P("ep", None, "tp", None),
            P("ep", None, "tp", None),
            P("ep", "tp", None),
            P("ep", "tp", None),
            P("ep", "tp", None),
            P("ep", "tp", None),
            P(None, ("ep", "tp")),
            P(None, ("ep", "tp")),
            P(None, ("ep", "tp")),
            P(None, ("ep", "tp")),
        ),
        check_vma=False,
    )
```

profile of v0, /device:TPU:0, one launch (start us, length us, event | category | flops | bytes accessed | tf_op | source)
XLA Modules:
  0.0 1720.6 jit_solution(1781933786425982399)
XLA Ops:
  12.8 69.9 %all-gather = bf16[32,40,2]{1,2,0:T(2,128)(2,1)S(1)} all-gather(bf16[1,40,2]{1,2,0:T(2,128)(2,1)S(1)} %convert_bitcast_fusion.1), channel_id=1, replica_groups=mesh['ep'=16,'tp'=2] {'ep','tp'}, dimensions={0}, use_global_device_ids=true | all-gather | bytes 5280 | tf_op jit(solution)/shard_map/all_gather | solution.py:116
  97.1 11.8 gather_fusion.2
  108.9 10.5 gather_fusion.3
  139.3 20.2 %all-gather.11.cloned.1.call-done = bf16[1280,1280]{1,0:T(8,128)(2,1)} async-done(((bf16[40,1280]{1,0:T(8,128)(2,1)}), bf16[1280,1280]{1,0:T(8,128)(2,1)}) %all-gather.11.cloned.1.call-update) | async-done | bytes 3276816 | tf_op jit(solution)/shard_map/all_gather | solution.py:113
  162.8 10.0 gather_fusion
  172.7 8.0 fusion.10
  180.8 119.1 %all_to_all.20 = bf16[1,16,128,1280]{3,2,0,1:T(8,128)(2,1)} all-to-all(bf16[1,16,128,1280]{3,2,0,1:T(8,128)(2,1)S(1)} %get-tuple-element.87), channel_id=1, replica_groups=mesh['ep'=16,'tp'=2] {'ep'}, dimensions={1} | all-to-all | bytes 10485760 | tf_op jit(solution)/shard_map/all_to_all | solution.py:181
  299.9 120.2 %all_to_all.21 = bf16[1,16,128,1280]{3,2,0,1:T(8,128)(2,1)} all-to-all(bf16[1,16,128,1280]{3,2,0,1:T(8,128)(2,1)} %get-tuple-element.86), channel_id=1, replica_groups=mesh['ep'=16,'tp'=2] {'ep'}, dimensions={1} | all-to-all | bytes 10485760 | tf_op jit(solution)/shard_map/all_to_all | solution.py:211
  429.4 16.9 convolution_bitcast_fusion
  446.2 114.1 %all-gather.17.cloned.1.call-done = bf16[2,16,128,1280]{3,2,1,0:T(8,128)(2,1)} async-done(((bf16[1,16,128,1280]{3,2,1,0:T(8,128)(2,1)}), bf16[2,16,128,1280]{3,2,1,0:T(8,128)(2,1)}) %all-gather.17.cloned.1.call-update) | async-done | bytes 10485776 | tf_op jit(solution)/shard_map/all_gather | solution.py:218
  560.3 13.3 fusion.18
  576.7 15.6 bitcast_convert_fusion
  600.9 8.2 convolution_convert_fusion
  609.2 12.5 all-gather.19.cloned.1.call-done
  625.8 61.9 %all-gather.13.cloned.1.call-done = bf16[1280,1792]{1,0:T(8,128)(2,1)} async-done(((bf16[40,1792]{1,0:T(8,128)(2,1)}), bf16[1280,1792]{1,0:T(8,128)(2,1)}) %all-gather.13.cloned.1.call-update) | async-done | bytes 4587536 | tf_op jit(solution)/shard_map/all_gather | solution.py:114
  699.1 111.1 %reduce-scatter.11.cloned.1.call-done = bf16[2048,1280]{1,0:T(8,128)(2,1)} async-done(((bf16[4096,1280]{1,0:T(8,128)(2,1)}), bf16[2048,1280]{1,0:T(8,128)(2,1)}) %reduce-scatter.11.cloned.1.call-update) | async-done | bytes 5242896 | tf_op jit(solution)/shard_map/reduce_scatter | solution.py:229
  816.5 95.4 %all-to-all-done.3 = bf16[1,16,128,1280]{3,2,0,1:T(8,128)(2,1)} async-done(((bf16[1,16,128,1280]{3,2,0,1:T(8,128)(2,1)}), bf16[1,16,128,1280]{3,2,0,1:T(8,128)(2,1)}, u32[]{:S(2)}, u32[]{:S(2)}) %all-to-all-start.3) | async-done | bytes 5242912 | tf_op jit(solution)/shard_map/all_to_all | solution.py:238
  911.9 13.5 gather_fusion.4
  925.5 8.0 reshape.340
  933.5 8.3 reduce_sum.160
  971.2 8.5 fusion.60
  979.7 23.5 %all-to-all-start.1 = ((bf16[1,16,128,1280]{3,2,0,1:T(8,128)(2,1)}), bf16[1,16,128,1280]{3,2,0,1:T(8,128)(2,1)}, u32[]{:S(2)}, u32[]{:S(2)}) async-start(bf16[1,16,128,1280]{3,2,0,1:T(8,128)(2,1)} %bitcast.201), calls=%async_computation.2 | async-start | bytes 10485760 | tf_op jit(solution)/shard_map/all_to_all | solution.py:194
  1007.3 273.3 %fusion = f32[32,1280]{1,0:T(8,128)S(1)} fusion(f32[896,1280]{1,0:T(8,128)} %fusion.109), kind=kCustom, calls=%all-reduce-scatter | all-reduce-scatter fusion | flops 1310721 | bytes 4751360
  1292.8 15.3 collective-permute-start.3
  1320.1 12.2 multiply_reduce_fusion.2
  1332.3 16.2 multiply_reduce_fusion
  1352.6 13.7 gather_fusion.1
  1373.8 69.2 %all-reduce.1 = f32[2,1280]{1,0:T(2,128)S(1)} all-reduce(f32[2,1280]{1,0:T(2,128)S(1)} %pad_maximum_fusion.13), channel_id=8, replica_groups=mesh['ep'=16,'tp'=2] {'ep','tp'}, use_global_device_ids=true, to_apply=%region_26.27.clone | all-reduce | flops 2560 | bytes 20480
  1452.4 185.6 %reduce-scatter.13.cloned.1.call-done = f32[40,3840]{1,0:T(8,128)} async-done(((f32[1280,3840]{1,0:T(8,128)}), f32[40,3840]{1,0:T(8,128)}) %reduce-scatter.13.cloned.1.call-update) | async-done | bytes 614416 | tf_op jit(solution)/shard_map/reduce_scatter | solution.py:309
  1648.3 39.2 %psum.7 = f32[]{:T(128)} all-reduce(f32[]{:T(128)S(6)} %add.280), channel_id=1, replica_groups=mesh['ep'=16,'tp'=2] {'ep','tp'}, use_global_device_ids=true, to_apply=%region_28.29 | all-reduce | flops 1 | bytes 8 | tf_op jit(solution)/shard_map/psum | solution.py:322
  1690.9 8.2 fusion.92
  1699.3 9.4 fusion.94
  (292 shorter events, 176.0 us)
Async XLA Ops:
  7.2 81.8 %copy-start.61 = (f32[256,7]{0,1:T(8,128)S(1)}, f32[256,7]{0,1:T(8,128)}, u32[]{:S(2)}) copy-start(f32[256,7]{0,1:T(8,128)} %param.30) | copy-start | bytes 21508
  7.2 82.2 %copy-start.10 = (bf16[256,1280]{1,0:T(8,128)(2,1)S(1)}, bf16[256,1280]{1,0:T(8,128)(2,1)}, u32[]{:S(2)}) copy-start(bf16[256,1280]{1,0:T(8,128)(2,1)} %param.27) | copy-start | bytes 1966084
  7.2 113.8 %all-gather.9.cloned.1.call-start = ((), (), s32[]{:S(2)}) async-start(), calls=%async_computation.9 | async-start | bytes 10137600 | tf_op jit(solution)/shard_map/all_gather | solution.py:112
  9.2 150.3 %all-gather.11.cloned.1.call-start = ((), (), s32[]{:S(2)}) async-start(), calls=%async_computation.10 | async-start | bytes 3379200 | tf_op jit(solution)/shard_map/all_gather | solution.py:113
  10.8 418.5 %all-gather.15.cloned.1.call-start = ((), (), s32[]{:S(2)}) async-start(), calls=%async_computation.12 | async-start | bytes 15728640 | tf_op jit(solution)/shard_map/all_gather | solution.py:182
  162.6 783.7 %copy-start.2 = (f32[256,1280]{1,0:T(8,128)}, f32[256,1280]{1,0:T(8,128)S(1)}, u32[]{:S(2)}) copy-start(f32[256,1280]{1,0:T(8,128)S(1)} %get-tuple-element.93) | copy-start | bytes 3932164
  299.9 260.4 %all-gather.17.cloned.1.call-start = ((), (), s32[]{:S(2)}) async-start(), calls=%async_computation.14 | async-start | bytes 15728640 | tf_op jit(solution)/shard_map/all_gather | solution.py:218
  420.2 201.6 %all-gather.19.cloned.1.call-start = ((), (), s32[]{:S(2)}) async-start(), calls=%async_computation.19 | async-start | bytes 2703360 | tf_op jit(solution)/shard_map/all_gather | solution.py:115
  421.7 266.0 %all-gather.13.cloned.1.call-start = ((), (), s32[]{:S(2)}) async-start(), calls=%async_computation.11 | async-start | bytes 4730880 | tf_op jit(solution)/shard_map/all_gather | solution.py:114
  422.5 387.7 %reduce-scatter.11.cloned.1.call-start = ((), (), s32[]{:S(2)}) async-start(), calls=%async_computation.15 | async-start | bytes 15728640 | tf_op jit(solution)/shard_map/reduce_scatter | solution.py:229
  592.3 387.5 %reduce-scatter.9.cloned.1.call-start = ((), (), s32[]{:S(2)}) async-start(), calls=%async_computation.13 | async-start | bytes 15728640 | tf_op jit(solution)/shard_map/reduce_scatter | solution.py:188
  609.2 709.3 %reduce-scatter.17.cloned.1.call-start = ((), (), s32[]{:S(2)}) async-start(), calls=%async_computation.18 | async-start | bytes 9461760 | tf_op jit(solution)/shard_map/reduce_scatter | solution.py:311
  625.8 65.7 %copy-start.11 = (bf16[256,1280]{1,0:T(8,128)(2,1)S(1)}, bf16[256,1280]{1,0:T(8,128)(2,1)}, u32[]{:S(2)}) copy-start(bf16[256,1280]{1,0:T(8,128)(2,1)} %param.27) | copy-start | bytes 1966084
  810.2 101.7 %all-to-all-start.3 = ((bf16[1,16,128,1280]{3,2,0,1:T(8,128)(2,1)}), bf16[1,16,128,1280]{3,2,0,1:T(8,128)(2,1)}, u32[]{:S(2)}, u32[]{:S(2)}) async-start(bf16[1,16,128,1280]{3,2,0,1:T(8,128)(2,1)} %bitcast.202), calls=%async_computation.5 | async-start | bytes 10485760 | tf_op jit(solution)/shard_map/all_to_all | solution.py:238
  816.0 634.8 %reduce-scatter.15.cloned.1.call-start = ((), (), s32[]{:S(2)}) async-start(), calls=%async_computation.17 | async-start | bytes 6758400 | tf_op jit(solution)/shard_map/reduce_scatter | solution.py:310
  951.4 686.6 %reduce-scatter.13.cloned.1.call-start = ((), (), s32[]{:S(2)}) async-start(), calls=%async_computation.16 | async-start | bytes 20275200 | tf_op jit(solution)/shard_map/reduce_scatter | solution.py:309
  979.7 372.9 %all-to-all-start.1 = ((bf16[1,16,128,1280]{3,2,0,1:T(8,128)(2,1)}), bf16[1,16,128,1280]{3,2,0,1:T(8,128)(2,1)}, u32[]{:S(2)}, u32[]{:S(2)}) async-start(bf16[1,16,128,1280]{3,2,0,1:T(8,128)(2,1)} %bitcast.201), calls=%async_computation.2 | async-start | bytes 10485760 | tf_op jit(solution)/shard_map/all_to_all | solution.py:194
  1007.3 300.8 %copy-start.62 = (f32[256,7]{0,1:T(8,128)S(1)}, f32[256,7]{0,1:T(8,128)}, u32[]{:S(2)}) copy-start(f32[256,7]{0,1:T(8,128)} %param.30) | copy-start | bytes 21508
  1280.6 30.7 %collective-permute-start.2 = (f32[32,1280]{1,0:T(8,128)S(1)}, f32[32,1280]{1,0:T(8,128)S(1)}, u32[]{:S(2)}, u32[]{:S(2)}) collective-permute-start(f32[32,1280]{1,0:T(8,128)S(1)} %fusion), channel_id=1, source_target_pairs={{0,3},{1,4},{2,5},{3,6},{4,7},{5,8},{6,9},{7,10},{8,11},{9,12},{10... | collective-permute-start | bytes 491528
  1283.5 27.7 %collective-permute-start.1 = (f32[32,1280]{1,0:T(8,128)S(1)}, f32[32,1280]{1,0:T(8,128)S(1)}, u32[]{:S(2)}, u32[]{:S(2)}) collective-permute-start(f32[32,1280]{1,0:T(8,128)S(1)} %fusion), channel_id=1, source_target_pairs={{0,2},{1,3},{2,4},{3,5},{4,6},{5,7},{6,8},{7,9},{8,10},{9,11},{10,... | collective-permute-start | bytes 491528
  1289.5 23.2 %collective-permute-start = (f32[32,1280]{1,0:T(8,128)S(1)}, f32[32,1280]{1,0:T(8,128)}, u32[]{:S(2)}, u32[]{:S(2)}) collective-permute-start(f32[32,1280]{1,0:T(8,128)S(1)} %fusion), channel_id=1, source_target_pairs={{0,1},{1,2},{2,3},{3,4},{4,5},{5,6},{6,7},{7,8},{8,9},{9,10},{10,1... | collective-permute-start | bytes 491528
  1292.8 18.4 %collective-permute-start.3 = (f32[28,1280]{1,0:T(8,128)S(1)}, f32[28,1280]{1,0:T(8,128)S(1)}, u32[]{:S(2)}, u32[]{:S(2)}) collective-permute-start(f32[28,1280]{1,0:T(8,128)S(1)} %slice.108), channel_id=1, source_target_pairs={{0,4},{1,5},{2,6},{3,7},{4,8},{5,9},{6,10},{7,11},{8,12},{9,13},{1... | collective-permute-start | bytes 430088
  1366.3 77.4 %copy-start.45 = (bf16[256,7,1]{1,2,0:T(2,128)(2,1)S(1)}, bf16[256,7,1]{1,2,0:T(2,128)(2,1)}, u32[]{:S(2)}) copy-start(bf16[256,7,1]{1,2,0:T(2,128)(2,1)} %copy.122) | copy-start | bytes 10756
  1449.3 195.0 %copy-start.3 = (f32[256,1280]{1,0:T(8,128)S(1)}, f32[256,1280]{1,0:T(8,128)}, u32[]{:S(2)}) copy-start(f32[256,1280]{1,0:T(8,128)} %copy-done.2) | copy-start | bytes 3932164
  1449.3 195.1 %copy-start.23 = (bf16[256,896]{1,0:T(8,128)(2,1)S(1)}, bf16[256,896]{1,0:T(8,128)(2,1)}, u32[]{:S(2)}) copy-start(bf16[256,896]{1,0:T(8,128)(2,1)} %get-tuple-element.71) | copy-start | bytes 1376260
  1644.4 43.8 %copy-start.42 = (f32[28,1280]{1,0:T(8,128)S(1)}, f32[28,1280]{1,0:T(8,128)}, u32[]{:S(2)}) copy-start(f32[28,1280]{1,0:T(8,128)} %param.40) | copy-start | bytes 430084
  1644.4 43.8 %copy-start.54 = (f32[28,1280]{1,0:T(8,128)S(1)}, f32[28,1280]{1,0:T(8,128)}, u32[]{:S(2)}) copy-start(f32[28,1280]{1,0:T(8,128)} %param.41) | copy-start | bytes 430084
  1644.4 43.8 %copy-start.55 = (f32[28,1280]{1,0:T(8,128)S(1)}, f32[28,1280]{1,0:T(8,128)}, u32[]{:S(2)}) copy-start(f32[28,1280]{1,0:T(8,128)} %param.42) | copy-start | bytes 430084
  1644.4 45.8 %copy-start.68 = (f32[2,40]{1,0:T(2,128)S(1)}, f32[2,40]{1,0:T(2,128)}, u32[]{:S(2)}) copy-start(f32[2,40]{1,0:T(2,128)} %param.49) | copy-start | bytes 964
  1644.4 45.8 %copy-start.69 = (f32[2,40]{1,0:T(2,128)S(1)}, f32[2,40]{1,0:T(2,128)}, u32[]{:S(2)}) copy-start(f32[2,40]{1,0:T(2,128)} %param.50) | copy-start | bytes 964
  1644.5 45.8 %copy-start.70 = (f32[2,40]{1,0:T(2,128)S(1)}, f32[2,40]{1,0:T(2,128)}, u32[]{:S(2)}) copy-start(f32[2,40]{1,0:T(2,128)} %param.51) | copy-start | bytes 964
  1644.5 54.7 %slice-start = ((s8[4587520]{0:T(1024)(128)(4,1)}), s8[393216]{0:T(1024)(128)(4,1)S(1)}, s32[]{:S(2)}) async-start(s8[4587520]{0:T(1024)(128)(4,1)} %bitcast.203), calls=%async_computation.20 | async-start | bytes 786432
  (67 other events, 486.4 us)
Sparse Core Ops, SparseCore 0:
  11.5 86.5 all-gather.8
  101.5 57.8 all-gather.10
  300.0 129.3 all-gather.14
  430.8 129.5 all-gather.16
  563.6 58.0 all-gather.18
  625.1 62.5 all-gather.12
  690.0 120.1 reduce-scatter.10
  812.5 121.8 reduce-scatter.8
  936.7 277.5 reduce-scatter.16
  1216.4 194.0 reduce-scatter.14
  1416.9 221.0 reduce-scatter.12
where the time goes:
time: 1720 us
  blocking collectives  691 us (40%)
  waiting for transfers between devices  610 us (35%)
  matrix products  149 us (9%)
  local copies, waits for them, and re-layouts  116 us (7%)
  other arithmetic  74.4 us (4%)
  starting transfers between devices  58.4 us (3%)
  between operations  21.9 us (1%)
    unnamed x2, blocking collectives  342 us
    reduce_scatter x1, waiting for transfers between devices, per_device(): lax.psum_scatter(qkv_grad, ('ep', 'tp'), scatter_dimension=0, tiled=True)  186 us
    all_to_all x1, blocking collectives, per_device(): lax.all_to_all(slot_grad.reshape(1, ep_count, capacity, width), 'ep', spl...  120 us
    all_to_all x1, blocking collectives, per_device(): lax.all_to_all(send_rows, 'ep', split_axis=1, concat_axis=1, tiled=True)  119 us
    all_gather x1, waiting for transfers between devices, per_device(): lax.all_gather(grad_arrived, 'tp', axis=0, tiled=True).reshape(-1, width)  114 us
    reduce_scatter x1, waiting for transfers between devices, per_device(): lax.psum_scatter(jnp.einsum('krf,kfd->rd', piece, in_low, preferred_eleme...  111 us
    all_to_all x1, waiting for transfers between devices, per_device(): lax.all_to_all(input_rows.reshape(1, ep_count, capacity, width), 'ep', sp...  95.4 us
    all_gather x1, blocking collectives, per_device(): lax.all_gather(norm_gains.astype(jnp.bfloat16), ('ep', 'tp'), axis=1, til...  69.9 us
  transfers between devices with their start and end apart: 17, of which 9 were waited for; matrix products, arithmetic and copies ran while one was open for 32% of the time, Pallas kernels for 0%

commit v1 on v0

--- a/solution.py
+++ b/solution.py
@@ -1,6 +1,9 @@
+import functools
 import jax
 import jax.numpy as jnp
 from jax import lax
+from jax.experimental import pallas as pl
+from jax.experimental.pallas import tpu as pltpu
 from jax.sharding import PartitionSpec as P
 
 HEADS = 10
@@ -10,6 +13,8 @@
 STEP = 10
 
 
+MESH = pl.DeviceIdType.MESH
+VMEM_MOST = 60 * 1024 * 1024
 NEG_BIG = -1000000000.0
 NORM_EPS = 1e-06
 ROPE_BASE = 10000.0
@@ -20,6 +25,622 @@
 WEIGHT_DECAY = 0.1
 MATRIX_RATE = 0.05
 GAIN_RATE = 0.5
+
+
+class Place:
+    def __init__(self, ep_count, tp_count):
+        chips = ep_count // 2
+        nb = 1
+        while nb * nb * 4 <= chips:
+            nb *= 2
+        self.nb, self.na, self.nt = nb, chips // nb, tp_count
+        self.ep_count = ep_count
+        e = lax.axis_index("ep")
+        self.t = lax.axis_index("tp")
+        self.core = lax.rem(e, 2)
+        self.b = lax.rem(e // 2, nb)
+        self.a = e // (2 * nb)
+
+    def dims(self, whole):
+        if not whole:
+            return (("a", self.na), ("b", self.nb))
+        if self.nb == self.nt:
+            return (("a", self.na), ("u", self.nb), ("v", self.nt))
+        return (("a", self.na), ("b", self.nb), ("t", self.nt))
+
+    def own(self, name):
+        even = self.core == 0
+        if name == "u":
+            return jnp.where(even, self.b, self.t)
+        if name == "v":
+            return jnp.where(even, self.t, self.b)
+        return getattr(self, name)
+
+    def chip(self, at):
+        a = at.get("a", self.a)
+        b, t = at.get("b", self.b), at.get("t", self.t)
+        if "u" in at:
+            even = self.core == 0
+            b = jnp.where(even, at["u"], at["v"])
+            t = jnp.where(even, at["v"], at["u"])
+        return a, b, t
+
+    def device(self, at, core):
+        a, b, t = self.chip(at)
+        return ((a * self.nb + b) * 2 + core, t)
+
+    def index(self, at, core, whole):
+        e, t = self.device(at, core)
+        return e * self.nt + t if whole else e
+
+    def slot(self, at, whole):
+        a, b, t = self.chip(at)
+        chip = a * self.nb + b
+        return chip * self.nt + t if whole else chip
+
+
+def shifts(extent):
+    if extent == 2:
+        return [0, 1]
+    found = [0]
+    for step in range(1, extent):
+        found += [step, -step]
+    return found
+
+
+def moved(own, shift, extent):
+    if shift == 0:
+        return own, None
+    if extent == 2:
+        return 1 - own, None
+    there = own + shift
+    return there, (there >= 0) & (there < extent)
+
+
+def both(one, other):
+    if one is None:
+        return other
+    return one if other is None else one & other
+
+
+def guarded(condition, body):
+    if condition is None:
+        body()
+    else:
+        pl.when(condition)(body)
+
+
+def sides(extent):
+    return [1] if extent == 2 else [1, -1]
+
+
+def greet(place, whole):
+    barrier = pltpu.get_barrier_semaphore()
+    here = {name: place.own(name) for name, _ in place.dims(whole)}
+    pl.semaphore_signal(barrier, inc=1, device_id=place.device(here, 1 - place.core), device_id_type=MESH)
+    count = jnp.int32(1)
+    for name, extent in place.dims(whole):
+        for side in sides(extent):
+            there, on = moved(here[name], side, extent)
+            target = place.device({**here, name: there}, place.core)
+
+            def signal(target=target):
+                pl.semaphore_signal(barrier, inc=1, device_id=target, device_id_type=MESH)
+
+            guarded(on, signal)
+            count = count + (1 if on is None else on.astype(jnp.int32))
+    pl.semaphore_wait(barrier, count)
+
+
+def relative_blocks(dims):
+    blocks = [()]
+    for _, extent in dims:
+        blocks = [block + (shift,) for block in blocks for shift in shifts(extent)]
+    return blocks
+
+
+def gather_events(place, whole, pairs, send_sems, recv_sems):
+    dims = place.dims(whole)
+    here = {name: place.own(name) for name, _ in dims}
+    counter = [0]
+    ends = []
+    starts = []
+
+    def copies(at, target, core_of_block, own):
+        index = place.index(at, core_of_block, whole)
+        number = counter[0]
+        counter[0] += 1
+        made = []
+        for k, (block, gathered) in enumerate(pairs):
+            made.append(
+                pltpu.make_async_remote_copy(
+                    src_ref=block if own else gathered.at[index],
+                    dst_ref=gathered.at[index],
+                    send_sem=send_sems.at[k, number],
+                    recv_sem=recv_sems.at[k, index],
+                    device_id=target,
+                    device_id_type=MESH,
+                )
+            )
+        return made
+
+    def send(at, on, target, own, todo):
+        made = copies(at, target, place.core, own)
+
+        def start(made=made):
+            for copy in made:
+                copy.start()
+
+        def finish(made=made):
+            for copy in made:
+                copy.wait_send()
+
+        todo.append((on, start))
+        ends.append((on, finish))
+
+    steps = []
+    for block in relative_blocks(dims):
+        at, valid = dict(here), None
+        for (name, extent), shift in zip(dims, block):
+            at[name], on = moved(here[name], shift, extent)
+            valid = both(valid, on)
+        last = max([k for k, shift in enumerate(block) if shift], default=-1)
+        own = last < 0
+        todo = []
+        for k in range(len(dims) - 1, -1, -1):
+            name, extent = dims[k]
+            if k < last:
+                continue
+            if k == last:
+                if extent == 2:
+                    continue
+                ways = [-1 if block[k] > 0 else 1]
+            else:
+                ways = sides(extent)
+            for way in ways:
+                there, on = moved(here[name], way, extent)
+                target = place.device({**here, name: there}, place.core)
+                send(at, both(valid, on), target, own, todo)
+        send(at, valid, place.device(here, 1 - place.core), own, todo)
+        index = place.index(at, place.core, whole)
+
+        def step(index=index, valid=valid, todo=todo, own=own):
+            def body():
+                if not own:
+                    for k, (_, gathered) in enumerate(pairs):
+                        pltpu.make_async_copy(gathered.at[index], gathered.at[index], recv_sems.at[k, index]).wait()
+
+            guarded(valid, body)
+            for on, start in todo:
+                guarded(on, start)
+
+        key = abs(block[0]) + sum(1.0 for s in block[1:] if s) + 0.1 * last
+        steps.append((key, step))
+        other = place.index(at, 1 - place.core, whole)
+
+        def arrived(other=other):
+            for k, (_, gathered) in enumerate(pairs):
+                pltpu.make_async_copy(gathered.at[other], gathered.at[other], recv_sems.at[k, other]).wait()
+
+        ends.append((valid, arrived))
+    return steps, ends, counter[0]
+
+
+def count_gather_sends(dims):
+    total = 0
+    for block in relative_blocks(dims):
+        last = max([k for k, shift in enumerate(block) if shift], default=-1)
+        for k, (_, extent) in enumerate(dims):
+            if k > last:
+                total += len(sides(extent))
+            elif k == last and extent > 2:
+                total += 1
+        total += 1
+    return total
+
+
+def gather_kernel(ep_count, tp_count, groups, *refs):
+    count = sum(n for _, n in groups)
+    blocks, gathered, scratch = refs[:count], refs[count : 2 * count], refs[2 * count :]
+    place = Place(ep_count, tp_count)
+    greet(place, any(whole for whole, _ in groups))
+    steps, ends, first = [], [], 0
+    locals_ = []
+    for g, (whole, n) in enumerate(groups):
+        send_sems, recv_sems, own_sems = scratch[3 * g : 3 * g + 3]
+        pairs = list(zip(blocks[first : first + n], gathered[first : first + n]))
+        first += n
+        more, finish, _ = gather_events(place, whole, pairs, send_sems, recv_sems)
+        steps += more
+        ends += finish
+        here = {name: place.own(name) for name, _ in place.dims(whole)}
+        mine = place.index(here, place.core, whole)
+        for k, (block, out) in enumerate(pairs):
+            locals_.append(pltpu.make_async_copy(block, out.at[mine], own_sems.at[k]))
+    order = sorted(range(len(steps)), key=lambda i: steps[i][0])
+    steps[order[0]][1]()
+    for copy in locals_:
+        copy.start()
+    for i in order[1:]:
+        steps[i][1]()
+    for on, finish in ends:
+        guarded(on, finish)
+    for copy in locals_:
+        copy.wait()
+
+
+def gather(ep_count, tp_count, collective_id, name, whole_blocks, ep_blocks):
+    groups, arrays, shapes, scratch = [], [], [], []
+    place = Place(ep_count, tp_count)
+    for whole, blocks in ((True, whole_blocks), (False, ep_blocks)):
+        if not blocks:
+            continue
+        groups.append((whole, len(blocks)))
+        total = ep_count * tp_count if whole else ep_count
+        for block in blocks:
+            arrays.append(block)
+            shapes.append(jax.ShapeDtypeStruct((total,) + block.shape, block.dtype))
+        sends = count_gather_sends(place.dims(whole))
+        scratch += [
+            pltpu.SemaphoreType.DMA((len(blocks), sends)),
+            pltpu.SemaphoreType.DMA((len(blocks), total)),
+            pltpu.SemaphoreType.DMA((len(blocks),)),
+        ]
+    return pl.pallas_call(
+        functools.partial(gather_kernel, ep_count, tp_count, tuple(groups)),
+        out_shape=tuple(shapes),
+        in_specs=[pl.BlockSpec(memory_space=pl.ANY)] * len(arrays),
+        out_specs=tuple([pl.BlockSpec(memory_space=pl.ANY)] * len(arrays)),
+        scratch_shapes=scratch,
+        compiler_params=pltpu.CompilerParams(collective_id=collective_id, has_side_effects=True),
+        name=name,
+    )(*arrays)
+
+
+def add_into(target, sources, dtype):
+    rows, columns = target.shape
+    piece = 128
+    while columns % (piece * 2) == 0 and rows * piece * 2 <= 40 * 1024:
+        piece *= 2
+
+    def body(i, carry):
+        window = pl.ds(pl.multiple_of(i * piece, piece), piece)
+        total = sources[0][:, window].astype(jnp.float32)
+        for source in sources[1:]:
+            total = total + source[:, window].astype(jnp.float32)
+        target[:, window] = total.astype(dtype)
+        return carry
+
+    lax.fori_loop(0, columns // piece, body, 0)
+
+
+def scatter_kernel(ep_count, tp_count, whole, count, *refs):
+    partials, outs = refs[:count], refs[count : 2 * count]
+    scratch = refs[2 * count :]
+    place = Place(ep_count, tp_count)
+    greet(place, whole)
+    dims = place.dims(whole)
+    here = {name: place.own(name) for name, _ in dims}
+    owns = scratch[:count]
+    sibs = scratch[count : 2 * count]
+    lands = [scratch[2 * count + k * count : 2 * count + (k + 1) * count] for k in range(len(dims))]
+    sems = scratch[2 * count + len(dims) * count :]
+    own_sem, sib_send, sib_recv, line_send = sems[:4]
+    line_recv, accs = sems[4 : 4 + len(dims)], sems[4 + len(dims) :]
+    order = sorted(relative_blocks(dims), key=lambda block: -sum(abs(s) for s in block))
+    order = sorted(order, key=lambda block: -max([k for k, s in enumerate(block) if s], default=-1))
+    info = {}
+    ends = []
+    for block in order:
+        at, valid = dict(here), None
+        for (name, extent), shift in zip(dims, block):
+            at[name], on = moved(here[name], shift, extent)
+            valid = both(valid, on)
+        slot = place.slot(at, whole)
+        info[block] = (at, valid, slot)
+        local = [
+            pltpu.make_async_copy(
+                partials[k].at[place.index(at, place.core, whole)], owns[k].at[slot], own_sem.at[k, slot]
+            )
+            for k in range(count)
+        ]
+        across = [
+            pltpu.make_async_remote_copy(
+                src_ref=partials[k].at[place.index(at, 1 - place.core, whole)],
+                dst_ref=sibs[k].at[slot],
+                send_sem=sib_send.at[k, slot],
+                recv_sem=sib_recv.at[k, slot],
+                device_id=place.device(here, 1 - place.core),
+                device_id_type=MESH,
+            )
+            for k in range(count)
+        ]
+
+        def start(local=local, across=across):
+            for copy in local + across:
+                copy.start()
+
+        def finish(across=across):
+            for copy in across:
+                copy.wait_send()
+
+        guarded(valid, start)
+        ends.append((valid, finish))
+        info[block] += (local, across)
+
+    def land_slot(level, at, shift, side):
+        name, extent = dims[level]
+        inner = 0
+        for earlier, wide in dims[:level]:
+            inner = inner * wide + at[earlier]
+        wide = 1
+        for _, e in dims[:level]:
+            wide = wide * e
+        if extent == 2:
+            return inner
+        place_on = at[name] if (shift != 0 or side < 0) else extent
+        return place_on * wide + inner
+
+    number = 0
+    for block in order:
+        at, valid, slot, local, across = info[block]
+        last = max([k for k, shift in enumerate(block) if shift], default=-1)
+        waits = []
+        extra = []
+        for level in range(len(dims) - 1, -1, -1):
+            name, extent = dims[level]
+            if level < last:
+                break
+            if level == last:
+                if extent == 2:
+                    continue
+                froms = [-1 if block[level] > 0 else 1]
+            elif extent == 2:
+                froms = [1]
+            else:
+                froms = [-1, 1]
+            for side in froms:
+                _, on = moved(here[name], side, extent)
+                spot = land_slot(level, at, block[level], side)
+                extra.append((level, spot, on))
+
+        def arrive(local=local, across=across):
+            for copy in local:
+                copy.wait()
+            for copy in across:
+                copy.wait_recv()
+
+        guarded(valid, arrive)
+        for k in range(count):
+            sure = [owns[k].at[slot], sibs[k].at[slot]]
+            maybe = []
+            for level, spot, on in extra:
+                ref = lands[level][k].at[spot]
+
+                def wait(ref=ref, k=k, level=level, spot=spot):
+                    pltpu.make_async_copy(ref, ref, line_recv[level].at[k, spot]).wait()
+
+                guarded(both(valid, on), wait)
+                if on is None:
+                    sure.append(ref)
+                else:
+                    maybe.append((ref, on))
+            if last >= 0:
+                target, dtype = owns[k].at[slot], owns[k].dtype
+            else:
+                target, dtype = outs[k], outs[k].dtype
+
+            def add(sure=sure, maybe=maybe, target=target, dtype=dtype, k=k):
+                if not maybe:
+                    add_into(target, sure, dtype)
+                elif len(maybe) == 1:
+                    (ref, on), = maybe
+                    pl.when(on)(lambda: add_into(target, sure + [ref], dtype))
+                    pl.when(jnp.logical_not(on))(lambda: add_into(target, sure, dtype))
+                elif len(maybe) > 2:
+                    acc = accs[k]
+                    add_into(acc, sure, jnp.float32)
+                    for ref, on in maybe:
+                        pl.when(on)(functools.partial(add_into, acc, [acc, ref], jnp.float32))
+                    add_into(target, [acc], dtype)
+                else:
+                    (low, on_low), (high, on_high) = maybe
+                    pl.when(on_low & on_high)(lambda: add_into(target, sure + [low, high], dtype))
+                    pl.when(on_low & jnp.logical_not(on_high))(lambda: add_into(target, sure + [low], dtype))
+                    pl.when(on_high & jnp.logical_not(on_low))(lambda: add_into(target, sure + [high], dtype))
+
+            guarded(valid, add)
+        if last >= 0:
+            name, extent = dims[last]
+            way = 1 if block[last] > 0 else -1
+            there, _ = moved(here[name], way, extent)
+            arriving = 0 if extent == 2 else block[last] - way
+            spot = land_slot(last, at, arriving, -way)
+            made = [
+                pltpu.make_async_remote_copy(
+                    src_ref=owns[k].at[slot],
+                    dst_ref=lands[last][k].at[spot],
+                    send_sem=line_send.at[k, number],
+                    recv_sem=line_recv[last].at[k, spot],
+                    device_id=place.device({**here, name: there}, place.core),
+                    device_id_type=MESH,
+                )
+                for k in range(count)
+            ]
+            number += 1
+
+            def start(made=made):
+                for copy in made:
+                    copy.start()
+
+            def finish(made=made):
+                for copy in made:
+                    copy.wait_send()
+
+            guarded(valid, start)
+            ends.append((valid, finish))
+    for on, finish in ends:
+        guarded(on, finish)
+
+
+def scatter_add(ep_count, tp_count, collective_id, name, whole, partials):
+    place = Place(ep_count, tp_count)
+    dims = place.dims(whole)
+    count = len(partials)
+    slots = 1
+    for _, extent in dims:
+        slots *= extent
+    blocks = [p.shape[1:] for p in partials]
+    kinds = [p.dtype for p in partials]
+    scratch = []
+    for _ in range(2):
+        scratch += [pltpu.VMEM((slots,) + b, d) for b, d in zip(blocks, kinds)]
+    land_counts = []
+    wide = 1
+    for _, extent in dims:
+        land_counts.append(wide if extent == 2 else (extent + 1) * wide)
+        wide *= extent
+    for lands in land_counts:
+        scratch += [pltpu.VMEM((lands,) + b, d) for b, d in zip(blocks, kinds)]
+    sends = sum(1 for block in relative_blocks(dims) if any(block))
+    scratch += [pltpu.SemaphoreType.DMA((count, slots))] * 3 + [pltpu.SemaphoreType.DMA((count, sends))]
+    scratch += [pltpu.SemaphoreType.DMA((count, lands)) for lands in land_counts]
+    if sum(extent > 2 for _, extent in dims) > 1:
+        scratch += [pltpu.VMEM(b, jnp.float32) for b in blocks]
+    return pl.pallas_call(
+        functools.partial(scatter_kernel, ep_count, tp_count, whole, count),
+        out_shape=tuple(jax.ShapeDtypeStruct(b, jnp.float32) for b in blocks),
+        in_specs=[pl.BlockSpec(memory_space=pl.ANY)] * count,
+        out_specs=tuple([pl.BlockSpec(memory_space=pltpu.VMEM)] * count),
+        scratch_shapes=scratch,
+        compiler_params=pltpu.CompilerParams(
+            collective_id=collective_id, has_side_effects=True, vmem_limit_bytes=VMEM_MOST
+        ),
+        name=name,
+    )(*partials)
+
+
+def expert_kernel(parts, per_step, cap, *refs):
+    normed, cot, info = refs[:3]
+    ins, outs_w = refs[3 : 3 + parts], refs[3 + parts : 3 + 2 * parts]
+    result_ref, input_ref, own_grad = refs[3 + 2 * parts : 6 + 2 * parts]
+    sent = refs[6 + 2 * parts : 5 + 3 * parts]
+    scratch = refs[5 + 3 * parts :]
+    rows_x, rows_g, gate_col, result_acc, input_acc = scratch[:5]
+    sums = (own_grad,) + tuple(scratch[5:])
+    step = pl.program_id(0)
+    tok = normed.shape[1]
+    width = normed.shape[2]
+    chunk = 256
+
+    @pl.when(step == 0)
+    def _():
+        for total in sums:
+            total[...] = jnp.zeros_like(total)
+
+    slots = lax.broadcasted_iota(jnp.int32, (cap, tok), 0).astype(jnp.float32)
+    for s in range(per_step):
+        hit = slots == info[s, 0:1, :]
+        picks = jnp.where(hit, 1.0, 0.0).astype(jnp.bfloat16)
+        gates = jnp.sum(jnp.where(hit, info[s, 1:2, :], 0.0), axis=1, keepdims=True)
+        window = pl.ds(s * cap, cap)
+        gate_col[window, :] = jnp.broadcast_to(gates, (cap, 128))
+        rows_x[window, :] = jnp.dot(picks, normed[s], preferred_element_type=jnp.float32).astype(
+            jnp.bfloat16
+        )
+        taken = jnp.dot(picks, cot[s], preferred_element_type=jnp.float32)
+        rows_g[window, :] = (gates * taken).astype(jnp.bfloat16)
+    across = (((1,), (1,)), ((), ()))
+    down = (((0,), (0,)), ((), ()))
+
+    def mul(left, right, dims):
+        return lax.dot_general(left, right, dims, preferred_element_type=jnp.float32)
+
+    straight = (((1,), (0,)), ((), ()))
+    for p in range(parts):
+        gate_pre = mul(rows_x[...], ins[p][0], across)
+        up_pre = mul(rows_x[...], ins[p][1], across)
+        sigmoid = jax.nn.sigmoid(gate_pre)
+        active = (gate_pre * sigmoid * up_pre).astype(jnp.bfloat16)
+        grad_act = mul(rows_g[...], outs_w[p][...], across)
+        grad_up = (grad_act * gate_pre * sigmoid).astype(jnp.bfloat16)
+        grad_gate = (grad_act * up_pre * sigmoid * (1.0 + gate_pre * (1.0 - sigmoid))).astype(
+            jnp.bfloat16
+        )
+        for first in range(0, width, chunk):
+            window = slice(first, first + chunk)
+            result = mul(active, outs_w[p][:, window], straight)
+            back = mul(grad_gate, ins[p][0, :, window], straight) + mul(
+                grad_up, ins[p][1, :, window], straight
+            )
+            if p == 0:
+                result_acc[:, window] = result
+                input_acc[:, window] = back
+            else:
+                result_acc[:, window] += result
+                input_acc[:, window] += back
+            sums[p][0, :, window] += mul(grad_gate, rows_x[:, window], down)
+            sums[p][1, :, window] += mul(grad_up, rows_x[:, window], down)
+            sums[p][2, :, window] += mul(active, rows_g[:, window], down)
+    for s in range(per_step):
+        hit = slots == info[s, 0:1, :]
+        picks = jnp.where(hit, 1.0, 0.0).astype(jnp.bfloat16)
+        window = pl.ds(s * cap, cap)
+        rounded = result_acc[window, :].astype(jnp.bfloat16).astype(jnp.float32)
+        weighted = (gate_col[window, 0:1] * rounded).astype(jnp.bfloat16)
+        result_ref[s] = mul(picks, weighted, down).astype(jnp.bfloat16)
+        input_ref[s] = mul(picks, input_acc[window, :].astype(jnp.bfloat16), down).astype(
+            jnp.bfloat16
+        )
+
+    @pl.when(step == pl.num_programs(0) - 1)
+    def _():
+        for p in range(1, parts):
+            sent[p - 1][...] = sums[p][...].astype(jnp.bfloat16)
+
+
+def expert_pass(normed_all, cot_all, info, ins, outs_w, cap):
+    ep_count, tok, width = normed_all.shape
+    parts = len(ins)
+    hidden = ins[0].shape[1]
+    per_step = max(1, min(ep_count, 256 // cap))
+    rows = per_step * cap
+    token_spec = pl.BlockSpec((per_step, tok, width), lambda i: (i, 0, 0))
+    once = pl.Buffered(1)
+    in_specs = [token_spec, token_spec, pl.BlockSpec((per_step, 2, tok), lambda i: (i, 0, 0))]
+    in_specs += [
+        pl.BlockSpec((2, hidden, width), lambda i: (0, 0, 0), pipeline_mode=once)
+    ] * parts
+    in_specs += [pl.BlockSpec((hidden, width), lambda i: (0, 0), pipeline_mode=once)] * parts
+    grad_spec = pl.BlockSpec((3, hidden, width), lambda i: (0, 0, 0), pipeline_mode=once)
+    token_shape = jax.ShapeDtypeStruct((ep_count, tok, width), jnp.bfloat16)
+    out_shape = [token_shape, token_shape, jax.ShapeDtypeStruct((3, hidden, width), jnp.float32)]
+    out_shape += [jax.ShapeDtypeStruct((3, hidden, width), jnp.bfloat16)] * (parts - 1)
+    scratch = [
+        pltpu.VMEM((rows, width), jnp.bfloat16),
+        pltpu.VMEM((rows, width), jnp.bfloat16),
+        pltpu.VMEM((rows, 128), jnp.float32),
+        pltpu.VMEM((rows, width), jnp.float32),
+        pltpu.VMEM((rows, width), jnp.float32),
+    ] + [pltpu.VMEM((3, hidden, width), jnp.float32)] * (parts - 1)
+    found = pl.pallas_call(
+        functools.partial(expert_kernel, parts, per_step, cap),
+        grid=(ep_count // per_step,),
+        in_specs=in_specs,
+        out_specs=[token_spec, token_spec] + [grad_spec] * parts,
+        out_shape=out_shape,
+        scratch_shapes=scratch,
+        compiler_params=pltpu.CompilerParams(
+            dimension_semantics=("arbitrary",), vmem_limit_bytes=VMEM_MOST
+        ),
+        cost_estimate=pl.CostEstimate(
+            flops=18 * ep_count * cap * parts * hidden * width,
+            bytes_accessed=8 * ep_count * tok * width + 30 * parts * hidden * width,
+            transcendentals=ep_count * cap * parts * hidden,
+        ),
+        name="expert_pass",
+    )(normed_all, cot_all, info, *ins, *outs_w)
+    return found[0], found[1], found[2], found[3:]
 
 
 def rope_tables(length):
@@ -105,22 +726,38 @@
     tok_count = tokens.shape[0]
     width = tokens.shape[1]
     ep_count = lax.axis_size("ep")
+    tp_count = lax.axis_size("tp")
     capacity = tok_count * 8 // ep_count
-    slot_total = ep_count * capacity
-    pair_count = tok_count * TOPK
-    gathered = (
-        lax.all_gather(qkv_weight.astype(jnp.bfloat16), ("ep", "tp"), axis=0, tiled=True),
-        lax.all_gather(out_weight.astype(jnp.bfloat16), ("ep", "tp"), axis=0, tiled=True),
-        lax.all_gather(shared_in.astype(jnp.bfloat16), ("ep", "tp"), axis=0, tiled=True),
-        lax.all_gather(shared_out.astype(jnp.bfloat16), ("ep", "tp"), axis=0, tiled=True),
-        lax.all_gather(norm_gains.astype(jnp.bfloat16), ("ep", "tp"), axis=1, tiled=True),
-    )
-    qkv_low, out_low, shin_low, shout_low, gains_low = gathered
-    gain_one = gains_low[0].astype(jnp.float32)
-    gain_two = gains_low[1].astype(jnp.float32)
-    experts_low = (expert_in.astype(jnp.bfloat16), expert_out.astype(jnp.bfloat16))
-    in_low = experts_low[0][0]
-    ex_out_low = experts_low[1][0]
+    low = jnp.bfloat16
+    ep_ring = [
+        [((i + shift) % tp_count, i) for i in range(tp_count)] for shift in range(1, tp_count)
+    ]
+    in_own, out_own = expert_in[0].astype(low), expert_out[0].astype(low)
+    ins_low = [in_own] + [lax.ppermute(in_own, "tp", ring) for ring in ep_ring]
+    outs_low = [out_own] + [lax.ppermute(out_own, "tp", ring) for ring in ep_ring]
+    cot_all = lax.all_gather(cotangent, "ep", axis=0)
+    gain_columns = jnp.pad(norm_gains.T.astype(low), ((0, 0), (0, 126)))
+    qkv_low, out_low, gains_low = gather(
+        ep_count,
+        tp_count,
+        1,
+        "gather_attention",
+        [qkv_weight.astype(low), out_weight.astype(low), gain_columns],
+        [],
+    )
+    qkv_low = qkv_low.reshape(width, 3 * width)
+    out_low = out_low.reshape(width, width)
+    gains_low = gains_low.reshape(width, 128)
+    gain_one = gains_low[:, 0].astype(jnp.float32)
+    gain_two = gains_low[:, 1].astype(jnp.float32)
+    expert_ids = jnp.arange(ep_count, dtype=jnp.int32)
+    chosen = routes[:, :, None] == expert_ids[None, None, :]
+    onehot = jnp.sum(chosen.astype(jnp.float32), axis=1)
+    gate_of = jnp.sum(jnp.where(chosen, gates[:, :, None], 0.0), axis=1)
+    earlier = jnp.tril(jnp.ones((tok_count, tok_count), low), -1)
+    rank = jnp.dot(earlier, onehot.astype(low), preferred_element_type=jnp.float32)
+    slot_of = jnp.where(onehot > 0.0, rank, -1.0)
+    info_own = jnp.concatenate([slot_of, gate_of], axis=1).T
     tok_float = tokens.astype(jnp.float32)
     factor_one = lax.rsqrt(jnp.mean(tok_float * tok_float, axis=-1, keepdims=True) + NORM_EPS)
     unit_one = tok_float * factor_one
@@ -157,96 +794,34 @@
     factor_two = lax.rsqrt(jnp.mean(hidden * hidden, axis=-1, keepdims=True) + NORM_EPS)
     unit_two = hidden * factor_two
     normed_two = (unit_two * gain_two).astype(jnp.bfloat16)
+    shin_low, shout_low, normed_all, info_all = gather(
+        ep_count,
+        tp_count,
+        2,
+        "gather_tokens",
+        [shared_in.astype(low), shared_out.astype(low)],
+        [normed_two, info_own],
+    )
+    shin_low = shin_low.reshape(width, 2 * FF)
+    shout_low = shout_low.reshape(FF, width)
+    info = lax.dynamic_index_in_dim(
+        info_all.reshape(ep_count, 2, ep_count, tok_count), lax.axis_index("ep"), axis=2, keepdims=False
+    )
+    result_part, input_part, own_grad, sent_grads = expert_pass(
+        normed_all, cot_all, info, ins_low, outs_low, capacity
+    )
+    for shift, sent in enumerate(sent_grads, 1):
+        ring = [(i, (i + shift) % tp_count) for i in range(tp_count)]
+        own_grad = own_grad + lax.ppermute(sent, "tp", ring).astype(jnp.float32)
+    routed = lax.psum_scatter(
+        result_part, "ep", scatter_dimension=0, tiled=True
+    )[0].astype(jnp.float32)
+    (routed_grad,) = scatter_add(ep_count, tp_count, 3, "scatter_inputs", False, [input_part])
     shared_pre = jnp.dot(normed_two, shin_low, preferred_element_type=jnp.float32)
     shared_act = (jax.nn.silu(shared_pre[:, :FF]) * shared_pre[:, FF:]).astype(jnp.bfloat16)
     shared_res = jnp.dot(shared_act, shout_low, preferred_element_type=jnp.float32)
-    flat_routes = routes.reshape(pair_count)
-    onehot = (flat_routes[:, None] == jnp.arange(ep_count, dtype=jnp.int32)[None, :]).astype(
-        jnp.int32
-    )
-    slot_rank = jnp.sum((jnp.cumsum(onehot, axis=0) - onehot) * onehot, axis=1)
-    positions = flat_routes * capacity + slot_rank
-    slot_owner = (
-        jnp.zeros((slot_total,), jnp.int32)
-        .at[positions]
-        .set(jnp.arange(pair_count, dtype=jnp.int32) + 1)
-    )
-    filled = (slot_owner > 0)[:, None]
-    pair_index = jnp.maximum(slot_owner - 1, 0)
-    token_index = pair_index // TOPK
-    zero_low = jnp.zeros((), jnp.bfloat16)
-    send_rows = jnp.where(filled, normed_two[token_index], zero_low).reshape(
-        1, ep_count, capacity, width
-    )
-    arrived = lax.all_to_all(send_rows, "ep", split_axis=1, concat_axis=1, tiled=True)
-    expert_rows = lax.all_gather(arrived, "tp", axis=0, tiled=True).reshape(-1, width)
-    pre_both = jnp.einsum("rd,kfd->krf", expert_rows, in_low, preferred_element_type=jnp.float32)
-    gate_pre = pre_both[0]
-    up_pre = pre_both[1]
-    expert_act = (jax.nn.silu(gate_pre) * up_pre).astype(jnp.bfloat16)
-    piece = expert_act
-    expert_result = lax.psum_scatter(
-        jnp.dot(piece, ex_out_low, preferred_element_type=jnp.float32).astype(jnp.bfloat16),
-        "tp",
-        scatter_dimension=0,
-        tiled=True,
-    )
-    returned = lax.all_to_all(
-        expert_result.reshape(1, ep_count, capacity, width),
-        "ep",
-        split_axis=1,
-        concat_axis=1,
-        tiled=True,
-    )
-    pair_rows = returned.reshape(slot_total, width)[positions].reshape(tok_count, TOPK, width)
-    routed = jnp.einsum("tk,tkd->td", gates, pair_rows, preferred_element_type=jnp.float32)
     block_out = (hidden + shared_res + routed).astype(jnp.bfloat16)
     grad_top = cotangent.astype(jnp.float32)
-    flat_gates = gates.reshape(pair_count)
-    slot_grad = jnp.where(
-        filled,
-        (flat_gates[pair_index][:, None] * grad_top[token_index]).astype(jnp.bfloat16),
-        zero_low,
-    )
-    grad_arrived = lax.all_to_all(
-        slot_grad.reshape(1, ep_count, capacity, width),
-        "ep",
-        split_axis=1,
-        concat_axis=1,
-        tiled=True,
-    )
-    grad_rows = lax.all_gather(grad_arrived, "tp", axis=0, tiled=True).reshape(-1, width)
-    grad_act = jnp.einsum("rd,fd->rf", grad_rows, ex_out_low, preferred_element_type=jnp.float32)
-    out_grad_expert = jnp.einsum(
-        "rf,rd->fd", expert_act, grad_rows, preferred_element_type=jnp.float32
-    )
-    grad_gate, grad_up = swiglu_back(grad_act, gate_pre, up_pre)
-    grad_pre = jnp.stack([grad_gate, grad_up])
-    in_grad_expert = jnp.einsum(
-        "krf,rd->kfd", grad_pre, expert_rows, preferred_element_type=jnp.float32
-    )
-    piece = grad_pre
-    input_rows = lax.psum_scatter(
-        jnp.einsum("krf,kfd->rd", piece, in_low, preferred_element_type=jnp.float32).astype(
-            jnp.bfloat16
-        ),
-        "tp",
-        scatter_dimension=0,
-        tiled=True,
-    )
-    expert_grads = (in_grad_expert[None], out_grad_expert[None])
-    input_back = lax.all_to_all(
-        input_rows.reshape(1, ep_count, capacity, width),
-        "ep",
-        split_axis=1,
-        concat_axis=1,
-        tiled=True,
-    )
-    routed_grad = jnp.sum(
-        input_back.reshape(slot_total, width)[positions].reshape(tok_count, TOPK, width),
-        axis=1,
-        dtype=jnp.float32,
-    )
     grad_low = grad_top.astype(jnp.bfloat16)
     shout_grad = jnp.einsum("tf,td->fd", shared_act, grad_low, preferred_element_type=jnp.float32)
     grad_shared_act = jnp.einsum(
@@ -304,16 +879,22 @@
     )
     passed_one, gain_one_grad = norm_back(grad_normed_one, unit_one, factor_one, gain_one)
     tokens_grad = grad_hidden + passed_one
-    gains_grad = jnp.stack([gain_one_grad, gain_two_grad])
-    dense_grads = (
-        lax.psum_scatter(qkv_grad, ("ep", "tp"), scatter_dimension=0, tiled=True),
-        lax.psum_scatter(out_grad, ("ep", "tp"), scatter_dimension=0, tiled=True),
-        lax.psum_scatter(shin_grad, ("ep", "tp"), scatter_dimension=0, tiled=True),
-        lax.psum_scatter(shout_grad, ("ep", "tp"), scatter_dimension=0, tiled=True),
-        lax.psum_scatter(gains_grad, ("ep", "tp"), scatter_dimension=1, tiled=True),
-    )
-    qkv_part, out_part, shin_part, shout_part, gains_part = dense_grads
-    exin_part, exout_part = expert_grads
+    gain_rows = jnp.pad(jnp.stack([gain_one_grad, gain_two_grad], axis=1), ((0, 0), (0, 126)))
+    devices = ep_count * tp_count
+    dense_grads = scatter_add(
+        ep_count,
+        tp_count,
+        4,
+        "scatter_weights",
+        True,
+        [
+            grad.astype(low).reshape(devices, -1, grad.shape[1])
+            for grad in (qkv_grad, out_grad, gain_rows, shin_grad, shout_grad)
+        ],
+    )
+    qkv_part, out_part, gains_part, shin_part, shout_part = dense_grads
+    gains_part = gains_part[:, :2].T
+    exin_part, exout_part = own_grad[None, :2], own_grad[2:]
     squares = (
         jnp.sum(qkv_part * qkv_part) + jnp.sum(out_part * out_part) + jnp.sum(shin_part * shin_part)
     )

time: 1720 us -> 746 us (0.43)
  blocking collectives: 691 us -> 60.4 us
  waiting for transfers between devices: 610 us -> 0.71 us
  Pallas kernels: 0 us -> 481 us
  matrix products: 149 us -> 48.3 us
  local copies, waits for them, and re-layouts: 116 us -> 54 us
  starting transfers between devices: 58.4 us -> 4.5 us
    pallas_call x0 -> x5, Pallas kernels: none -> 481 us  [the longest x2 225 us: gather(): pl.pallas_call(functools.partial(gather_kernel, ep_count, tp_count, tuple...]
    unnamed x2 -> x0, blocking collectives: 342 us -> none
    reduce_scatter x5 -> x1, waiting for transfers between devices: 297 us -> 0.01 us  [per_device(): lax.psum_scatter(result_part, 'ep', scatter_dimension=0, tiled=True)[0]]
    all_to_all x2 -> x0, blocking collectives: 239 us -> none  [the longest x1 120 us: per_device(): lax.all_to_all(slot_grad.reshape(1, ep_count, capacity, width), 'ep', spl...]
    all_gather x6 -> x1, waiting for transfers between devices: 215 us -> 0.01 us  [per_device(): cot_all = lax.all_gather(cotangent, 'ep', axis=0)]
    all_to_all x2 -> x0, waiting for transfers between devices: 95.4 us -> none  [the longest x1 95.4 us: per_device(): lax.all_to_all(input_rows.reshape(1, ep_count, capacity, width), 'ep', sp...]
    dot_general x7 -> x1, matrix products: 88 us -> 0.23 us  [per_device(): jnp.dot(earlier, onehot.astype(low), preferred_element_type=jnp.float32)]
    all_gather x1 -> x0, blocking collectives: 69.9 us -> none  [per_device(): lax.all_gather(norm_gains.astype(jnp.bfloat16), ('ep', 'tp'), axis=1, til...]
  transfers between devices with their start and end apart: 17 -> 5, of which waited for: 9 -> 0; matrix products, arithmetic and copies ran while one was open for 32% -> 21% of each run, Pallas kernels for 0% -> 56%
where the time goes in v1:
time: 746 us; the launch traced here: 737 us
  Pallas kernels  481 us (64%)
  other arithmetic  66.5 us (9%)
  blocking collectives  60.4 us (8%)
  local copies, waits for them, and re-layouts  54 us (7%)
  matrix products  48.3 us (6%)
  between operations  21.9 us (3%)
    pallas_call x2, Pallas kernels, gather(): pl.pallas_call(functools.partial(gather_kernel, ep_count, tp_count, tuple...  225 us
    pallas_call x2, Pallas kernels, scatter_add(): pl.pallas_call(functools.partial(scatter_kernel, ep_count, tp_count, whol...  186 us
    pallas_call x1, Pallas kernels, expert_pass(): pl.pallas_call(functools.partial(expert_kernel, parts, per_step, cap), gr...  70 us
    psum x1, blocking collectives, per_device(): grad_norm = jnp.sqrt(lax.psum(squares, ('ep', 'tp')))  60.4 us
    convert_element_type x7, other arithmetic, adam_update(): return (weight_new, first_new, second_new, weight_new.astype(jnp.bfloat16))  24.7 us
    unnamed x149, local copies, waits for them, and re-layouts  20 us
  transfers between devices with their start and end apart: 5, of which 0 were waited for; matrix products, arithmetic and copies ran while one was open for 21% of the time, Pallas kernels for 56%

profile of v1, /device:TPU:0, one launch (start us, length us, event | category | flops | bytes accessed | tf_op | source)
XLA Modules:
  0.0 737.5 jit_solution(8131641196282936512)
XLA Ops:
  8.0 4.1 convert_bitcast_fusion.refs_3_
  12.1 3.0 collective-permute-start
  19.0 128.9 %gather_attention.1 = (bf16[32,40,3840]{2,1,0:T(8,128)(2,1)}, bf16[32,40,1280]{2,1,0:T(8,128)(2,1)}, bf16[32,40,128]{2,1,0:T(8,128)(2,1)}) custom-call(bf16[40,3840]{1,0:T(8,128)(2,1)} %convert_element_type.170.refs_0_, bf16[40,1280]{1,0:T(8,128)(2,1)} %convert_element_type.171.refs_1_, bf16[40,128]{1,0:T(8,128)(2,1)} %pad.9.refs_2_), custom_call_target="tpu_custom_call" | custom-call | tf_op jit(solution)/shard_map/gather_attention/pallas_call | solution.py:289
  149.4 13.8 %copy.150 = bf16[3840,1280]{1,0:T(8,128)(2,1)} copy(bf16[3840,1280]{0,1:T(8,128)(2,1)} %bitcast.105) | data formatting | bytes 19660800 | tf_op jit(solution)/shard_map/dot_general | solution.py:765
  166.4 5.7 fusion.20
  180.2 96.3 %gather_tokens.1 = (bf16[32,40,1792]{2,1,0:T(8,128)(2,1)}, bf16[32,28,1280]{2,1,0:T(8,128)(2,1)}, bf16[16,256,1280]{2,1,0:T(8,128)(2,1)}, f32[16,32,256]{2,1,0:T(8,128)}) custom-call(bf16[40,1792]{1,0:T(8,128)(2,1)} %convert_element_type.185.refs_0_, bf16[28,1280]{1,0:T(8,128)(2,1)} %convert_element_type.186.refs_1_, ...), custom_call_target="tpu_custom_call" | custom-call | tf_op jit(solution)/shard_map/gather_tokens/pallas_call | solution.py:289
  278.2 4.1 reshape.260
  282.3 3.8 fusion.71
  286.1 2.0 multiply_convert_fusion.3
  288.9 2.2 convolution_convert_fusion.3
  291.1 4.1 reshape.267.refs_4_
  300.4 4.9 convolution_convert_fusion.2
  305.3 2.0 convolution_add_fusion
  307.3 70.0 %expert_pass.1 = (bf16[16,256,1280]{2,1,0:T(8,128)(2,1)}, bf16[16,256,1280]{2,1,0:T(8,128)(2,1)}, f32[3,448,1280]{2,1,0:T(8,128)}, bf16[3,448,1280]{2,1,0:T(8,128)(2,1)}) custom-call(bf16[16,256,1280]{2,1,0:T(8,128)(2,1)} %get-tuple-element.52.refs_0_, bf16[16,256,1280]{2,1,0:T(8,128)(2,1)} %bitcast.124, f32[16,2,256]{2,1,0:T(2,128)} %bitcast.121, ...), custom_call_target="tpu_custom_call" | custom-call | flops 42278584320 | bytes 76349440 | tf_op jit(solution)/shard_map/expert_pass/pallas_call | solution.py:626
  378.8 69.7 %scatter_inputs.1 = f32[256,1280]{1,0:T(8,128)} custom-call(bf16[16,256,1280]{2,1,0:T(8,128)(2,1)} %get-tuple-element.55.refs_0_), custom_call_target="tpu_custom_call" | custom-call | tf_op jit(solution)/shard_map/scatter_inputs/pallas_call | solution.py:510
  449.5 5.5 multiply_reduce_fusion.3
  457.9 1.9 convolution_convert_fusion.4
  461.2 2.4 multiply_reduce_fusion.1
  469.9 4.0 fusion.16
  476.7 3.9 convolution_convert_fusion.1
  480.6 5.6 convolution_convert_fusion
  486.2 116.3 %scatter_weights.1 = (f32[40,3840]{1,0:T(8,128)}, f32[40,1280]{1,0:T(8,128)}, f32[40,128]{1,0:T(8,128)}, f32[40,1792]{1,0:T(8,128)}, f32[28,1280]{1,0:T(8,128)}) custom-call(bf16[32,40,3840]{2,1,0:T(8,128)(2,1)} %bitcast.100, bf16[32,40,1280]{2,1,0:T(8,128)(2,1)} %bitcast.102, bf16[32,40,128]{2,1,0:T(8,128)(2,1)} %bitcast.119, ...), custom_call_target="tpu_custom_call" | custom-call | tf_op jit(solution)/shard_map/scatter_weights/pallas_call | solution.py:510
  613.7 4.6 convert_add_fusion
  618.3 2.8 copy-done
  623.6 2.8 multiply_reduce_fusion.2
  627.8 3.3 fusion.15
  631.1 60.4 %psum.7 = f32[]{:T(128)} all-reduce(f32[]{:T(128)S(6)} %add.236), channel_id=1, replica_groups=mesh['ep'=16,'tp'=2] {'ep','tp'}, use_global_device_ids=true, to_apply=%region_19.20 | all-reduce | flops 1 | bytes 8 | tf_op jit(solution)/shard_map/psum | solution.py:903
  703.1 2.2 fusion.62
  705.3 2.4 fusion.64
  710.5 7.6 %fusion.58 = (bf16[1,448,1280]{2,1,0:T(8,128)(2,1)}, f32[1,448,1280]{2,1,0:T(8,128)}, f32[1,448,1280]{2,1,0:T(8,128)}, f32[1,448,1280]{2,1,0:T(8,128)}) fusion(f32[1,448,1280]{2,1,0:T(8,128)S(1)} %copy-done.7, f32[]{:T(128)S(6)} %min.3, f32[3,448,1280]{2,1,0:T(8,128)S(1)} %bitcast.99, f32[1,448,1280]{2,1,0:T(8,128)} %param.47, f32[1,448,1280]{2,1,0:T(8,128)} %param.48), kind=kLoop, calls=%fused_computation.152 | loop fusion | flops 9748480 | bytes 17203204 | tf_op jit(solution)/shard_map/convert_element_type | solution.py:695
  718.1 8.6 %fusion.60 = (bf16[1,2,448,1280]{3,2,1,0:T(8,128)(2,1)}, f32[1,2,448,1280]{3,2,1,0:T(8,128)}, f32[1,2,448,1280]{3,2,1,0:T(8,128)}, f32[1,2,448,1280]{3,2,1,0:T(8,128)}) fusion(f32[1,2,448,1280]{3,2,1,0:T(8,128)S(1)} %bitcast.104, f32[]{:T(128)S(6)} %min.3, f32[3,448,1280]{2,1,0:T(8,128)S(1)} %bitcast.99, f32[1,2,448,1280]{3,2,1,0:T(8,128)S(1)} %bitcast.115, ...), kind=kLoop, calls=%fused_computation.153 | loop fusion | flops 19496960 | bytes 34406404 | tf_op jit(solution)/shard_map/convert_element_type | solution.py:695
  726.6 2.4 fusion.18
  (226 shorter events, 64.4 us)
Async XLA Ops:
  7.2 300.1 %all-gather.3.cloned.1.call-start = ((), (), s32[]{:S(2)}) async-start(), calls=%async_computation.2 | async-start | bytes 11141120 | tf_op jit(solution)/shard_map/all_gather | solution.py:738
  7.9 7.1 copy-start.6
  7.9 718.7 %reduce-scatter.2.cloned.1.call-start = ((), (), s32[]{:S(2)}) async-start(), calls=%async_computation.1 | async-start | bytes 11141120 | tf_op jit(solution)/shard_map/reduce_scatter | solution.py:816
  12.1 5.6 copy-start.34
  12.1 295.2 %collective-permute-start = (bf16[2,448,1280]{2,1,0:T(8,128)(2,1)}, bf16[2,448,1280]{2,1,0:T(8,128)(2,1)}, u32[]{:S(2)}, u32[]{:S(2)}) collective-permute-start(bf16[2,448,1280]{2,1,0:T(8,128)(2,1)} %convert_bitcast_fusion.refs_3_), channel_id=1, source_target_pairs={{1,0},{0,1},{3,2},{2,3},{5,4},{4,5},{7,6},{6,7},{9,8},{8,9},{11,10... | collective-permute-start | bytes 6881288 | tf_op jit(solution)/shard_map/ppermute | solution.py:736
  16.2 291.1 %collective-permute-start.1 = (bf16[448,1280]{1,0:T(8,128)(2,1)}, bf16[448,1280]{1,0:T(8,128)(2,1)}, u32[]{:S(2)}, u32[]{:S(2)}) collective-permute-start(bf16[448,1280]{1,0:T(8,128)(2,1)} %convert_bitcast_fusion.1.refs_5_), channel_id=1, source_target_pairs={{1,0},{0,1},{3,2},{2,3},{5,4},{4,5},{7,6},{6,7},{9,8},{8,9},{11,10... | collective-permute-start | bytes 3440648 | tf_op jit(solution)/shard_map/ppermute | solution.py:737
  149.3 14.0 %copy-start.33 = (f32[40,1792]{1,0:T(8,128)S(1)}, f32[40,1792]{1,0:T(8,128)}, u32[]{:S(2)}) copy-start(f32[40,1792]{1,0:T(8,128)} %param.37) | copy-start | bytes 860164
  149.3 14.7 %copy-start.36 = (f32[28,1280]{1,0:T(8,128)S(1)}, f32[28,1280]{1,0:T(8,128)}, u32[]{:S(2)}) copy-start(f32[28,1280]{1,0:T(8,128)} %param.40) | copy-start | bytes 430084
  149.3 15.4 %copy-start.54 = (s32[256,7]{0,1:T(8,128)S(1)}, s32[256,7]{0,1:T(8,128)}, u32[]{:S(2)}) copy-start(s32[256,7]{0,1:T(8,128)} %param.29) | copy-start | bytes 21508
  149.3 15.4 %copy-start.55 = (f32[256,7]{0,1:T(8,128)S(1)}, f32[256,7]{0,1:T(8,128)}, u32[]{:S(2)}) copy-start(f32[256,7]{0,1:T(8,128)} %param.30) | copy-start | bytes 21508
  149.3 16.4 %copy-start.11 = (bf16[256,1280]{1,0:T(8,128)(2,1)S(1)}, bf16[256,1280]{1,0:T(8,128)(2,1)}, u32[]{:S(2)}) copy-start(bf16[256,1280]{1,0:T(8,128)(2,1)} %param.26) | copy-start | bytes 1966084
  149.3 16.6 %copy-start.56 = (s32[1,256]{1,0:T(1,128)S(1)}, s32[1,256]{1,0:T(1,128)}, u32[]{:S(2)}) copy-start(s32[1,256]{1,0:T(1,128)} %param.28) | copy-start | bytes 3076
  164.8 13.4 %copy-start.48 = (f32[1280]{0:T(1024)}, f32[1280]{0:T(1024)S(1)}, u32[]{:S(2)}) copy-start(f32[1280]{0:T(1024)S(1)} %convert_reduce_fusion.1) | copy-start | bytes 15364
  165.9 6.2 copy-start.50
  166.4 5.9 copy-start.39
  166.4 5.9 copy-start.41
  178.2 98.4 %copy-start.52 = (f32[256]{0:T(256)}, f32[256]{0:T(256)S(1)}, u32[]{:S(2)}) copy-start(f32[256]{0:T(256)S(1)} %add_rsqrt_fusion) | copy-start | bytes 3076
  377.3 236.4 %collective-permute-start.2 = (bf16[3,448,1280]{2,1,0:T(8,128)(2,1)}, bf16[3,448,1280]{2,1,0:T(8,128)(2,1)}, u32[]{:S(2)}, u32[]{:S(2)}) collective-permute-start(bf16[3,448,1280]{2,1,0:T(8,128)(2,1)} %get-tuple-element.61), channel_id=1, source_target_pairs={{0,1},{1,0},{2,3},{3,2},{4,5},{5,4},{6,7},{7,6},{8,9},{9,8},{10,11... | collective-permute-start | bytes 10321928 | tf_op jit(solution)/shard_map/ppermute | solution.py:815
  449.5 5.5 copy-start.17
  469.9 6.8 copy-start.5
  627.8 82.7 %slice-start = ((s8[6881280]{0:T(1024)(128)(4,1)}), s8[2686976]{0:T(1024)(128)(4,1)S(1)}, s32[]{:S(2)}) async-start(s8[6881280]{0:T(1024)(128)(4,1)} %bitcast.98), calls=%async_computation.3 | async-start | bytes 5373952
  631.1 76.7 %copy-start.35 = (f32[40,1280]{1,0:T(8,128)S(1)}, f32[40,1280]{1,0:T(8,128)}, u32[]{:S(2)}) copy-start(f32[40,1280]{1,0:T(8,128)} %get-tuple-element.57) | copy-start | bytes 614404
  631.1 76.7 %copy-start.46 = (f32[40,1280]{1,0:T(8,128)S(1)}, f32[40,1280]{1,0:T(8,128)}, u32[]{:S(2)}) copy-start(f32[40,1280]{1,0:T(8,128)} %param.35) | copy-start | bytes 614404
  631.1 76.7 %copy-start.47 = (f32[40,1280]{1,0:T(8,128)S(1)}, f32[40,1280]{1,0:T(8,128)}, u32[]{:S(2)}) copy-start(f32[40,1280]{1,0:T(8,128)} %param.36) | copy-start | bytes 614404
  703.1 5.6 copy-start.21
  703.1 5.6 copy-start.22
  703.1 5.6 copy-start.37
  703.1 5.6 copy-start.38
  707.8 10.3 %slice-start.2 = ((s8[4587520]{0:T(1024)(128)(4,1)}), s8[4194304]{0:T(1024)(128)(4,1)S(1)}, s32[]{:S(2)}) async-start(s8[4587520]{0:T(1024)(128)(4,1)} %bitcast.103), calls=%async_computation.5 | async-start | bytes 8388608
  707.8 10.3 %slice-start.7 = ((s8[4587520]{0:T(1024)(128)(4,1)}), s8[4194304]{0:T(1024)(128)(4,1)S(1)}, s32[]{:S(2)}) async-start(s8[4587520]{0:T(1024)(128)(4,1)} %bitcast.114), calls=%async_computation.10 | async-start | bytes 8388608
  710.4 7.6 %slice-start.3 = ((s8[4587520]{0:T(1024)(128)(4,1)}), s8[393216]{0:T(1024)(128)(4,1)S(1)}, s32[]{:S(2)}) async-start(s8[4587520]{0:T(1024)(128)(4,1)} %bitcast.103), calls=%async_computation.6 | async-start | bytes 786432
  710.4 7.6 %slice-start.8 = ((s8[4587520]{0:T(1024)(128)(4,1)}), s8[393216]{0:T(1024)(128)(4,1)S(1)}, s32[]{:S(2)}) async-start(s8[4587520]{0:T(1024)(128)(4,1)} %bitcast.114), calls=%async_computation.11 | async-start | bytes 786432
  (43 other events, 120.5 us)
Sparse Core Ops, SparseCore 0:
  10.3 104.2 all-gather.2
  448.6 141.1 reduce-scatter.1

commit v2 on v1

v2 whole, which is shorter than its diff:
```python
import functools
import jax
import jax.numpy as jnp
import numpy as np
from jax import lax
from jax.experimental import pallas as pl
from jax.experimental.pallas import tpu as pltpu
from jax.sharding import PartitionSpec as P

HEADS = 10
HDIM = 128
FF = 896
TOPK = 7
STEP = 10


MESH = pl.DeviceIdType.MESH
VMEM_MOST = 60 * 1024 * 1024
NEG_BIG = -1000000000.0
NORM_EPS = 1e-06
ROPE_BASE = 10000.0
CLIP_LEVEL = 1.0
BETA_ONE = 0.9
BETA_TWO = 0.95
ADAM_EPS = 1e-08
WEIGHT_DECAY = 0.1
MATRIX_RATE = 0.05
GAIN_RATE = 0.5


class Place:
    def __init__(self, ep_count, tp_count):
        chips = ep_count // 2
        nb = 1
        while nb * nb * 4 <= chips:
            nb *= 2
        self.nb, self.na, self.nt = nb, chips // nb, tp_count
        self.ep_count = ep_count
        self.wrap = chips * tp_count >= 64
        e = lax.axis_index("ep")
        self.t = lax.axis_index("tp")
        self.core = lax.rem(e, 2)
        self.b = lax.rem(e // 2, nb)
        self.a = e // (2 * nb)

    def dims(self, order):
        if "u" in order and self.nb != self.nt:
            order = "abt"
        extents = {"a": self.na, "b": self.nb, "t": self.nt, "u": self.nb, "v": self.nt}
        return tuple((name, shifts(extents[name], self.wrap)) for name in order)

    def extent(self, name):
        return {"a": self.na, "b": self.nb, "t": self.nt, "u": self.nb, "v": self.nt}[name]

    def moved(self, name, shift):
        own, extent = self.own(name), self.extent(name)
        if shift == 0:
            return own, None
        if extent == 2:
            return 1 - own, None
        if self.wrap:
            return lax.rem(own + shift + extent, extent), None
        there = own + shift
        return there, (there >= 0) & (there < extent)

    def own(self, name):
        even = self.core == 0
        if name == "u":
            return jnp.where(even, self.b, self.t)
        if name == "v":
            return jnp.where(even, self.t, self.b)
        return getattr(self, name)

    def chip(self, at):
        a = at.get("a", self.a)
        b, t = at.get("b", self.b), at.get("t", self.t)
        if "u" in at:
            even = self.core == 0
            b = jnp.where(even, at["u"], at["v"])
            t = jnp.where(even, at["v"], at["u"])
        return a, b, t

    def device(self, at, core):
        a, b, t = self.chip(at)
        return ((a * self.nb + b) * 2 + core, t)

    def index(self, at, core, whole):
        e, t = self.device(at, core)
        return e * self.nt + t if whole else e

    def slot(self, at, whole):
        a, b, t = self.chip(at)
        chip = a * self.nb + b
        return chip * self.nt + t if whole else chip


def shifts(extent, wrap):
    if extent == 1:
        return (0,)
    if extent == 2:
        return (0, 1)
    found = [0]
    for step in range(1, extent // 2 + 1 if wrap else extent):
        found += [step, -step]
    return tuple(found[:extent] if wrap else found)


def ways(spread):
    return (1,) if len(spread) == 2 else (1, -1) if len(spread) > 2 else ()


def onward(spread, shift):
    way = -1 if shift > 0 else 1
    return way if len(spread) > 2 and shift - way in spread else 0


def both(one, other):
    if one is None:
        return other
    return one if other is None else one & other


def guarded(condition, body):
    if condition is None:
        body()
    else:
        pl.when(condition)(body)


def greet(place, order):
    barrier = pltpu.get_barrier_semaphore()
    here = {name: place.own(name) for name, _ in place.dims(order)}
    pl.semaphore_signal(barrier, inc=1, device_id=place.device(here, 1 - place.core), device_id_type=MESH)
    count = jnp.int32(1)
    for name, spread in place.dims(order):
        for way in ways(spread):
            there, on = place.moved(name, way)
            target = place.device({**here, name: there}, place.core)

            def signal(target=target):
                pl.semaphore_signal(barrier, inc=1, device_id=target, device_id_type=MESH)

            guarded(on, signal)
            count = count + (1 if on is None else on.astype(jnp.int32))
    if len(order) > 2:
        for s in range(2, place.nt - 1):
            target = place.device({"t": lax.rem(place.t + s, place.nt)}, place.core)
            pl.semaphore_signal(barrier, inc=1, device_id=target, device_id_type=MESH)
            count = count + 1
    pl.semaphore_wait(barrier, count)


def relative_blocks(dims):
    blocks = [()]
    for _, spread in dims:
        blocks = [block + (shift,) for block in blocks for shift in spread]
    return blocks


def gather_events(place, order, pairs, send_sems, recv_sems):
    dims = place.dims(order)
    whole = len(dims) > 2
    here = {name: place.own(name) for name, _ in dims}
    counter = [0]
    ends = []

    def copies(at, target, core_of_block, own):
        index = place.index(at, core_of_block, whole)
        number = counter[0]
        counter[0] += 1
        made = []
        for k, (block, gathered) in enumerate(pairs):
            made.append(
                pltpu.make_async_remote_copy(
                    src_ref=block if own else gathered.at[index],
                    dst_ref=gathered.at[index],
                    send_sem=send_sems.at[k, number],
                    recv_sem=recv_sems.at[k, index],
                    device_id=target,
                    device_id_type=MESH,
                )
            )
        return made

    def send(at, on, target, own, todo):
        made = copies(at, target, place.core, own)

        def start(made=made):
            for copy in made:
                copy.start()

        def finish(made=made):
            for copy in made:
                copy.wait_send()

        todo.append((on, start))
        ends.append((on, finish))

    steps = []
    times = arrival_times(dims)
    for block in relative_blocks(dims):
        at, valid = dict(here), None
        for (name, _), shift in zip(dims, block):
            at[name], on = place.moved(name, shift)
            valid = both(valid, on)
        last = max([k for k, shift in enumerate(block) if shift], default=-1)
        own = last < 0
        todo = []
        for k in range(len(dims) - 1, -1, -1):
            name, spread = dims[k]
            if k < last:
                continue
            if k == last:
                way = onward(spread, block[k])
                sent = [way] if way else []
            else:
                sent = ways(spread)
            for way in sent:
                there, on = place.moved(name, way)
                target = place.device({**here, name: there}, place.core)
                send(at, both(valid, on), target, own, todo)
        send(at, valid, place.device(here, 1 - place.core), own, todo)
        index = place.index(at, place.core, whole)

        def step(index=index, valid=valid, todo=todo, own=own):
            def body():
                if not own:
                    for k, (_, gathered) in enumerate(pairs):
                        pltpu.make_async_copy(gathered.at[index], gathered.at[index], recv_sems.at[k, index]).wait()

            guarded(valid, body)
            for on, start in todo:
                guarded(on, start)

        steps.append((times[block], step))
        other = place.index(at, 1 - place.core, whole)

        def arrived(other=other):
            for k, (_, gathered) in enumerate(pairs):
                pltpu.make_async_copy(gathered.at[other], gathered.at[other], recv_sems.at[k, other]).wait()

        ends.append((valid, arrived))
    return steps, ends, counter[0]


def arrival_times(dims):
    times = {(): 0}
    for _, spread in dims:
        earlier = sorted(times, key=lambda block: times[block])
        found = {block + (0,): times[block] for block in earlier}
        for shift in spread:
            for i, block in enumerate(earlier):
                if shift:
                    far = abs(shift)
                    found[block + (shift,)] = max(times[block] + far, (far - 1) * len(earlier) + i + 1)
        times = found
    return times


def count_gather_sends(dims):
    total = 0
    for block in relative_blocks(dims):
        last = max([k for k, shift in enumerate(block) if shift], default=-1)
        for k, (_, spread) in enumerate(dims):
            if k > last:
                total += len(ways(spread))
            elif k == last and onward(spread, block[k]):
                total += 1
        total += 1
    return total


def exchange_copies(place, blocks, others, send_sems, recv_sems):
    copies = []
    for s in range(1, place.nt):
        back = blocks[0].shape == others[0].shape
        there = lax.rem(place.t + (s if back else place.nt - s), place.nt)
        target = place.device({"t": there}, place.core)
        for k, (block, other) in enumerate(zip(blocks, others)):
            copies.append(
                pltpu.make_async_remote_copy(
                    src_ref=block.at[s - 1] if back else block,
                    dst_ref=other.at[s - 1],
                    send_sem=send_sems.at[k, s - 1],
                    recv_sem=recv_sems.at[k, s - 1],
                    device_id=target,
                    device_id_type=MESH,
                )
            )
    return copies


def gather_kernel(ep_count, tp_count, groups, *refs):
    count = sum(n for _, n in groups)
    blocks, gathered, scratch = refs[:count], refs[count : 2 * count], refs[2 * count :]
    place = Place(ep_count, tp_count)
    greet(place, max((order for order, _ in groups), key=len))
    steps, ends, first = [], [], 0
    local, swaps = [], []
    for order, n in groups:
        mine_in, mine_out = blocks[first : first + n], gathered[first : first + n]
        first += n
        if order == "t":
            swaps += exchange_copies(place, mine_in, mine_out, scratch[0], scratch[1])
            scratch = scratch[2:]
            continue
        send_sems, recv_sems, own_sems = scratch[:3]
        scratch = scratch[3:]
        pairs = list(zip(mine_in, mine_out))
        more, finish, _ = gather_events(place, order, pairs, send_sems, recv_sems)
        size = sum(block.shape[0] * block.shape[1] * (4 if block.dtype == jnp.float32 else 2) for block in mine_in)
        steps += [(key * size, len(steps) + i, step) for i, (key, step) in enumerate(more)]
        ends += finish
        here = {name: place.own(name) for name, _ in place.dims(order)}
        mine = place.index(here, place.core, len(order) > 2)
        for k, (block, out) in enumerate(pairs):
            local.append(pltpu.make_async_copy(block, out.at[mine], own_sems.at[k]))
    steps.sort(key=lambda entry: entry[:2])
    lead = sum(1 for key, _, _ in steps if key == 0)
    for _, _, step in steps[:lead]:
        step()
    for copy in swaps + local:
        copy.start()
    for _, _, step in steps[lead:]:
        step()
    for on, finish in ends:
        guarded(on, finish)
    for copy in swaps + local:
        copy.wait()


def gather(ep_count, tp_count, collective_id, name, groups):
    arrays, shapes, scratch = [], [], []
    place = Place(ep_count, tp_count)
    for order, blocks in groups:
        total = ep_count * tp_count if len(order) > 2 else ep_count if order != "t" else tp_count - 1
        for block in blocks:
            arrays.append(block)
            shapes.append(jax.ShapeDtypeStruct((total,) + block.shape, block.dtype))
        if order == "t":
            scratch += [pltpu.SemaphoreType.DMA((len(blocks), total))] * 2
            continue
        sends = count_gather_sends(place.dims(order))
        scratch += [
            pltpu.SemaphoreType.DMA((len(blocks), sends)),
            pltpu.SemaphoreType.DMA((len(blocks), total)),
            pltpu.SemaphoreType.DMA((len(blocks),)),
        ]
    return pl.pallas_call(
        functools.partial(
            gather_kernel, ep_count, tp_count, tuple((order, len(blocks)) for order, blocks in groups)
        ),
        out_shape=tuple(shapes),
        in_specs=[pl.BlockSpec(memory_space=pl.ANY)] * len(arrays),
        out_specs=tuple([pl.BlockSpec(memory_space=pl.ANY)] * len(arrays)),
        scratch_shapes=scratch,
        compiler_params=pltpu.CompilerParams(collective_id=collective_id, has_side_effects=True),
        name=name,
    )(*arrays)


def add_into(target, sources, dtype):
    rows, columns = target.shape
    piece = 128
    while columns % (piece * 2) == 0 and rows * piece * 2 <= 40 * 1024:
        piece *= 2

    def body(i, carry):
        window = pl.ds(pl.multiple_of(i * piece, piece), piece)
        total = sources[0][:, window].astype(jnp.float32)
        for source in sources[1:]:
            total = total + source[:, window].astype(jnp.float32)
        target[:, window] = total.astype(dtype)
        return carry

    lax.fori_loop(0, columns // piece, body, 0)


def norm_kernel(ep_count, tp_count, count, *refs):
    parts, extra, out = refs[:count], refs[count], refs[count + 1]
    tile, tiles, send, recv = refs[count + 2 :]
    devices = ep_count * tp_count
    me = lax.axis_index("ep") * tp_count + lax.axis_index("tp")

    def place(i):
        other = lax.rem(me + i, devices)
        return other, (other // tp_count, lax.rem(other, tp_count))

    barrier = pltpu.get_barrier_semaphore()

    def signal(i, carry):
        pl.semaphore_signal(barrier, inc=1, device_id=place(i)[1], device_id_type=MESH)
        return carry

    lax.fori_loop(1, devices, signal, 0)
    tile[...] = jnp.zeros_like(tile)
    for first in range(0, extra.shape[1], 128):
        tile[0:1, :] += extra[:, first : first + 128]
    for part in parts:

        def add(i, carry, part=part):
            piece = part[:, pl.ds(pl.multiple_of(i * 128, 128), 128)]
            tile[0:1, :] += jnp.sum(piece * piece, axis=0, keepdims=True)
            return carry

        lax.fori_loop(0, part.shape[1] // 128, add, 0)
    pl.semaphore_wait(barrier, devices - 1)

    def share(i, carry):
        pltpu.make_async_remote_copy(
            src_ref=tile,
            dst_ref=tiles.at[me],
            send_sem=send.at[i],
            recv_sem=recv.at[me],
            device_id=place(i)[1],
            device_id_type=MESH,
        ).start()
        return carry

    lax.fori_loop(1, devices, share, 0)
    out[...] = tile[...]

    def collect(i, carry):
        other = place(i)[0]
        pltpu.make_async_copy(tiles.at[other], tiles.at[other], recv.at[other]).wait()
        out[...] += tiles[other]
        return carry

    lax.fori_loop(1, devices, collect, 0)

    def sent(i, carry):
        pltpu.make_async_copy(tile, tile, send.at[i]).wait()
        return carry

    lax.fori_loop(1, devices, sent, 0)


def sum_of_squares(ep_count, tp_count, collective_id, parts, extra):
    devices = ep_count * tp_count
    inside = pl.BlockSpec(memory_space=pltpu.VMEM)
    total = pl.pallas_call(
        functools.partial(norm_kernel, ep_count, tp_count, len(parts)),
        out_shape=jax.ShapeDtypeStruct((8, 128), jnp.float32),
        in_specs=[inside] * (len(parts) + 1),
        out_specs=inside,
        scratch_shapes=[
            pltpu.VMEM((8, 128), jnp.float32),
            pltpu.VMEM((devices, 8, 128), jnp.float32),
            pltpu.SemaphoreType.DMA((devices,)),
            pltpu.SemaphoreType.DMA((devices,)),
        ],
        compiler_params=pltpu.CompilerParams(collective_id=collective_id, has_side_effects=True),
        name="sum_of_squares",
    )(*parts, extra)
    return jnp.sum(total)


def scatter_events(place, order, partials, outs, refs):
    count = len(partials)
    dims = place.dims(order)
    whole = len(dims) > 2
    here = {name: place.own(name) for name, _ in dims}
    owns, sibs = refs[:count], refs[count : 2 * count]
    lands = [refs[(2 + k) * count : (3 + k) * count] for k in range(len(dims))]
    sems = refs[(2 + len(dims)) * count :]
    own_sem, sib_send, sib_recv, line_send = sems[:4]
    line_recv = sems[4:]
    blocks = sorted(relative_blocks(dims), key=lambda block: -sum(abs(s) for s in block))
    blocks = sorted(blocks, key=lambda block: -max([k for k, s in enumerate(block) if s], default=-1))
    info = {}
    starts, steps, ends = [], [], []
    for block in blocks:
        at, valid = dict(here), None
        for (name, _), shift in zip(dims, block):
            at[name], on = place.moved(name, shift)
            valid = both(valid, on)
        slot = place.slot(at, whole)
        local = [
            pltpu.make_async_copy(
                partials[k].at[place.index(at, place.core, whole)], owns[k].at[slot], own_sem.at[k, slot]
            )
            for k in range(count)
        ]
        across = [
            pltpu.make_async_remote_copy(
                src_ref=partials[k].at[place.index(at, 1 - place.core, whole)],
                dst_ref=sibs[k].at[slot],
                send_sem=sib_send.at[k, slot],
                recv_sem=sib_recv.at[k, slot],
                device_id=place.device(here, 1 - place.core),
                device_id_type=MESH,
            )
            for k in range(count)
        ]

        def start(local=local, across=across):
            for copy in across + local:
                copy.start()

        def finish(across=across):
            for copy in across:
                copy.wait_send()

        starts.append((valid, start))
        ends.append((valid, finish))
        info[block] = (at, valid, slot, local, across)

    def land_slot(level, at, shift, side):
        inner, wide = 0, 1
        for name, _ in dims[:level]:
            inner = inner * place.extent(name) + at[name]
            wide = wide * place.extent(name)
        return landings(dims[level][1]).index((shift, side)) * wide + inner

    number = 0
    for block in blocks:
        at, valid, slot, local, across = info[block]
        todo = []
        last = max([k for k, shift in enumerate(block) if shift], default=-1)
        extra_refs = []
        for level in range(len(dims) - 1, max(last, 0) - 1, -1):
            name, spread = dims[level]
            for shift, side in landings(spread):
                if shift == block[level]:
                    _, on = place.moved(name, side)
                    extra_refs.append((level, land_slot(level, at, shift, side), on))

        def arrive(local=local, across=across):
            for copy in local:
                copy.wait()
            for copy in across:
                copy.wait_recv()

        todo.append((valid, arrive))
        for k in range(count):
            sure = [owns[k].at[slot], sibs[k].at[slot]]
            maybe = []
            for level, spot, on in extra_refs:
                ref = lands[level][k].at[spot]

                def wait(ref=ref, k=k, level=level, spot=spot):
                    pltpu.make_async_copy(ref, ref, line_recv[level].at[k, spot]).wait()

                todo.append((both(valid, on), wait))
                if on is None:
                    sure.append(ref)
                else:
                    maybe.append((ref, on))
            if last >= 0:
                target, dtype = owns[k].at[slot], owns[k].dtype
            else:
                target, dtype = outs[k], outs[k].dtype

            def add(sure=sure, maybe=maybe, target=target, dtype=dtype):
                if not maybe:
                    add_into(target, sure, dtype)
                elif len(maybe) == 1:
                    ((ref, on),) = maybe
                    pl.when(on)(lambda: add_into(target, sure + [ref], dtype))
                    pl.when(jnp.logical_not(on))(lambda: add_into(target, sure, dtype))
                else:
                    (low, on_low), (high, on_high) = maybe
                    pl.when(on_low & on_high)(lambda: add_into(target, sure + [low, high], dtype))
                    pl.when(on_low & jnp.logical_not(on_high))(lambda: add_into(target, sure + [low], dtype))
                    pl.when(on_high & jnp.logical_not(on_low))(lambda: add_into(target, sure + [high], dtype))

            todo.append((valid, add))
        if last >= 0:
            name, spread = dims[last]
            way = 1 if block[last] > 0 else -1
            there, _ = place.moved(name, way)
            spot = land_slot(last, at, block[last] - way, -way if len(spread) > 2 else 1)
            made = [
                pltpu.make_async_remote_copy(
                    src_ref=owns[k].at[slot],
                    dst_ref=lands[last][k].at[spot],
                    send_sem=line_send.at[k, number],
                    recv_sem=line_recv[last].at[k, spot],
                    device_id=place.device({**here, name: there}, place.core),
                    device_id_type=MESH,
                )
                for k in range(count)
            ]
            number += 1

            def start(made=made):
                for copy in made:
                    copy.start()

            def finish(made=made):
                for copy in made:
                    copy.wait_send()

            todo.append((valid, start))
            ends.append((valid, finish))
        steps.append(todo)
    return starts, steps, ends


def scatter_sizes(place, order):
    dims = place.dims(order)
    slots, lands = 1, []
    for name, spread in dims:
        lands.append(len(landings(spread)) * slots)
        slots *= place.extent(name)
    return slots, lands, sum(1 for block in relative_blocks(dims) if any(block))


def scatter_kernel(ep_count, tp_count, groups, *refs):
    count = sum(n for _, n in groups)
    partials, outs, refs = refs[:count], refs[count : 2 * count], refs[2 * count :]
    place = Place(ep_count, tp_count)
    greet(place, max((order for order, _ in groups), key=len))
    starts, steps, ends, swaps, first = [], [], [], [], 0
    for order, n in groups:
        mine_in, mine_out = partials[first : first + n], outs[first : first + n]
        first += n
        if order == "t":
            swaps += exchange_copies(place, mine_in, mine_out, refs[0], refs[1])
            refs = refs[2:]
            continue
        used = n * (2 + len(order)) + 4 + len(order)
        more, done, finish = scatter_events(place, order, mine_in, mine_out, refs[:used])
        refs = refs[used:]
        starts += [(i / len(more), len(starts) + i, entry) for i, entry in enumerate(more)]
        steps += [(i / len(done), len(steps) + i, todo) for i, todo in enumerate(done)]
        ends += finish
    for copy in swaps:
        copy.start()
    for _, _, (on, start) in sorted(starts, key=lambda entry: entry[:2]):
        guarded(on, start)
    for _, _, todo in sorted(steps, key=lambda entry: entry[:2]):
        for on, act in todo:
            guarded(on, act)
    for on, finish in ends:
        guarded(on, finish)
    for copy in swaps:
        copy.wait()


def landings(spread):
    if len(spread) == 2:
        return [(0, 1)]
    return [(shift, way) for shift in spread for way in (-1, 1) if shift - way in spread and shift * way <= 0]


def scatter_add(ep_count, tp_count, collective_id, name, groups):
    place = Place(ep_count, tp_count)
    arrays, shapes, scratch, specs = [], [], [], []
    dma = pltpu.SemaphoreType.DMA
    for order, partials in groups:
        arrays += partials
        count = len(partials)
        if order == "t":
            shapes += [jax.ShapeDtypeStruct(p.shape, p.dtype) for p in partials]
            specs += [pl.BlockSpec(memory_space=pl.ANY)] * count
            scratch += [dma((count, tp_count - 1))] * 2
            continue
        slots, lands, sends = scatter_sizes(place, order)
        blocks = [(p.shape[1:], p.dtype) for p in partials]
        shapes += [jax.ShapeDtypeStruct(shape, jnp.float32) for shape, _ in blocks]
        specs += [pl.BlockSpec(memory_space=pltpu.VMEM)] * count
        for wide in [slots, slots] + lands:
            scratch += [pltpu.VMEM((wide,) + shape, dtype) for shape, dtype in blocks]
        scratch += [dma((count, slots))] * 3 + [dma((count, sends))] + [dma((count, wide)) for wide in lands]
    return pl.pallas_call(
        functools.partial(
            scatter_kernel, ep_count, tp_count, tuple((order, len(partials)) for order, partials in groups)
        ),
        out_shape=tuple(shapes),
        in_specs=[pl.BlockSpec(memory_space=pl.ANY)] * len(arrays),
        out_specs=tuple(specs),
        scratch_shapes=scratch,
        compiler_params=pltpu.CompilerParams(
            collective_id=collective_id, has_side_effects=True, vmem_limit_bytes=VMEM_MOST
        ),
        name=name,
    )(*arrays)


def scatter_all(ep_count, tp_count, collective_ids, name, groups):
    place = Place(ep_count, tp_count)
    calls, room = [[]], 0
    for order, partials in groups:
        need = 0
        if order != "t":
            slots, lands, _ = scatter_sizes(place, order)
            for p in partials:
                rows = (p.shape[1] + 15) // 16 * 16
                need += (2 * slots + sum(lands)) * rows * p.shape[2] * p.dtype.itemsize
        if calls[-1] and room + need > VMEM_MOST * 19 // 20:
            calls.append([])
            room = 0
        calls[-1].append((order, partials))
        room += need
    found = []
    for i, call in enumerate(calls):
        found += scatter_add(ep_count, tp_count, collective_ids[i], "%s_%d" % (name, i), call)
    return found

OVER_LAST = (((1,), (1,)), ((), ()))
OVER_FIRST = (((0,), (0,)), ((), ()))
STRAIGHT = (((1,), (0,)), ((), ()))


def mul(left, right, dims=STRAIGHT):
    return lax.dot_general(left, right, dims, preferred_element_type=jnp.float32)


def rope_rows(length):
    places = np.arange(length, dtype=np.float32)
    frequencies = ROPE_BASE ** (-np.arange(HDIM // 2, dtype=np.float32) * np.float32(2.0 / HDIM))
    angles = places[:, None] * frequencies.astype(np.float32)[None, :]
    cosine, sine = np.cos(angles), np.sin(angles)
    return (
        np.concatenate([cosine, cosine], axis=1).astype(np.float32),
        np.concatenate([-sine, sine], axis=1).astype(np.float32),
    )


def unit_of(values):
    factor = lax.rsqrt(jnp.mean(values * values, axis=-1, keepdims=True) + NORM_EPS)
    return values * factor, factor


def masked_probs(queries, keys, allowed):
    raw = mul(queries, keys, OVER_LAST) * HDIM ** (-0.5)
    scores = jnp.where(allowed, raw, NEG_BIG)
    weights = jnp.exp(scores - jnp.max(scores, axis=-1, keepdims=True))
    return weights * (1.0 / jnp.sum(weights, axis=-1, keepdims=True))


def allowed_pairs(seg_row, seg_column):
    length = seg_row.shape[1]
    later = lax.broadcasted_iota(jnp.int32, (length, length), 0)
    earlier = lax.broadcasted_iota(jnp.int32, (length, length), 1)
    return (later >= earlier) & (seg_column[:, 0:1] == seg_row[0:1, :])


def forward_kernel(tokens, seg_row, seg_column, gains, cosine, sine, wq, wk, wv, wo,
                   qkv_out, attended, hidden, normed_two, normed):
    pair = pl.program_id(0)
    width = tokens.shape[1]
    wide = 2 * HDIM

    @pl.when(pair == 0)
    def _():
        values = tokens[...].astype(jnp.float32)
        normed[...] = (unit_of(values)[0] * gains[0:1, :]).astype(jnp.bfloat16)
        hidden[...] = values

    allowed = allowed_pairs(seg_row, seg_column)
    window = pl.ds(pl.multiple_of(pair * wide, wide), wide)
    made = []
    for part, weight in enumerate((wq, wk, wv)):
        projected = mul(normed[...], weight[...])
        heads = []
        for j in range(2):
            head = projected[:, j * HDIM : (j + 1) * HDIM]
            if part < 2:
                head = head * cosine[...] + pltpu.roll(head, HDIM // 2, 1) * sine[...]
            heads.append(head.astype(jnp.bfloat16))
            qkv_out[:, pl.ds(pl.multiple_of(part * width + pair * wide + j * HDIM, HDIM), HDIM)] = heads[j]
        made.append(heads)
    for j in range(2):
        probs = masked_probs(made[0][j], made[1][j], allowed).astype(jnp.bfloat16)
        attended[:, pl.ds(pl.multiple_of(pair * wide + j * HDIM, HDIM), HDIM)] = mul(
            probs, made[2][j]
        ).astype(jnp.bfloat16)
    hidden[...] += mul(attended[:, window], wo[...])

    @pl.when(pair == pl.num_programs(0) - 1)
    def _():
        normed_two[...] = (unit_of(hidden[...])[0] * gains[1:2, :]).astype(jnp.bfloat16)


def attention_forward(tokens, segments, gains, qkv_low, out_low):
    length, width = tokens.shape
    wide, pairs = 2 * HDIM, HEADS // 2
    cosine, sine = rope_rows(length)
    seg_row = jnp.broadcast_to(segments, (8, length))
    seg_column = jnp.broadcast_to(segments.T, (length, 128))
    low = jnp.bfloat16

    def whole(*shape):
        return pl.BlockSpec(shape, lambda i: (0,) * len(shape))

    def columns(part):
        return pl.BlockSpec((width, wide), lambda i: (0, part * pairs + i))

    return pl.pallas_call(
        forward_kernel,
        grid=(pairs,),
        in_specs=[
            whole(length, width), whole(8, length), whole(length, 128), whole(8, width),
            whole(length, HDIM), whole(length, HDIM), columns(0), columns(1), columns(2),
            pl.BlockSpec((wide, width), lambda i: (i, 0)),
        ],
        out_specs=[whole(length, 3 * width), whole(length, width), whole(length, width), whole(length, width)],
        out_shape=[
            jax.ShapeDtypeStruct((length, 3 * width), low),
            jax.ShapeDtypeStruct((length, width), low),
            jax.ShapeDtypeStruct((length, width), jnp.float32),
            jax.ShapeDtypeStruct((length, width), low),
        ],
        scratch_shapes=[pltpu.VMEM((length, width), low)],
        compiler_params=pltpu.CompilerParams(
            dimension_semantics=("arbitrary",), vmem_limit_bytes=VMEM_MOST
        ),
        name="attention_forward",
    )(tokens, seg_row, seg_column, gains, jnp.asarray(cosine), jnp.asarray(sine), qkv_low, qkv_low, qkv_low, out_low)


def spread_matrix(units, padded, group, step):
    unit = lax.broadcasted_iota(jnp.int32, (units, padded), 0)
    spot = lax.broadcasted_iota(jnp.int32, (units, padded), 1)
    within = jnp.bitwise_and(spot, step - 1)
    source = (spot - within) // step * group + within
    return jnp.where((unit == source) & (within < group), 1.0, 0.0).astype(jnp.bfloat16)


def backward_kernel(group, step, tokens, cot, seg_row, seg_column, gains, cosine, sine, qkv_act, attended,
                    hidden, normed_two, routed_grad, wq, wk, wv, wo, shin, shout,
                    base, tokens_grad, gain_grads, qkv_grad, out_grad, shin_grad, shout_grad,
                    normed, normed_turned, branch, grad_hidden, grad_one, pieces, stage, stage_sem):
    at = pl.program_id(0)
    width = tokens.shape[1]
    wide = 2 * HDIM
    low = jnp.bfloat16
    units = shin.shape[1] // 2

    def stage_copy(part, pair):
        return pltpu.make_async_copy(
            stage.at[part],
            qkv_grad.at[:, pl.ds(pl.multiple_of(part * width + pair * wide, wide), wide)],
            stage_sem.at[part],
        )

    @pl.when(at == 0)
    def _():
        unit_one = unit_of(tokens[...].astype(jnp.float32))[0]
        first = unit_one * gains[0:1, :]
        normed[...] = first.astype(low)
        normed_turned[...] = first.T.astype(low)
        pre_gate = mul(normed_two[...], shin[:, :units])
        pre_up = mul(normed_two[...], shin[:, units:])
        sigmoid = jax.nn.sigmoid(pre_gate)
        act = (pre_gate * sigmoid * pre_up).astype(low)
        spread = spread_matrix(units, shout.shape[0], group, step)
        act_spread = mul(act, spread).astype(low)
        base[...] = hidden[...] + mul(act_spread, shout[...])
        shout_grad[...] = mul(act_spread, cot[...], OVER_FIRST).astype(low)
        shout_tight = mul(spread, shout[...]).astype(low)
        grad_act = mul(cot[...], shout_tight, OVER_LAST)
        grad_up = (grad_act * pre_gate * sigmoid).astype(low)
        grad_gate = (grad_act * pre_up * sigmoid * (1.0 + pre_gate * (1.0 - sigmoid))).astype(low)
        shin_grad[:, :units] = mul(normed_two[...], grad_gate, OVER_FIRST).astype(low)
        shin_grad[:, units:] = mul(normed_two[...], grad_up, OVER_FIRST).astype(low)
        grad_two = (
            routed_grad[...]
            + mul(grad_gate, shin[:, :units], OVER_LAST)
            + mul(grad_up, shin[:, units:], OVER_LAST)
        )
        unit_two, factor_two = unit_of(hidden[...])
        gain_grads[...] = jnp.zeros_like(gain_grads)
        gain_grads[1:2, :] = jnp.sum(grad_two * unit_two, axis=0, keepdims=True)
        grad_unit = grad_two * gains[1:2, :]
        back = factor_two * (
            grad_unit - unit_two * jnp.mean(grad_unit * unit_two, axis=-1, keepdims=True)
        )
        grad_hidden[...] = cot[...].astype(jnp.float32) + back
        branch[...] = grad_hidden[...].astype(low)
        grad_one[...] = jnp.zeros_like(grad_one)

    @pl.when(at > 0)
    def _():
        pair = at - 1
        allowed = allowed_pairs(seg_row, seg_column)
        window = pl.ds(pl.multiple_of(pair * wide, wide), wide)
        out_grad[...] = mul(attended[:, window], branch[...], OVER_FIRST).astype(low)
        grad_att = mul(branch[...], wo[...], OVER_LAST).astype(low)
        for j in range(2):

            def head(part):
                start = pl.multiple_of(part * width + pair * wide + j * HDIM, HDIM)
                return qkv_act[:, pl.ds(start, HDIM)]

            queries, keys, values = head(0), head(1), head(2)
            own = slice(j * HDIM, (j + 1) * HDIM)
            grad_own = grad_att[:, own]
            probs = masked_probs(queries, keys, allowed)
            grad_probs = mul(grad_own, values, OVER_LAST)
            grad_values = mul(probs.astype(low), grad_own, OVER_FIRST)
            row_dot = jnp.sum(probs * grad_probs, axis=-1, keepdims=True)
            grad_scores = (probs * (grad_probs - row_dot)).astype(low)
            grad_queries = mul(grad_scores, keys) * HDIM ** (-0.5)
            grad_keys = mul(grad_scores, queries, OVER_FIRST) * HDIM ** (-0.5)
            for part, grad in ((0, grad_queries), (1, grad_keys), (2, grad_values)):
                if part < 2:
                    grad = grad * cosine[...] - pltpu.roll(grad, HDIM // 2, 1) * sine[...]
                pieces[part, :, own] = grad.astype(low)
        for part, weight in enumerate((wq, wk, wv)):

            @pl.when(pair > 0)
            def _(part=part):
                stage_copy(part, pair - 1).wait()

            stage[part] = mul(normed_turned[...], pieces[part]).astype(low)
            stage_copy(part, pair).start()
            grad_one[...] += mul(pieces[part], weight[...], OVER_LAST)

        @pl.when(at == pl.num_programs(0) - 1)
        def _():
            unit_one, factor_one = unit_of(tokens[...].astype(jnp.float32))
            total = grad_one[...]
            gain_grads[0:1, :] = jnp.sum(total * unit_one, axis=0, keepdims=True)
            grad_unit = total * gains[0:1, :]
            back = factor_one * (
                grad_unit - unit_one * jnp.mean(grad_unit * unit_one, axis=-1, keepdims=True)
            )
            tokens_grad[...] = grad_hidden[...] + back
            for part in range(3):
                stage_copy(part, pair).wait()


def dense_backward(group, step, tokens, cot, segments, gains, qkv_act, attended, hidden, normed_two,
                   routed_grad, qkv_low, out_low, shin_low, shout_spread):
    length, width = tokens.shape
    wide, pairs = 2 * HDIM, HEADS // 2
    cosine, sine = rope_rows(length)
    seg_row = jnp.broadcast_to(segments, (8, length))
    seg_column = jnp.broadcast_to(segments.T, (length, 128))
    low = jnp.bfloat16
    once = pl.Buffered(1)

    def whole(*shape):
        return pl.BlockSpec(shape, lambda i: (0,) * len(shape), pipeline_mode=once)

    def kept(*shape):
        return pl.BlockSpec(shape, lambda i: (0,) * len(shape))

    def columns(part):
        return pl.BlockSpec((width, wide), lambda i: (0, part * pairs + jnp.maximum(i - 1, 0)))

    rows = pl.BlockSpec((wide, width), lambda i: (jnp.maximum(i - 1, 0), 0))
    return pl.pallas_call(
        functools.partial(backward_kernel, group, step),
        grid=(pairs + 1,),
        in_specs=[
            whole(length, width), whole(length, width), whole(8, length), whole(length, 128),
            whole(8, width), whole(length, HDIM), whole(length, HDIM), whole(length, 3 * width),
            whole(length, width), whole(length, width), whole(length, width), whole(length, width),
            columns(0), columns(1), columns(2), rows,
            whole(*shin_low.shape), whole(*shout_spread.shape),
        ],
        out_specs=[
            kept(length, width), kept(length, width), kept(8, width),
            pl.BlockSpec(memory_space=pl.ANY), rows, kept(*shin_low.shape), kept(*shout_spread.shape),
        ],
        out_shape=[
            jax.ShapeDtypeStruct((length, width), jnp.float32),
            jax.ShapeDtypeStruct((length, width), jnp.float32),
            jax.ShapeDtypeStruct((8, width), jnp.float32),
            jax.ShapeDtypeStruct((width, 3 * width), low),
            jax.ShapeDtypeStruct((width, width), low),
            jax.ShapeDtypeStruct(shin_low.shape, low),
            jax.ShapeDtypeStruct(shout_spread.shape, low),
        ],
        scratch_shapes=[
            pltpu.VMEM((length, width), low), pltpu.VMEM((width, length), low),
            pltpu.VMEM((length, width), low), pltpu.VMEM((length, width), jnp.float32),
            pltpu.VMEM((length, width), jnp.float32), pltpu.VMEM((3, length, wide), low),
            pltpu.VMEM((3, width, wide), low), pltpu.SemaphoreType.DMA((3,)),
        ],
        compiler_params=pltpu.CompilerParams(
            dimension_semantics=("arbitrary",), vmem_limit_bytes=VMEM_MOST
        ),
        name="dense_backward",
    )(tokens, cot, seg_row, seg_column, gains, jnp.asarray(cosine), jnp.asarray(sine), qkv_act, attended,
      hidden, normed_two, routed_grad, qkv_low, qkv_low, qkv_low, out_low, shin_low, shout_spread)


def expert_kernel(parts, per_step, cap, *refs):
    normed, cot, info = refs[:3]
    ins, outs_w = refs[3 : 3 + parts], refs[3 + parts : 3 + 2 * parts]
    result_ref, input_ref, own_grad = refs[3 + 2 * parts : 6 + 2 * parts]
    sent = refs[6 + 2 * parts : 5 + 3 * parts]
    scratch = refs[5 + 3 * parts :]
    rows_x, rows_g, gate_col, result_acc, input_acc = scratch[:5]
    sums = (own_grad,) + tuple(scratch[5:])
    step = pl.program_id(0)
    tok = normed.shape[1]
    width = normed.shape[2]
    chunk = 256

    @pl.when(step == 0)
    def _():
        for total in sums:
            total[...] = jnp.zeros_like(total)

    slots = lax.broadcasted_iota(jnp.int32, (cap, tok), 0).astype(jnp.float32)
    for s in range(per_step):
        hit = slots == info[s, 0:1, :]
        picks = jnp.where(hit, 1.0, 0.0).astype(jnp.bfloat16)
        gates = jnp.sum(jnp.where(hit, info[s, 1:2, :], 0.0), axis=1, keepdims=True)
        window = pl.ds(s * cap, cap)
        gate_col[window, :] = jnp.broadcast_to(gates, (cap, 128))
        rows_x[window, :] = jnp.dot(picks, normed[s], preferred_element_type=jnp.float32).astype(
            jnp.bfloat16
        )
        taken = jnp.dot(picks, cot[s], preferred_element_type=jnp.float32)
        rows_g[window, :] = (gates * taken).astype(jnp.bfloat16)
    across = (((1,), (1,)), ((), ()))
    down = (((0,), (0,)), ((), ()))

    def mul(left, right, dims):
        return lax.dot_general(left, right, dims, preferred_element_type=jnp.float32)

    straight = (((1,), (0,)), ((), ()))
    for p in range(parts):
        gate_pre = mul(rows_x[...], ins[p][0], across)
        up_pre = mul(rows_x[...], ins[p][1], across)
        sigmoid = jax.nn.sigmoid(gate_pre)
        active = (gate_pre * sigmoid * up_pre).astype(jnp.bfloat16)
        grad_act = mul(rows_g[...], outs_w[p][...], across)
        grad_up = (grad_act * gate_pre * sigmoid).astype(jnp.bfloat16)
        grad_gate = (grad_act * up_pre * sigmoid * (1.0 + gate_pre * (1.0 - sigmoid))).astype(
            jnp.bfloat16
        )
        for first in range(0, width, chunk):
            window = slice(first, first + chunk)
            result = mul(active, outs_w[p][:, window], straight)
            back = mul(grad_gate, ins[p][0, :, window], straight) + mul(
                grad_up, ins[p][1, :, window], straight
            )
            if p == 0:
                result_acc[:, window] = result
                input_acc[:, window] = back
            else:
                result_acc[:, window] += result
                input_acc[:, window] += back
            sums[p][0, :, window] += mul(grad_gate, rows_x[:, window], down)
            sums[p][1, :, window] += mul(grad_up, rows_x[:, window], down)
            sums[p][2, :, window] += mul(active, rows_g[:, window], down)
    for s in range(per_step):
        hit = slots == info[s, 0:1, :]
        picks = jnp.where(hit, 1.0, 0.0).astype(jnp.bfloat16)
        window = pl.ds(s * cap, cap)
        rounded = result_acc[window, :].astype(jnp.bfloat16).astype(jnp.float32)
        weighted = (gate_col[window, 0:1] * rounded).astype(jnp.bfloat16)
        result_ref[s] = mul(picks, weighted, down).astype(jnp.bfloat16)
        input_ref[s] = mul(picks, input_acc[window, :].astype(jnp.bfloat16), down).astype(
            jnp.bfloat16
        )

    @pl.when(step == pl.num_programs(0) - 1)
    def _():
        for p in range(1, parts):
            sent[p - 1][...] = sums[p][...].astype(jnp.bfloat16)


def expert_pass(normed_all, cot_all, info, ins, outs_w, cap):
    ep_count, tok, width = normed_all.shape
    parts = len(ins)
    hidden = ins[0].shape[1]
    per_step = max(1, min(ep_count, 256 // cap))
    rows = per_step * cap
    token_spec = pl.BlockSpec((per_step, tok, width), lambda i: (i, 0, 0))
    once = pl.Buffered(1)
    in_specs = [token_spec, token_spec, pl.BlockSpec((per_step, 2, tok), lambda i: (i, 0, 0))]
    in_specs += [
        pl.BlockSpec((2, hidden, width), lambda i: (0, 0, 0), pipeline_mode=once)
    ] * parts
    in_specs += [pl.BlockSpec((hidden, width), lambda i: (0, 0), pipeline_mode=once)] * parts
    grad_spec = pl.BlockSpec((3, hidden, width), lambda i: (0, 0, 0), pipeline_mode=once)
    token_shape = jax.ShapeDtypeStruct((ep_count, tok, width), jnp.bfloat16)
    out_shape = [token_shape, token_shape, jax.ShapeDtypeStruct((3, hidden, width), jnp.float32)]
    out_shape += [jax.ShapeDtypeStruct((3, hidden, width), jnp.bfloat16)] * (parts - 1)
    scratch = [
        pltpu.VMEM((rows, width), jnp.bfloat16),
        pltpu.VMEM((rows, width), jnp.bfloat16),
        pltpu.VMEM((rows, 128), jnp.float32),
        pltpu.VMEM((rows, width), jnp.float32),
        pltpu.VMEM((rows, width), jnp.float32),
    ] + [pltpu.VMEM((3, hidden, width), jnp.float32)] * (parts - 1)
    found = pl.pallas_call(
        functools.partial(expert_kernel, parts, per_step, cap),
        grid=(ep_count // per_step,),
        in_specs=in_specs,
        out_specs=[token_spec, token_spec] + [grad_spec] * parts,
        out_shape=out_shape,
        scratch_shapes=scratch,
        compiler_params=pltpu.CompilerParams(
            dimension_semantics=("arbitrary",), vmem_limit_bytes=VMEM_MOST
        ),
        cost_estimate=pl.CostEstimate(
            flops=18 * ep_count * cap * parts * hidden * width,
            bytes_accessed=8 * ep_count * tok * width + 30 * parts * hidden * width,
            transcendentals=ep_count * cap * parts * hidden,
        ),
        name="expert_pass",
    )(normed_all, cot_all, info, *ins, *outs_w)
    return found[0], found[1], found[2], found[3:]


def nearest(place):
    count = place.na
    table = [sorted(range(count), key=lambda other: abs(other - own)) for own in range(count)]

    def chip_at(r):
        found = jnp.int32(0)
        for own in range(count):
            for rank in range(count):
                found = found + jnp.where((place.a == own) & (r == rank), table[own][rank], 0)
        return found

    return chip_at


def fused_kernel(parts, ep_count, tp_count, cap, *refs):
    normed, info, cot = refs[:3]
    w_in, w_out = refs[3 : 3 + parts], refs[3 + parts : 3 + 2 * parts]
    refs = refs[3 + 2 * parts :]
    result_ref, routed_ref, own_grad = refs[:3]
    sent = refs[3 : 2 + parts]
    scratch = refs[2 + parts :]
    tok, infos, cots, vin, vout, own, sib, sib_stage, bland, aland, res_stage = scratch[:11]
    rows_x, rows_g, gate_col, result_acc, input_acc, stage = scratch[11:17]
    sums = (own_grad,) + tuple(scratch[17 : 16 + parts])
    (tok_recv, tok_send, local_sem, cot_sem, sib_recv, sib_send, b_recv, b_send, a_recv, a_send,
     res_sem, stage_sem) = scratch[16 + parts :]
    place = Place(ep_count, tp_count)
    na, a, b, core = place.na, place.a, place.b, place.core
    width = normed.shape[1]
    me = (a * 2 + b) * 2 + core
    chip_at = nearest(place)
    chunk = 256

    def device(a_, b_, core_):
        return ((a_ * 2 + b_) * 2 + core_, place.t)

    sibling, across = device(a, b, 1 - core), device(a, 1 - b, core)
    barrier = pltpu.get_barrier_semaphore()
    for target in (sibling, across):
        pl.semaphore_signal(barrier, inc=1, device_id=target, device_id_type=MESH)
    for step in range(1, na):
        pl.semaphore_signal(
            barrier, inc=1, device_id=device(lax.rem(a + step, na), b, core), device_id_type=MESH
        )
    pl.semaphore_wait(barrier, na + 1)

    def hop(index, number, target, first=False):
        return [
            pltpu.make_async_remote_copy(
                src_ref=own_block if first else held.at[index],
                dst_ref=held.at[index],
                send_sem=tok_send.at[k, number],
                recv_sem=tok_recv.at[k, index],
                device_id=target,
                device_id_type=MESH,
            )
            for k, (own_block, held) in enumerate(((normed, tok), (info, infos)))
        ]

    def start(copies):
        for copy in copies:
            copy.start()

    def arrived(index):
        for k, held in enumerate((tok, infos)):
            pltpu.make_async_copy(held.at[index], held.at[index], tok_recv.at[k, index]).wait()

    ends = []

    def launch(on, copies):
        def finish():
            for copy in copies:
                copy.wait_send()

        guarded(on, lambda: start(copies))
        ends.append((on, finish))

    up, down_ok = a + 1 < na, a > 0
    launch(up, hop(me, 0, device(a + 1, b, core), True))
    launch(down_ok, hop(me, 1, device(a - 1, b, core), True))
    launch(None, hop(me, 2, across, True))
    launch(None, hop(me, 3, sibling, True))
    loads = [pltpu.make_async_copy(normed, tok.at[me], local_sem.at[0])]
    loads.append(pltpu.make_async_copy(info, infos.at[me], local_sem.at[1]))
    for p in range(parts):
        loads.append(pltpu.make_async_copy(w_in[p], vin.at[p], local_sem.at[2 + 2 * p]))
        loads.append(pltpu.make_async_copy(w_out[p], vout.at[p], local_sem.at[3 + 2 * p]))
    start(loads)

    def chip_of(k):
        side = lax.rem(k, 2)
        return chip_at(k // 2) * 2 + jnp.where(side == 0, b, 1 - b)

    def cot_copies(k):
        chip, buffer = chip_of(k), lax.rem(k, 2)
        return [
            pltpu.make_async_copy(cot.at[chip * 2 + j], cots.at[buffer, j], cot_sem.at[buffer, j])
            for j in range(2)
        ]

    start(cot_copies(jnp.int32(0)))
    for total in sums:
        total[...] = jnp.zeros_like(total)
    for load in loads:
        load.wait()

    def from_a(r):
        other = chip_at(r)
        index = (other * 2 + b) * 2 + core
        arrived(index)
        first = 4 + 3 * (r - 1)
        beyond = jnp.where(other > a, a - 1, a + 1)
        on = (beyond >= 0) & (beyond < na)
        copies = hop(index, first, device(beyond, b, core))
        pl.when(on)(lambda: start(copies))
        start(hop(index, first + 1, across))
        start(hop(index, first + 2, sibling))

    def from_b(r):
        index = (chip_at(r) * 2 + 1 - b) * 2 + core
        arrived(index)
        start(hop(index, 4 + 3 * (na - 1) + r, sibling))

    def sent_from_a(r):
        other = chip_at(r)
        index = (other * 2 + b) * 2 + core
        first = 4 + 3 * (r - 1)
        beyond = jnp.where(other > a, a - 1, a + 1)
        on = (beyond >= 0) & (beyond < na)

        def finish(number):
            for copy in hop(index, number, sibling):
                copy.wait_send()

        pl.when(on)(lambda: finish(first))
        finish(first + 1)
        finish(first + 2)

    def sib_wait(chip):
        pltpu.make_async_copy(sib.at[chip], sib.at[chip], sib_recv.at[chip]).wait()

    def to_b(r):
        chip = chip_at(r) * 2 + 1 - b
        sib_wait(chip)
        add_into(own.at[chip], [own.at[chip], sib.at[chip]], own.dtype)
        pltpu.make_async_remote_copy(
            src_ref=own.at[chip],
            dst_ref=bland.at[r],
            send_sem=b_send.at[r],
            recv_sem=b_recv.at[r],
            device_id=across,
            device_id_type=MESH,
        ).start()

    def b_wait(r):
        pltpu.make_async_copy(bland.at[r], bland.at[r], b_recv.at[r]).wait()

    def to_a(r):
        other = chip_at(r)
        chip = other * 2 + b
        sib_wait(chip)
        b_wait(r)
        add_into(own.at[chip], [own.at[chip], sib.at[chip], bland.at[r]], own.dtype)
        pltpu.make_async_remote_copy(
            src_ref=own.at[chip],
            dst_ref=aland.at[a],
            send_sem=a_send.at[r],
            recv_sem=a_recv.at[a],
            device_id=device(other, b, core),
            device_id_type=MESH,
        ).start()

    over_last = (((1,), (1,)), ((), ()))
    over_first = (((0,), (0,)), ((), ()))
    straight = (((1,), (0,)), ((), ()))

    def mul(left, right, dims):
        return lax.dot_general(left, right, dims, preferred_element_type=jnp.float32)

    slots = lax.broadcasted_iota(jnp.int32, (cap, normed.shape[0]), 0).astype(jnp.float32)

    def picks_of(source):
        return slots == infos[source, pl.ds(me, 1), :]

    def work(k, carry):
        chip, buffer = chip_of(k), lax.rem(k, 2)

        @pl.when(k + 1 < 2 * na)
        def _():
            start(cot_copies(k + 1))

        for r in range(na):
            if r == 1:
                pl.when(k == 1)(functools.partial(from_a, r))
            pl.when(k == 2 * r + 1)(functools.partial(from_b, r))
        pl.when(k == 2 * na - 2)(functools.partial(to_b, 1))
        arrived(chip * 2 + 1 - core)
        for copy in cot_copies(k):
            copy.wait()
        for j in range(2):
            hit = picks_of(chip * 2 + j)
            picks = jnp.where(hit, 1.0, 0.0).astype(jnp.bfloat16)
            gate_row = infos[chip * 2 + j, pl.ds(ep_count + me, 1), :]
            gates = jnp.sum(jnp.where(hit, gate_row, 0.0), axis=1, keepdims=True)
            window = pl.ds(j * cap, cap)
            gate_col[window, :] = jnp.broadcast_to(gates, (cap, 128))
            rows_x[window, :] = mul(picks, tok[chip * 2 + j], straight).astype(jnp.bfloat16)
            taken = mul(picks, cots[buffer, j], straight)
            rows_g[window, :] = (gates * taken).astype(jnp.bfloat16)
        for p in range(parts):
            gate_pre = mul(rows_x[...], vin[p, 0], over_last)
            up_pre = mul(rows_x[...], vin[p, 1], over_last)
            sigmoid = jax.nn.sigmoid(gate_pre)
            active = (gate_pre * sigmoid * up_pre).astype(jnp.bfloat16)
            grad_act = mul(rows_g[...], vout[p], over_last)
            grad_up = (grad_act * gate_pre * sigmoid).astype(jnp.bfloat16)
            grad_gate = (
                grad_act * up_pre * sigmoid * (1.0 + gate_pre * (1.0 - sigmoid))
            ).astype(jnp.bfloat16)
            for first in range(0, width, chunk):
                window = slice(first, first + chunk)
                result = mul(active, vout[p, :, window], straight)
                back = mul(grad_gate, vin[p, 0, :, window], straight) + mul(
                    grad_up, vin[p, 1, :, window], straight
                )
                if p == 0:
                    result_acc[:, window] = result
                    input_acc[:, window] = back
                else:
                    result_acc[:, window] += result
                    input_acc[:, window] += back
                sums[p][0, :, window] += mul(grad_gate, rows_x[:, window], over_first)
                sums[p][1, :, window] += mul(grad_up, rows_x[:, window], over_first)
                sums[p][2, :, window] += mul(active, rows_g[:, window], over_first)
            if p == 0:
                for r in range(2, na):
                    pl.when(k == 2 * r - 2)(functools.partial(from_a, r))
                    if r < na - 1:
                        pl.when(k == 2 * na - 2)(functools.partial(to_b, r))

        @pl.when(k > 0)
        def _():
            pltpu.make_async_copy(sib_stage, sib_stage, sib_send.at[0]).wait()
            for j in range(2):
                pltpu.make_async_copy(res_stage.at[j], res_stage.at[j], res_sem.at[j]).wait()

        for other in range(2):
            j = 1 - core if other == 0 else core
            source = chip * 2 + j
            picks = jnp.where(picks_of(source), 1.0, 0.0).astype(jnp.bfloat16)
            window = pl.ds(pl.multiple_of(j * cap, cap), cap)
            back = mul(picks, input_acc[window, :].astype(jnp.bfloat16), over_first)
            if other == 0:
                sib_stage[...] = back.astype(jnp.bfloat16)
                pltpu.make_async_remote_copy(
                    src_ref=sib_stage,
                    dst_ref=sib.at[chip],
                    send_sem=sib_send.at[0],
                    recv_sem=sib_recv.at[chip],
                    device_id=sibling,
                    device_id_type=MESH,
                ).start()
            else:
                own[chip] = back.astype(jnp.bfloat16)
            rounded = result_acc[window, :].astype(jnp.bfloat16).astype(jnp.float32)
            weighted = (gate_col[window, 0:1] * rounded).astype(jnp.bfloat16)
            res_stage[other] = mul(picks, weighted, over_first).astype(jnp.bfloat16)
            pltpu.make_async_copy(res_stage.at[other], result_ref.at[source], res_sem.at[other]).start()
        return carry

    lax.fori_loop(0, 2 * na, work, 0)
    to_b(na - 1)
    for p in range(1, parts):
        for q in range(3):
            if p > 1 or q > 0:
                pltpu.make_async_copy(stage, stage, stage_sem.at[0]).wait()
            stage[...] = sums[p][q].astype(jnp.bfloat16)
            pltpu.make_async_copy(stage, sent[p - 1].at[q], stage_sem.at[0]).start()
    for r in range(1, na):
        if r == na - 1:
            to_b(0)
        to_a(r)
    chip = a * 2 + b
    sib_wait(chip)
    b_wait(0)
    add_into(routed_ref, [own.at[chip], sib.at[chip], bland.at[0]], jnp.float32)
    for r in range(1, na):
        other = chip_at(r)
        pltpu.make_async_copy(aland.at[other], aland.at[other], a_recv.at[other]).wait()
        add_into(routed_ref, [routed_ref, aland.at[other]], jnp.float32)
    for on, finish in ends:
        guarded(on, finish)
    for r in range(na):
        if r:
            sent_from_a(r)
            pltpu.make_async_copy(own.at[0], own.at[0], a_send.at[r]).wait()
        for copy in hop(me, 4 + 3 * (na - 1) + r, sibling):
            copy.wait_send()
        pltpu.make_async_copy(own.at[0], own.at[0], b_send.at[r]).wait()
    pltpu.make_async_copy(sib_stage, sib_stage, sib_send.at[0]).wait()
    for j in range(2):
        pltpu.make_async_copy(res_stage.at[j], res_stage.at[j], res_sem.at[j]).wait()
    pltpu.make_async_copy(stage, stage, stage_sem.at[0]).wait()


def fused_experts(ep_count, tp_count, collective_id, normed, info, cot_all, ins, outs_w, cap):
    place = Place(ep_count, tp_count)
    tok, width = normed.shape
    parts = len(ins)
    hidden = ins[0].shape[1]
    na, chips, rows = place.na, 2 * place.na, 2 * cap
    low = jnp.bfloat16
    anywhere = pl.BlockSpec(memory_space=pl.ANY)
    inside = pl.BlockSpec(memory_space=pltpu.VMEM)
    out_shape = [
        jax.ShapeDtypeStruct((ep_count, tok, width), low),
        jax.ShapeDtypeStruct((tok, width), jnp.float32),
        jax.ShapeDtypeStruct((3, hidden, width), jnp.float32),
    ] + [jax.ShapeDtypeStruct((3, hidden, width), low)] * (parts - 1)
    scratch = [
        pltpu.VMEM((ep_count, tok, width), low),
        pltpu.VMEM((ep_count, 2 * ep_count, tok), jnp.float32),
        pltpu.VMEM((2, 2, tok, width), low),
        pltpu.VMEM((parts, 2, hidden, width), low),
        pltpu.VMEM((parts, hidden, width), low),
        pltpu.VMEM((chips, tok, width), low),
        pltpu.VMEM((chips, tok, width), low),
        pltpu.VMEM((tok, width), low),
        pltpu.VMEM((na, tok, width), low),
        pltpu.VMEM((na, tok, width), low),
        pltpu.VMEM((2, tok, width), low),
        pltpu.VMEM((rows, width), low),
        pltpu.VMEM((rows, width), low),
        pltpu.VMEM((rows, 128), jnp.float32),
        pltpu.VMEM((rows, width), jnp.float32),
        pltpu.VMEM((rows, width), jnp.float32),
        pltpu.VMEM((hidden, width), low),
    ] + [pltpu.VMEM((3, hidden, width), jnp.float32)] * (parts - 1)
    dma = pltpu.SemaphoreType.DMA
    scratch += [
        dma((2, ep_count)), dma((2, 4 + 3 * (na - 1) + na)), dma((2 + 2 * parts,)), dma((2, 2)),
        dma((chips,)), dma((1,)), dma((na,)), dma((na,)), dma((na,)), dma((na,)), dma((2,)), dma((1,)),
    ]
    found = pl.pallas_call(
        functools.partial(fused_kernel, parts, ep_count, tp_count, cap),
        in_specs=[anywhere] * (3 + 2 * parts),
        out_specs=[anywhere, inside, inside] + [anywhere] * (parts - 1),
        out_shape=out_shape,
        scratch_shapes=scratch,
        compiler_params=pltpu.CompilerParams(
            collective_id=collective_id, has_side_effects=True, vmem_limit_bytes=VMEM_MOST
        ),
        name="fused_experts",
    )(normed, info, cot_all, *ins, *outs_w)
    return found[0], found[1], found[2], found[3:]


def adam_update(weight, gradient, first, second, clip_scale, rate, decay):
    clipped = gradient * clip_scale
    first_new = BETA_ONE * first + (1.0 - BETA_ONE) * clipped
    second_new = BETA_TWO * second + (1.0 - BETA_TWO) * clipped * clipped
    corr_one = 1.0 - BETA_ONE**STEP
    corr_two = 1.0 - BETA_TWO**STEP
    stepped = first_new / corr_one / (jnp.sqrt(second_new / corr_two) + ADAM_EPS)
    weight_new = weight - rate * (stepped + decay * weight)
    return (weight_new, first_new, second_new, weight_new.astype(jnp.bfloat16))


def per_device(
    tokens,
    cotangent,
    segments,
    routes,
    gates,
    qkv_weight,
    qkv_first,
    qkv_second,
    out_weight,
    out_first,
    out_second,
    shared_in,
    shared_in_first,
    shared_in_second,
    shared_out,
    shared_out_first,
    shared_out_second,
    expert_in,
    expert_in_first,
    expert_in_second,
    expert_out,
    expert_out_first,
    expert_out_second,
    norm_gains,
    gains_first,
    gains_second,
):
    tok_count = tokens.shape[0]
    width = tokens.shape[1]
    ep_count = lax.axis_size("ep")
    tp_count = lax.axis_size("tp")
    devices = ep_count * tp_count
    capacity = tok_count * 8 // ep_count
    low = jnp.bfloat16
    in_own, out_own = expert_in[0].astype(low), expert_out[0].astype(low)
    gain_columns = jnp.pad(norm_gains.T.astype(low), ((0, 0), (0, 126)))
    group = shared_out.shape[0]
    step = 16 * ((group + 15) // 16)
    while step & (step - 1):
        step += 16
    shout_own = jnp.pad(shared_out.astype(low), ((0, step - group), (0, 0)))
    qkv_low, out_low, gains_low, cot_all, in_others, out_others, shin_low, shout_low = gather(
        ep_count,
        tp_count,
        1,
        "gather_weights",
        [
            ("auv", [qkv_weight.astype(low), out_weight.astype(low), gain_columns]),
            ("ab", [cotangent]),
            ("t", [in_own, out_own]),
            ("tba", [shared_in.astype(low), shout_own]),
        ],
    )
    qkv_low = qkv_low.reshape(width, 3 * width)
    out_low = out_low.reshape(width, width)
    shin_low = shin_low.reshape(width, 2 * FF)
    shout_low = shout_low.reshape(devices * step, width)
    gains = jnp.pad(gains_low.reshape(width, 128)[:, :2].T.astype(jnp.float32), ((0, 6), (0, 0)))
    ins_low = [in_own] + [in_others[s] for s in range(tp_count - 1)]
    outs_low = [out_own] + [out_others[s] for s in range(tp_count - 1)]
    expert_ids = jnp.arange(ep_count, dtype=jnp.int32)
    chosen = routes[:, :, None] == expert_ids[None, None, :]
    onehot = jnp.sum(chosen.astype(jnp.float32), axis=1)
    gate_of = jnp.sum(jnp.where(chosen, gates[:, :, None], 0.0), axis=1)
    earlier = jnp.tril(jnp.ones((tok_count, tok_count), low), -1)
    rank = jnp.dot(earlier, onehot.astype(low), preferred_element_type=jnp.float32)
    slot_of = jnp.where(onehot > 0.0, rank, -1.0)
    info_own = jnp.concatenate([slot_of, gate_of], axis=1).T
    qkv_act, attended, hidden, normed_two = attention_forward(
        tokens, segments, gains, qkv_low, out_low
    )
    chips = ep_count // 2
    held = tok_count * width * 2 * (ep_count + 3 * chips + 12) + 9 * tp_count * expert_in.size
    if Place(ep_count, tp_count).nb == 2 and held <= VMEM_MOST * 9 // 10:
        result_part, routed_grad, own_grad, sent_grads = fused_experts(
            ep_count, tp_count, 3, normed_two, info_own, cot_all, ins_low, outs_low, capacity
        )
    else:
        normed_all, info_all = gather(
            ep_count, tp_count, 2, "gather_tokens", [("ab", [normed_two, info_own])]
        )
        info = lax.dynamic_index_in_dim(
            info_all.reshape(ep_count, 2, ep_count, tok_count),
            lax.axis_index("ep"),
            axis=2,
            keepdims=False,
        )
        result_part, input_part, own_grad, sent_grads = expert_pass(
            normed_all, cot_all, info, ins_low, outs_low, capacity
        )
        (routed_grad,) = scatter_add(ep_count, tp_count, 3, "scatter_inputs", [("ab", [input_part])])
    base, tokens_grad, gain_grads, qkv_grad, out_grad, shin_grad, shout_grad = dense_backward(
        group, step, tokens, cotangent, segments, gains, qkv_act, attended, hidden, normed_two,
        routed_grad, qkv_low, out_low, shin_low, shout_low,
    )
    gain_rows = jnp.pad(gain_grads[:2].T.astype(low), ((0, 0), (0, 126)))

    def by_owner(grad):
        return grad.reshape(devices, -1, grad.shape[1])

    qkv_part, out_part, gains_part, shin_part, shout_part, routed, *others = scatter_all(
        ep_count,
        tp_count,
        (4, 6, 7, 8),
        "scatter_weights",
        [
            ("auv", [by_owner(qkv_grad), by_owner(out_grad), by_owner(gain_rows)]),
            ("tba", [by_owner(shin_grad), by_owner(shout_grad)]),
            ("ab", [result_part]),
            ("t", [jnp.stack(sent_grads)]),
        ],
    )
    for shift in range(tp_count - 1):
        own_grad = own_grad + others[0][shift].astype(jnp.float32)
    block_out = (base + routed).astype(low)
    exin_part, exout_part = own_grad[None, :2], own_grad[2:]
    extra = jnp.sum(own_grad * own_grad, axis=(0, 1))[None, :]
    grad_norm = jnp.sqrt(
        sum_of_squares(
            ep_count, tp_count, 5, [qkv_part, out_part, gains_part, shin_part, shout_part], extra
        )
    )
    shout_part = shout_part[:group]
    gains_part = gains_part[:, :2].T
    clip_scale = jnp.minimum(1.0, CLIP_LEVEL / (grad_norm + 1e-06))
    qkv_new, qkv_first_new, qkv_second_new, qkv_copy = adam_update(
        qkv_weight, qkv_part, qkv_first, qkv_second, clip_scale, MATRIX_RATE, WEIGHT_DECAY
    )
    out_new, out_first_new, out_second_new, out_copy = adam_update(
        out_weight, out_part, out_first, out_second, clip_scale, MATRIX_RATE, WEIGHT_DECAY
    )
    shin_new, shin_first_new, shin_second_new, shin_copy = adam_update(
        shared_in,
        shin_part,
        shared_in_first,
        shared_in_second,
        clip_scale,
        MATRIX_RATE,
        WEIGHT_DECAY,
    )
    shout_new, shout_first_new, shout_second_new, shout_copy = adam_update(
        shared_out,
        shout_part,
        shared_out_first,
        shared_out_second,
        clip_scale,
        MATRIX_RATE,
        WEIGHT_DECAY,
    )
    exin_new, exin_first_new, exin_second_new, exin_copy = adam_update(
        expert_in,
        exin_part,
        expert_in_first,
        expert_in_second,
        clip_scale,
        MATRIX_RATE,
        WEIGHT_DECAY,
    )
    exout_new, exout_first_new, exout_second_new, exout_copy = adam_update(
        expert_out,
        exout_part,
        expert_out_first,
        expert_out_second,
        clip_scale,
        MATRIX_RATE,
        WEIGHT_DECAY,
    )
    gains_new, gains_first_new, gains_second_new, gains_copy = adam_update(
        norm_gains, gains_part, gains_first, gains_second, clip_scale, GAIN_RATE, 0.0
    )
    return (
        block_out,
        tokens_grad,
        grad_norm,
        qkv_new,
        qkv_first_new,
        qkv_second_new,
        qkv_copy,
        out_new,
        out_first_new,
        out_second_new,
        out_copy,
        shin_new,
        shin_first_new,
        shin_second_new,
        shin_copy,
        shout_new,
        shout_first_new,
        shout_second_new,
        shout_copy,
        exin_new,
        exin_first_new,
        exin_second_new,
        exin_copy,
        exout_new,
        exout_first_new,
        exout_second_new,
        exout_copy,
        gains_new,
        gains_first_new,
        gains_second_new,
        gains_copy,
    )


def solution(mesh):
    placed = (
        P(("ep", "tp"), None),
        P(("ep", "tp"), None),
        P(("ep", "tp"), None),
        P(("ep", "tp"), None),
        P(("ep", "tp"), None),
        P(("ep", "tp"), None),
        P(("ep", "tp"), None),
        P(("ep", "tp"), None),
        P(("ep", "tp"), None),
        P(("ep", "tp"), None),
        P(("ep", "tp"), None),
        P(("ep", "tp"), None),
        P(("ep", "tp"), None),
        P(("ep", "tp"), None),
        P(("ep", "tp"), None),
        P(("ep", "tp"), None),
        P(("ep", "tp"), None),
        P("ep", None, "tp", None),
        P("ep", None, "tp", None),
        P("ep", None, "tp", None),
        P("ep", "tp", None),
        P("ep", "tp", None),
        P("ep", "tp", None),
        P(None, ("ep", "tp")),
        P(None, ("ep", "tp")),
        P(None, ("ep", "tp")),
    )
    return jax.shard_map(
        per_device,
        mesh=mesh,
        in_specs=placed,
        out_specs=(
            P(("ep", "tp"), None),
            P(("ep", "tp"), None),
            P(),
            P(("ep", "tp"), None),
            P(("ep", "tp"), None),
            P(("ep", "tp"), None),
            P(("ep", "tp"), None),
            P(("ep", "tp"), None),
            P(("ep", "tp"), None),
            P(("ep", "tp"), None),
            P(("ep", "tp"), None),
            P(("ep", "tp"), None),
            P(("ep", "tp"), None),
            P(("ep", "tp"), None),
            P(("ep", "tp"), None),
            P(("ep", "tp"), None),
            P(("ep", "tp"), None),
            P(("ep", "tp"), None),
            P(("ep", "tp"), None),
            P("ep", None, "tp", None),
            P("ep", None, "tp", None),
            P("ep", None, "tp", None),
            P("ep", None, "tp", None),
            P("ep", "tp", None),
            P("ep", "tp", None),
            P("ep", "tp", None),
            P("ep", "tp", None),
            P(None, ("ep", "tp")),
            P(None, ("ep", "tp")),
            P(None, ("ep", "tp")),
            P(None, ("ep", "tp")),
        ),
        check_vma=False,
    )
```

time: 746 us -> 624 us (0.84)
  Pallas kernels: 481 us -> 561 us
  blocking collectives: 60.4 us -> 0 us
  matrix products: 48.3 us -> 0.23 us
  local copies, waits for them, and re-layouts: 54 us -> 12.1 us
  other arithmetic: 66.5 us -> 42.9 us
  between operations: 21.9 us -> 3.06 us
    pallas_call x3 -> x5, Pallas kernels: 256 us -> 390 us  [the longest x1 166 us: scatter_add(): pl.pallas_call(functools.partial(scatter_kernel, ep_count, tp_count, tupl...]
    psum x1 -> x0, blocking collectives: 60.4 us -> none  [per_device(): grad_norm = jnp.sqrt(lax.psum(squares, ('ep', 'tp')))]
    pallas_call x2 -> x1, Pallas kernels: 225 us -> 171 us  [gather(): pl.pallas_call(functools.partial(gather_kernel, ep_count, tp_count, tuple...]
    dot_general x18 -> x0, matrix products: 48.1 us -> none  [the longest x1 5.67 us: per_device(): jnp.dot(normed_one, qkv_low, preferred_element_type=jnp.float32)]
    unnamed x149 -> x67, local copies, waits for them, and re-layouts: 20 us -> 6.14 us
    dot_general x1 -> x0, local copies, waits for them, and re-layouts: 13.8 us -> none  [per_device(): jnp.dot(normed_one, qkv_low, preferred_element_type=jnp.float32)]
    add x5 -> x0, other arithmetic: 8.74 us -> none  [the longest x1 4.58 us: per_device(): own_grad = own_grad + lax.ppermute(sent, 'tp', ring).astype(jnp.float32)]
    reshape x2 -> x0, local copies, waits for them, and re-layouts: 8.2 us -> none  [the longest x1 4.13 us: per_device(): shout_low = shout_low.reshape(FF, width)]
  transfers between devices with their start and end apart: 5 -> 0, of which waited for: 0 -> 0; matrix products, arithmetic and copies ran while one was open for 21% -> 0% of each run, Pallas kernels for 56% -> 0%
where the time goes in v2:
time: 624 us; the launch traced here: 620 us
  Pallas kernels  561 us (90%)
  other arithmetic  42.9 us (7%)
  local copies, waits for them, and re-layouts  12.1 us (2%)
    pallas_call x1, Pallas kernels, gather(): pl.pallas_call(functools.partial(gather_kernel, ep_count, tp_count, tuple...  171 us
    pallas_call x1, Pallas kernels, scatter_add(): pl.pallas_call(functools.partial(scatter_kernel, ep_count, tp_count, tupl...  166 us
    pallas_call x1, Pallas kernels, fused_experts(): pl.pallas_call(functools.partial(fused_kernel, parts, ep_count, tp_count,...  160 us
    pallas_call x1, Pallas kernels, dense_backward(): pl.pallas_call(functools.partial(backward_kernel, group, step), grid=(pai...  38.6 us
    convert_element_type x7, other arithmetic, adam_update(): return (weight_new, first_new, second_new, weight_new.astype(jnp.bfloat16))  24.5 us
    pallas_call x1, Pallas kernels, attention_forward(): pl.pallas_call(forward_kernel, grid=(pairs,), in_specs=[whole(length, wid...  14.4 us

profile of v2, /device:TPU:0, one launch (start us, length us, event | category | flops | bytes accessed | tf_op | source)
XLA Modules:
  0.0 619.6 jit_solution(11389137326238172033)
XLA Ops:
  0.7 4.1 convert_bitcast_fusion.refs_4_.refs_3_
  4.8 1.1 convert_bitcast_fusion.1.refs_5_
  5.9 0.8 convert_element_type.80.refs_0_
  6.7 0.6 pad.19.refs_7_
  7.3 0.7 convert_element_type.88.refs_6_
  8.0 0.7 convert_element_type.81.refs_1_
  9.4 171.0 %gather_weights.1 = (bf16[32,40,3840]{2,1,0:T(8,128)(2,1)}, bf16[32,40,1280]{2,1,0:T(8,128)(2,1)}, bf16[32,40,128]{2,1,0:T(8,128)(2,1)}, bf16[16,256,1280]{2,1,0...) custom-call(bf16[40,3840]{1,0:T(8,128)(2,1)} %convert_element_type.8, ...), custom_call_target="tpu_custom_call" | custom-call | tf_op jit(solution)/shard_map/gather_weights/pallas_call | solution.py:349
  180.3 1.1 copy.129
  181.5 0.6 pad_convert_fusion.gains
  182.1 0.8 broadcast_in_dim.50.seg_column
  183.5 14.4 %attention_forward.1 = (bf16[256,3840]{1,0:T(8,128)(2,1)}, bf16[256,1280]{1,0:T(8,128)(2,1)}, f32[256,1280]{1,0:T(8,128)}, bf16[256,1280]{1,0:T(8,128)(2,1)}) custom-call(bf16[256,1280]{1,0:T(8,128)(2,1)} %tokens.3, s32[8,256]{1,0:T(8,128)} %broadcast_in_dim.49.seg_row, s32[256,128]{1,0:T(8,128)} %broadcast_in_dim.50.seg_column, ...), custom_call_target="tpu_custom_call" | custom-call | tf_op jit(solution)/shard_map/attention_forward/pallas_call | solution.py:791
  198.1 0.6 maximum_bitcast_fusion.refs_1_
  198.8 160.2 %fused_experts.1 = (bf16[16,256,1280]{2,1,0:T(8,128)(2,1)}, f32[256,1280]{1,0:T(8,128)}, f32[3,448,1280]{2,1,0:T(8,128)}, bf16[3,448,1280]{2,1,0:T(8,128)(2,1)}) custom-call(bf16[256,1280]{1,0:T(8,128)(2,1)} %get-tuple-element.67.refs_0_.normed_two, f32[32,256]{1,0:T(8,128)} %maximum_bitcast_fusion.refs_1_, ...), custom_call_target="tpu_custom_call" | custom-call | tf_op jit(solution)/shard_map/fused_experts/pallas_call | solution.py:1449
  359.0 38.6 %dense_backward.1 = (f32[256,1280]{1,0:T(8,128)}, f32[256,1280]{1,0:T(8,128)}, f32[8,1280]{1,0:T(8,128)}, bf16[1280,3840]{1,0:T(8,128)(2,1)}, bf16[1280,1280]{1,...) custom-call(bf16[256,1280]{1,0:T(8,128)(2,1)} %tokens.3, bf16[256,1280]{1,0:T(8,128)(2,1)} %cot.1, ...), custom_call_target="tpu_custom_call" | custom-call | tf_op jit(solution)/shard_map/dense_backward/pallas_call | solution.py:946
  397.6 0.8 fusion.15
  398.6 0.8 pad.22.clone
  399.4 166.4 %scatter_weights_0.1 = (f32[40,3840]{1,0:T(8,128)}, f32[40,1280]{1,0:T(8,128)}, f32[40,128]{1,0:T(8,128)}, f32[40,1792]{1,0:T(8,128)}, f32[32,1280]{1,0:T(8,128)...) custom-call(bf16[32,40,3840]{2,1,0:T(8,128)(2,1)} %bitcast.54, bf16[32,40,1280]{2,1,0:T(8,128)(2,1)} %bitcast.58, ...), custom_call_target="tpu_custom_call" | custom-call | tf_op jit(solution)/shard_map/scatter_weights_0/pallas_call | solution.py:666
  565.9 7.6 %multiply_reduce_fusion = (f32[1280]{0:T(1024)S(1)}, f32[3,448,1280]{2,1,0:T(8,128)}) fusion(f32[3,448,1280]{2,1,0:T(8,128)} %get-tuple-element.89, bf16[1,3,448,1280]{3,2,1,0:T(8,128)(2,1)} %get-tuple-element.90), kind=kLoop, calls=%fused_computation.2 | loop fusion | flops 6880000 | bytes 17208320 | tf_op jit(solution)/shard_map/reduce_sum | solution.py:1591
  574.1 10.7 %sum_of_squares.1 = f32[8,128]{1,0:T(8,128)} custom-call(f32[40,3840]{1,0:T(8,128)} %get-tuple-element.84.refs_0_, f32[40,1280]{1,0:T(8,128)} %get-tuple-element.85.refs_1_, f32[40,128]{1,0:T(8,128)} %get-tuple-element.86.refs_2_, f32[40,1792]{1,0:T(8,128)} %get-tuple-element.87.refs_3_, f32[32,1280]{1,0:T(8,128)} %get-tuple-element.88.refs_4_, ...), custom_call_target="tpu_custom_call" | custom-call | tf_op jit(solution)/shard_map/sum_of_squares/pallas_call | solution.py:441
  584.9 1.3 reduce_sum.39
  587.3 0.7 copy.124
  588.0 0.7 copy.123
  588.7 1.4 fusion.18
  590.1 1.4 copy.125
  591.4 1.3 copy.128
  594.0 8.2 %fusion.21 = (bf16[1,448,1280]{2,1,0:T(8,128)(2,1)}, f32[1,448,1280]{2,1,0:T(8,128)}, f32[1,448,1280]{2,1,0:T(8,128)}, f32[1,448,1280]{2,1,0:T(8,128)}) fusion(f32[1,448,1280]{2,1,0:T(8,128)} %param.50, f32[]{:T(128)S(6)} %min.3, f32[3,448,1280]{2,1,0:T(8,128)} %get-tuple-element.248, f32[1,448,1280]{2,1,0:T(8,128)} %param.51, f32[1,448,1280]{2,1,0:T(8,128)} %param.52), kind=kLoop, calls=%fused_computation.61 | loop fusion | flops 9748480 | bytes 17203204 | tf_op jit(solution)/shard_map/convert_element_type | solution.py:1471
  602.3 10.3 %fusion.23 = (bf16[1,2,448,1280]{3,2,1,0:T(8,128)(2,1)}, f32[1,2,448,1280]{3,2,1,0:T(8,128)}, f32[1,2,448,1280]{3,2,1,0:T(8,128)}, f32[1,2,448,1280]{3,2,1,0:T(8,128)}) fusion(f32[1,2,448,1280]{3,2,1,0:T(8,128)} %param.47, f32[]{:T(128)S(6)} %min.3, f32[3,448,1280]{2,1,0:T(8,128)S(1)} %bitcast.51, f32[1,2,448,1280]{3,2,1,0:T(8,128)} %param.48, ...), kind=kLoop, calls=%fused_computation.62 | loop fusion | flops 19496960 | bytes 34406404 | tf_op jit(solution)/shard_map/convert_element_type | solution.py:1471
  612.7 0.9 fusion.25
  613.6 1.1 fusion.27
  614.7 0.9 fusion.29
  615.7 1.7 fusion.31
  617.3 1.0 add_convert_fusion
  (81 shorter events, 4.2 us)
Async XLA Ops:
  0.7 4.1 copy-start
  4.7 1.2 copy-start.1
  4.7 1.9 copy-start.11
  4.7 2.6 copy-start.6
  4.8 3.2 copy-start.8
  4.8 3.9 copy-start.25
  6.7 175.5 %copy-start.24 = (s32[1,256]{1,0:T(1,128)S(1)}, s32[1,256]{1,0:T(1,128)}, u32[]{:S(2)}) copy-start(s32[1,256]{1,0:T(1,128)} %param.32) | copy-start | bytes 3076
  183.5 14.4 %copy-start.22 = (s32[256,7]{0,1:T(8,128)S(1)}, s32[256,7]{0,1:T(8,128)}, u32[]{:S(2)}) copy-start(s32[256,7]{0,1:T(8,128)} %param.33) | copy-start | bytes 21508
  183.5 14.4 %copy-start.23 = (f32[256,7]{0,1:T(8,128)S(1)}, f32[256,7]{0,1:T(8,128)}, u32[]{:S(2)}) copy-start(f32[256,7]{0,1:T(8,128)} %param.34) | copy-start | bytes 21508
  565.9 21.0 %copy-start.26 = (f32[2,40]{1,0:T(2,128)S(1)}, f32[2,40]{1,0:T(2,128)}, u32[]{:S(2)}) copy-start(f32[2,40]{1,0:T(2,128)} %param.54) | copy-start | bytes 964
  565.9 21.1 %copy-start.27 = (f32[2,40]{1,0:T(2,128)S(1)}, f32[2,40]{1,0:T(2,128)}, u32[]{:S(2)}) copy-start(f32[2,40]{1,0:T(2,128)} %param.55) | copy-start | bytes 964
  565.9 21.2 %copy-start.21 = (f32[40,128]{1,0:T(8,128)S(1)}, f32[40,128]{1,0:T(8,128)}, u32[]{:S(2)}) copy-start(f32[40,128]{1,0:T(8,128)} %get-tuple-element.86.refs_2_) | copy-start | bytes 61444
  587.3 14.9 %slice-start = ((s8[6881280]{0:T(1024)(128)(4,1)}), s8[2686976]{0:T(1024)(128)(4,1)S(1)}, s32[]{:S(2)}) async-start(s8[6881280]{0:T(1024)(128)(4,1)} %bitcast.50), calls=%async_computation | async-start | bytes 5373952
  594.0 8.2 %slice-start.1 = ((s8[6881280]{0:T(1024)(128)(4,1)}), s8[4194304]{0:T(1024)(128)(4,1)S(1)}, s32[]{:S(2)}) async-start(s8[6881280]{0:T(1024)(128)(4,1)} %bitcast.50), calls=%async_computation.1 | async-start | bytes 8388608
  602.2 10.4 %copy-start.10 = (f32[32,1280]{1,0:T(8,128)S(1)}, f32[32,1280]{1,0:T(8,128)}, u32[]{:S(2)}) copy-start(f32[32,1280]{1,0:T(8,128)} %get-tuple-element.88.refs_4_) | copy-start | bytes 491524
  602.2 10.4 %copy-start.12 = (f32[28,1280]{1,0:T(8,128)S(1)}, f32[28,1280]{1,0:T(8,128)}, u32[]{:S(2)}) copy-start(f32[28,1280]{1,0:T(8,128)} %param.44) | copy-start | bytes 430084
  602.3 10.4 %copy-start.19 = (f32[28,1280]{1,0:T(8,128)S(1)}, f32[28,1280]{1,0:T(8,128)}, u32[]{:S(2)}) copy-start(f32[28,1280]{1,0:T(8,128)} %param.45) | copy-start | bytes 430084
  602.3 10.4 %copy-start.20 = (f32[28,1280]{1,0:T(8,128)S(1)}, f32[28,1280]{1,0:T(8,128)}, u32[]{:S(2)}) copy-start(f32[28,1280]{1,0:T(8,128)} %param.46) | copy-start | bytes 430084
  602.3 11.3 %copy-start.5 = (f32[40,1792]{1,0:T(8,128)S(1)}, f32[40,1792]{1,0:T(8,128)}, u32[]{:S(2)}) copy-start(f32[40,1792]{1,0:T(8,128)} %get-tuple-element.87.refs_3_) | copy-start | bytes 860164
  602.3 11.3 %copy-start.7 = (f32[40,1792]{1,0:T(8,128)S(1)}, f32[40,1792]{1,0:T(8,128)}, u32[]{:S(2)}) copy-start(f32[40,1792]{1,0:T(8,128)} %param.41) | copy-start | bytes 860164
  602.3 11.3 %copy-start.15 = (f32[40,1792]{1,0:T(8,128)S(1)}, f32[40,1792]{1,0:T(8,128)}, u32[]{:S(2)}) copy-start(f32[40,1792]{1,0:T(8,128)} %param.42) | copy-start | bytes 860164
  602.3 11.3 %copy-start.16 = (f32[40,1792]{1,0:T(8,128)S(1)}, f32[40,1792]{1,0:T(8,128)}, u32[]{:S(2)}) copy-start(f32[40,1792]{1,0:T(8,128)} %param.43) | copy-start | bytes 860164
  612.6 2.1 copy-start.9
  612.6 2.1 copy-start.17
  612.6 2.1 copy-start.18
  612.6 3.1 copy-start.2
  612.6 3.1 copy-start.13
  612.6 3.0 copy-start.14
  614.7 2.7 copy-start.3
  614.7 2.7 copy-start.4

commit v3 on v2

--- a/solution.py
+++ b/solution.py
@@ -157,7 +157,17 @@
     return blocks
 
 
-def gather_events(place, order, pairs, send_sems, recv_sems):
+def by_core(place, order):
+    if isinstance(order, str):
+        return [(order, None)]
+    return [(order[core], place.core == core) for core in range(2)]
+
+
+def longest(groups):
+    return max((order if isinstance(order, str) else order[0] for order, _ in groups), key=len)
+
+
+def gather_events(place, order, only, pairs, send_sems, recv_sems):
     dims = place.dims(order)
     whole = len(dims) > 2
     here = {name: place.own(name) for name, _ in dims}
@@ -199,7 +209,7 @@
     steps = []
     times = arrival_times(dims)
     for block in relative_blocks(dims):
-        at, valid = dict(here), None
+        at, valid = dict(here), only
         for (name, _), shift in zip(dims, block):
             at[name], on = place.moved(name, shift)
             valid = both(valid, on)
@@ -294,7 +304,7 @@
     count = sum(n for _, n in groups)
     blocks, gathered, scratch = refs[:count], refs[count : 2 * count], refs[2 * count :]
     place = Place(ep_count, tp_count)
-    greet(place, max((order for order, _ in groups), key=len))
+    greet(place, longest(groups))
     steps, ends, first = [], [], 0
     local, swaps = [], []
     for order, n in groups:
@@ -307,12 +317,17 @@
         send_sems, recv_sems, own_sems = scratch[:3]
         scratch = scratch[3:]
         pairs = list(zip(mine_in, mine_out))
-        more, finish, _ = gather_events(place, order, pairs, send_sems, recv_sems)
+        more, finish = [], []
+        for lines, only in by_core(place, order):
+            found = gather_events(place, lines, only, pairs, send_sems, recv_sems)
+            more += found[0]
+            finish += found[1]
+        lines = by_core(place, order)[0][0]
         size = sum(block.shape[0] * block.shape[1] * (4 if block.dtype == jnp.float32 else 2) for block in mine_in)
         steps += [(key * size, len(steps) + i, step) for i, (key, step) in enumerate(more)]
         ends += finish
-        here = {name: place.own(name) for name, _ in place.dims(order)}
-        mine = place.index(here, place.core, len(order) > 2)
+        here = {name: place.own(name) for name, _ in place.dims(lines)}
+        mine = place.index(here, place.core, len(lines) > 2)
         for k, (block, out) in enumerate(pairs):
             local.append(pltpu.make_async_copy(block, out.at[mine], own_sems.at[k]))
     steps.sort(key=lambda entry: entry[:2])
@@ -333,14 +348,15 @@
     arrays, shapes, scratch = [], [], []
     place = Place(ep_count, tp_count)
     for order, blocks in groups:
-        total = ep_count * tp_count if len(order) > 2 else ep_count if order != "t" else tp_count - 1
+        lines = [line for line, _ in by_core(place, order)]
+        total = ep_count * tp_count if len(lines[0]) > 2 else ep_count if order != "t" else tp_count - 1
         for block in blocks:
             arrays.append(block)
             shapes.append(jax.ShapeDtypeStruct((total,) + block.shape, block.dtype))
         if order == "t":
             scratch += [pltpu.SemaphoreType.DMA((len(blocks), total))] * 2
             continue
-        sends = count_gather_sends(place.dims(order))
+        sends = max(count_gather_sends(place.dims(line)) for line in lines)
         scratch += [
             pltpu.SemaphoreType.DMA((len(blocks), sends)),
             pltpu.SemaphoreType.DMA((len(blocks), total)),
@@ -455,7 +471,12 @@
     return jnp.sum(total)
 
 
-def scatter_events(place, order, partials, outs, refs):
+def scatter_order(dims):
+    blocks = sorted(relative_blocks(dims), key=lambda block: -sum(abs(s) for s in block))
+    return sorted(blocks, key=lambda block: -max([k for k, s in enumerate(block) if s], default=-1))
+
+
+def scatter_events(place, order, only, partials, outs, refs):
     count = len(partials)
     dims = place.dims(order)
     whole = len(dims) > 2
@@ -465,12 +486,11 @@
     sems = refs[(2 + len(dims)) * count :]
     own_sem, sib_send, sib_recv, line_send = sems[:4]
     line_recv = sems[4:]
-    blocks = sorted(relative_blocks(dims), key=lambda block: -sum(abs(s) for s in block))
-    blocks = sorted(blocks, key=lambda block: -max([k for k, s in enumerate(block) if s], default=-1))
+    blocks = scatter_order(dims)
     info = {}
     starts, steps, ends = [], [], []
     for block in blocks:
-        at, valid = dict(here), None
+        at, valid = dict(here), only
         for (name, _), shift in zip(dims, block):
             at[name], on = place.moved(name, shift)
             valid = both(valid, on)
@@ -598,19 +618,32 @@
 
 
 def scatter_sizes(place, order):
-    dims = place.dims(order)
-    slots, lands = 1, []
-    for name, spread in dims:
-        lands.append(len(landings(spread)) * slots)
-        slots *= place.extent(name)
-    return slots, lands, sum(1 for block in relative_blocks(dims) if any(block))
+    found = []
+    for line, _ in by_core(place, order):
+        dims = place.dims(line)
+        slots, lands = 1, []
+        for name, spread in dims:
+            lands.append(len(landings(spread)) * slots)
+            slots *= place.extent(name)
+        found.append((slots, lands, sum(1 for block in relative_blocks(dims) if any(block))))
+    lands = [max(wide) for wide in zip(*[entry[1] for entry in found])]
+    return found[0][0], lands, max(entry[2] for entry in found)
+
+
+def scatter_scratch(place, order, partials):
+    slots, lands, sends = scatter_sizes(place, order)
+    count, dma = len(partials), pltpu.SemaphoreType.DMA
+    scratch = []
+    for wide in [slots, slots] + lands:
+        scratch += [pltpu.VMEM((wide,) + p.shape[1:], p.dtype) for p in partials]
+    return scratch + [dma((count, slots))] * 3 + [dma((count, sends))] + [dma((count, wide)) for wide in lands]
 
 
 def scatter_kernel(ep_count, tp_count, groups, *refs):
     count = sum(n for _, n in groups)
     partials, outs, refs = refs[:count], refs[count : 2 * count], refs[2 * count :]
     place = Place(ep_count, tp_count)
-    greet(place, max((order for order, _ in groups), key=len))
+    greet(place, longest(groups))
     starts, steps, ends, swaps, first = [], [], [], [], 0
     for order, n in groups:
         mine_in, mine_out = partials[first : first + n], outs[first : first + n]
@@ -619,12 +652,14 @@
             swaps += exchange_copies(place, mine_in, mine_out, refs[0], refs[1])
             refs = refs[2:]
             continue
-        used = n * (2 + len(order)) + 4 + len(order)
-        more, done, finish = scatter_events(place, order, mine_in, mine_out, refs[:used])
+        lines = by_core(place, order)
+        used = n * (2 + len(lines[0][0])) + 4 + len(lines[0][0])
+        for line, only in lines:
+            more, done, finish = scatter_events(place, line, only, mine_in, mine_out, refs[:used])
+            starts += [(i / len(more), len(starts) + i, entry) for i, entry in enumerate(more)]
+            steps += [(i / len(done), len(steps) + i, todo) for i, todo in enumerate(done)]
+            ends += finish
         refs = refs[used:]
-        starts += [(i / len(more), len(starts) + i, entry) for i, entry in enumerate(more)]
-        steps += [(i / len(done), len(steps) + i, todo) for i, todo in enumerate(done)]
-        ends += finish
     for copy in swaps:
         copy.start()
     for _, _, (on, start) in sorted(starts, key=lambda entry: entry[:2]):
@@ -656,13 +691,9 @@
             specs += [pl.BlockSpec(memory_space=pl.ANY)] * count
             scratch += [dma((count, tp_count - 1))] * 2
             continue
-        slots, lands, sends = scatter_sizes(place, order)
-        blocks = [(p.shape[1:], p.dtype) for p in partials]
-        shapes += [jax.ShapeDtypeStruct(shape, jnp.float32) for shape, _ in blocks]
+        shapes += [jax.ShapeDtypeStruct(p.shape[1:], jnp.float32) for p in partials]
         specs += [pl.BlockSpec(memory_space=pltpu.VMEM)] * count
-        for wide in [slots, slots] + lands:
-            scratch += [pltpu.VMEM((wide,) + shape, dtype) for shape, dtype in blocks]
-        scratch += [dma((count, slots))] * 3 + [dma((count, sends))] + [dma((count, wide)) for wide in lands]
+        scratch += scatter_scratch(place, order, partials)
     return pl.pallas_call(
         functools.partial(
             scatter_kernel, ep_count, tp_count, tuple((order, len(partials)) for order, partials in groups)
@@ -678,16 +709,18 @@
     )(*arrays)
 
 
+def scatter_room(place, order, partials):
+    slots, lands, _ = scatter_sizes(place, order)
+    rows = [(p.shape[1] + 15) // 16 * 16 for p in partials]
+    sizes = [r * p.shape[2] * p.dtype.itemsize for r, p in zip(rows, partials)]
+    return (2 * slots + sum(lands)) * sum(sizes)
+
+
 def scatter_all(ep_count, tp_count, collective_ids, name, groups):
     place = Place(ep_count, tp_count)
     calls, room = [[]], 0
     for order, partials in groups:
-        need = 0
-        if order != "t":
-            slots, lands, _ = scatter_sizes(place, order)
-            for p in partials:
-                rows = (p.shape[1] + 15) // 16 * 16
-                need += (2 * slots + sum(lands)) * rows * p.shape[2] * p.dtype.itemsize
+        need = 0 if order == "t" else scatter_room(place, order, partials)
         if calls[-1] and room + need > VMEM_MOST * 19 // 20:
             calls.append([])
             room = 0
@@ -819,15 +852,41 @@
     return jnp.where((unit == source) & (within < group), 1.0, 0.0).astype(jnp.bfloat16)
 
 
-def backward_kernel(group, step, tokens, cot, seg_row, seg_column, gains, cosine, sine, qkv_act, attended,
-                    hidden, normed_two, routed_grad, wq, wk, wv, wo, shin, shout,
-                    base, tokens_grad, gain_grads, qkv_grad, out_grad, shin_grad, shout_grad,
-                    normed, normed_turned, branch, grad_hidden, grad_one, pieces, stage, stage_sem):
+def backward_kernel(group, step, carried, *refs):
+    (tokens, cot, seg_row, seg_column, gains, cosine, sine, qkv_act, attended, hidden, normed_two,
+     routed_grad, wq, wk, wv, wo, shin, shout) = refs[:18]
+    refs = refs[18:]
+    if carried:
+        ep_count, tp_count, order = carried
+        result_part, sent_grads, refs = refs[0], refs[1], refs[2:]
+    base, tokens_grad, gain_grads, qkv_grad, out_grad, shin_grad, shout_grad = refs[:7]
+    refs = refs[7:]
+    if carried:
+        routed, grads_back, refs = refs[0], refs[1], refs[2:]
+    (normed, normed_turned, branch, grad_one, pieces, stage, stage_sem) = refs[:7]
+    refs = refs[7:]
     at = pl.program_id(0)
     width = tokens.shape[1]
     wide = 2 * HDIM
     low = jnp.bfloat16
     units = shin.shape[1] // 2
+
+    if carried:
+        place = Place(ep_count, tp_count)
+        starts, lines, ends = scatter_events(place, order, None, [result_part], [routed], refs[:-2])
+        swaps = exchange_copies(place, [sent_grads], [grads_back], refs[-2], refs[-1])
+        first = sum(1 for block in scatter_order(place.dims(order)) if block[-1])
+        turns = {0: lines[:first], 2: lines[first : first + 2], 4: lines[first + 2 : first + 4]}
+        turns[5] = lines[first + 4 :]
+
+    def run(entries):
+        for on, act in entries:
+            guarded(on, act)
+
+    def carry(turn):
+        if carried:
+            for todo in turns.get(turn, []):
+                run(todo)
 
     def stage_copy(part, pair):
         return pltpu.make_async_copy(
@@ -838,6 +897,11 @@
 
     @pl.when(at == 0)
     def _():
+        if carried:
+            greet(place, "tab")
+            for copy in swaps:
+                copy.start()
+            run(starts)
         unit_one = unit_of(tokens[...].astype(jnp.float32))[0]
         first = unit_one * gains[0:1, :]
         normed[...] = first.astype(low)
@@ -850,6 +914,7 @@
         act_spread = mul(act, spread).astype(low)
         base[...] = hidden[...] + mul(act_spread, shout[...])
         shout_grad[...] = mul(act_spread, cot[...], OVER_FIRST).astype(low)
+        carry(0)
         shout_tight = mul(spread, shout[...]).astype(low)
         grad_act = mul(cot[...], shout_tight, OVER_LAST)
         grad_up = (grad_act * pre_gate * sigmoid).astype(low)
@@ -868,8 +933,8 @@
         back = factor_two * (
             grad_unit - unit_two * jnp.mean(grad_unit * unit_two, axis=-1, keepdims=True)
         )
-        grad_hidden[...] = cot[...].astype(jnp.float32) + back
-        branch[...] = grad_hidden[...].astype(low)
+        tokens_grad[...] = cot[...].astype(jnp.float32) + back
+        branch[...] = tokens_grad[...].astype(low)
         grad_one[...] = jnp.zeros_like(grad_one)
 
     @pl.when(at > 0)
@@ -909,6 +974,9 @@
             stage_copy(part, pair).start()
             grad_one[...] += mul(pieces[part], weight[...], OVER_LAST)
 
+        for turn in (2, 4):
+            pl.when(at == turn)(functools.partial(carry, turn))
+
         @pl.when(at == pl.num_programs(0) - 1)
         def _():
             unit_one, factor_one = unit_of(tokens[...].astype(jnp.float32))
@@ -918,13 +986,19 @@
             back = factor_one * (
                 grad_unit - unit_one * jnp.mean(grad_unit * unit_one, axis=-1, keepdims=True)
             )
-            tokens_grad[...] = grad_hidden[...] + back
+            tokens_grad[...] += back
             for part in range(3):
                 stage_copy(part, pair).wait()
+            carry(5)
+            if carried:
+                run(ends)
+                for copy in swaps:
+                    copy.wait()
 
 
 def dense_backward(group, step, tokens, cot, segments, gains, qkv_act, attended, hidden, normed_two,
-                   routed_grad, qkv_low, out_low, shin_low, shout_spread):
+                   routed_grad, qkv_low, out_low, shin_low, shout_spread, ep_count, tp_count,
+                   collective_id, order, result_part, sent_grads):
     length, width = tokens.shape
     wide, pairs = 2 * HDIM, HEADS // 2
     cosine, sine = rope_rows(length)
@@ -936,48 +1010,64 @@
     def whole(*shape):
         return pl.BlockSpec(shape, lambda i: (0,) * len(shape), pipeline_mode=once)
 
-    def kept(*shape):
-        return pl.BlockSpec(shape, lambda i: (0,) * len(shape))
-
     def columns(part):
         return pl.BlockSpec((width, wide), lambda i: (0, part * pairs + jnp.maximum(i - 1, 0)))
 
     rows = pl.BlockSpec((wide, width), lambda i: (jnp.maximum(i - 1, 0), 0))
+    in_specs = [
+        whole(length, width), whole(length, width), whole(8, length), whole(length, 128),
+        whole(8, width), whole(length, HDIM), whole(length, HDIM), whole(length, 3 * width),
+        whole(length, width), whole(length, width), whole(length, width), whole(length, width),
+        columns(0), columns(1), columns(2), rows,
+        whole(*shin_low.shape), whole(*shout_spread.shape),
+    ]
+    anywhere = pl.BlockSpec(memory_space=pl.ANY)
+    out_specs = [
+        whole(length, width), whole(length, width), whole(8, width),
+        anywhere, rows, whole(*shin_low.shape), whole(*shout_spread.shape),
+    ]
+    out_shape = [
+        jax.ShapeDtypeStruct((length, width), jnp.float32),
+        jax.ShapeDtypeStruct((length, width), jnp.float32),
+        jax.ShapeDtypeStruct((8, width), jnp.float32),
+        jax.ShapeDtypeStruct((width, 3 * width), low),
+        jax.ShapeDtypeStruct((width, width), low),
+        jax.ShapeDtypeStruct(shin_low.shape, low),
+        jax.ShapeDtypeStruct(shout_spread.shape, low),
+    ]
+    scratch = [
+        pltpu.VMEM((length, width), low), pltpu.VMEM((width, length), low),
+        pltpu.VMEM((length, width), low), pltpu.VMEM((length, width), jnp.float32),
+        pltpu.VMEM((3, length, wide), low),
+        pltpu.VMEM((3, width, wide), low), pltpu.SemaphoreType.DMA((3,)),
+    ]
+    arguments = [tokens, cot, seg_row, seg_column, gains, jnp.asarray(cosine), jnp.asarray(sine), qkv_act,
+                 attended, hidden, normed_two, routed_grad, qkv_low, qkv_low, qkv_low, out_low, shin_low,
+                 shout_spread]
+    carried, more = None, {}
+    if result_part is not None:
+        carried, more = (ep_count, tp_count, order), dict(collective_id=collective_id, has_side_effects=True)
+        arguments += [result_part, sent_grads]
+        in_specs += [anywhere, anywhere]
+        out_specs += [whole(length, width), anywhere]
+        out_shape += [
+            jax.ShapeDtypeStruct((length, width), jnp.float32),
+            jax.ShapeDtypeStruct(sent_grads.shape, sent_grads.dtype),
+        ]
+        scratch += scatter_scratch(Place(ep_count, tp_count), order, [result_part])
+        scratch += [pltpu.SemaphoreType.DMA((1, tp_count - 1))] * 2
     return pl.pallas_call(
-        functools.partial(backward_kernel, group, step),
+        functools.partial(backward_kernel, group, step, carried),
         grid=(pairs + 1,),
-        in_specs=[
-            whole(length, width), whole(length, width), whole(8, length), whole(length, 128),
-            whole(8, width), whole(length, HDIM), whole(length, HDIM), whole(length, 3 * width),
-            whole(length, width), whole(length, width), whole(length, width), whole(length, width),
-            columns(0), columns(1), columns(2), rows,
-            whole(*shin_low.shape), whole(*shout_spread.shape),
-        ],
-        out_specs=[
-            kept(length, width), kept(length, width), kept(8, width),
-            pl.BlockSpec(memory_space=pl.ANY), rows, kept(*shin_low.shape), kept(*shout_spread.shape),
-        ],
-        out_shape=[
-            jax.ShapeDtypeStruct((length, width), jnp.float32),
-            jax.ShapeDtypeStruct((length, width), jnp.float32),
-            jax.ShapeDtypeStruct((8, width), jnp.float32),
-            jax.ShapeDtypeStruct((width, 3 * width), low),
-            jax.ShapeDtypeStruct((width, width), low),
-            jax.ShapeDtypeStruct(shin_low.shape, low),
-            jax.ShapeDtypeStruct(shout_spread.shape, low),
-        ],
-        scratch_shapes=[
-            pltpu.VMEM((length, width), low), pltpu.VMEM((width, length), low),
-            pltpu.VMEM((length, width), low), pltpu.VMEM((length, width), jnp.float32),
-            pltpu.VMEM((length, width), jnp.float32), pltpu.VMEM((3, length, wide), low),
-            pltpu.VMEM((3, width, wide), low), pltpu.SemaphoreType.DMA((3,)),
-        ],
+        in_specs=in_specs,
+        out_specs=out_specs,
+        out_shape=out_shape,
+        scratch_shapes=scratch,
         compiler_params=pltpu.CompilerParams(
-            dimension_semantics=("arbitrary",), vmem_limit_bytes=VMEM_MOST
+            dimension_semantics=("arbitrary",), vmem_limit_bytes=VMEM_MOST, **more
         ),
         name="dense_backward",
-    )(tokens, cot, seg_row, seg_column, gains, jnp.asarray(cosine), jnp.asarray(sine), qkv_act, attended,
-      hidden, normed_two, routed_grad, qkv_low, qkv_low, qkv_low, out_low, shin_low, shout_spread)
+    )(*arguments)
 
 
 def expert_kernel(parts, per_step, cap, *refs):
@@ -1519,10 +1609,10 @@
         1,
         "gather_weights",
         [
-            ("auv", [qkv_weight.astype(low), out_weight.astype(low), gain_columns]),
-            ("ab", [cotangent]),
+            (("tab", "abt"), [qkv_weight.astype(low), out_weight.astype(low), gain_columns]),
+            (("ab", "ba"), [cotangent]),
             ("t", [in_own, out_own]),
-            ("tba", [shared_in.astype(low), shout_own]),
+            (("tab", "atb"), [shared_in.astype(low), shout_own]),
         ],
     )
     qkv_low = qkv_low.reshape(width, 3 * width)
@@ -1563,29 +1653,30 @@
             normed_all, cot_all, info, ins_low, outs_low, capacity
         )
         (routed_grad,) = scatter_add(ep_count, tp_count, 3, "scatter_inputs", [("ab", [input_part])])
-    base, tokens_grad, gain_grads, qkv_grad, out_grad, shin_grad, shout_grad = dense_backward(
+    sent = jnp.stack(sent_grads)
+    lean = scatter_room(Place(ep_count, tp_count), "ab", [result_part]) <= VMEM_MOST // 3
+    base, tokens_grad, gain_grads, qkv_grad, out_grad, shin_grad, shout_grad, *carried = dense_backward(
         group, step, tokens, cotangent, segments, gains, qkv_act, attended, hidden, normed_two,
-        routed_grad, qkv_low, out_low, shin_low, shout_low,
+        routed_grad, qkv_low, out_low, shin_low, shout_low, ep_count, tp_count, 9, "ab",
+        result_part if lean else None, sent,
     )
     gain_rows = jnp.pad(gain_grads[:2].T.astype(low), ((0, 0), (0, 126)))
 
     def by_owner(grad):
         return grad.reshape(devices, -1, grad.shape[1])
 
-    qkv_part, out_part, gains_part, shin_part, shout_part, routed, *others = scatter_all(
-        ep_count,
-        tp_count,
-        (4, 6, 7, 8),
-        "scatter_weights",
-        [
-            ("auv", [by_owner(qkv_grad), by_owner(out_grad), by_owner(gain_rows)]),
-            ("tba", [by_owner(shin_grad), by_owner(shout_grad)]),
-            ("ab", [result_part]),
-            ("t", [jnp.stack(sent_grads)]),
-        ],
+    scattered = [
+        (("abt", "tab"), [by_owner(qkv_grad), by_owner(out_grad), by_owner(gain_rows)]),
+        (("abt", "bta"), [by_owner(shin_grad), by_owner(shout_grad)]),
+    ]
+    if not lean:
+        scattered += [("ab", [result_part]), ("t", [sent])]
+    qkv_part, out_part, gains_part, shin_part, shout_part, *more = scatter_all(
+        ep_count, tp_count, (4, 6, 7, 8), "scatter_weights", scattered
     )
+    routed, others = carried or more
     for shift in range(tp_count - 1):
-        own_grad = own_grad + others[0][shift].astype(jnp.float32)
+        own_grad = own_grad + others[shift].astype(jnp.float32)
     block_out = (base + routed).astype(low)
     exin_part, exout_part = own_grad[None, :2], own_grad[2:]
     extra = jnp.sum(own_grad * own_grad, axis=(0, 1))[None, :]

time: 624 us -> 581 us (0.931)
  Pallas kernels: 561 us -> 518 us
    pallas_call x1, Pallas kernels: 166 us -> 94.8 us  [scatter_add(): pl.pallas_call(functools.partial(scatter_kernel, ep_count, tp_count, tupl...]
    pallas_call x1, Pallas kernels: 38.6 us -> 89.3 us  [dense_backward(): pl.pallas_call(functools.partial(backward_kernel, group, step, carried),...]
    pallas_call x1, Pallas kernels: 171 us -> 150 us  [gather(): pl.pallas_call(functools.partial(gather_kernel, ep_count, tp_count, tuple...]
where the time goes in v3:
time: 581 us; the launch traced here: 575 us
  Pallas kernels  518 us (89%)
  other arithmetic  41.3 us (7%)
  local copies, waits for them, and re-layouts  12.5 us (2%)
    pallas_call x1, Pallas kernels, fused_experts(): pl.pallas_call(functools.partial(fused_kernel, parts, ep_count, tp_count,...  159 us
    pallas_call x1, Pallas kernels, gather(): pl.pallas_call(functools.partial(gather_kernel, ep_count, tp_count, tuple...  150 us
    pallas_call x1, Pallas kernels, scatter_add(): pl.pallas_call(functools.partial(scatter_kernel, ep_count, tp_count, tupl...  94.8 us
    pallas_call x1, Pallas kernels, dense_backward(): pl.pallas_call(functools.partial(backward_kernel, group, step, carried),...  89.3 us
    convert_element_type x7, other arithmetic, adam_update(): return (weight_new, first_new, second_new, weight_new.astype(jnp.bfloat16))  22 us
    pallas_call x1, Pallas kernels, attention_forward(): pl.pallas_call(forward_kernel, grid=(pairs,), in_specs=[whole(length, wid...  14.4 us

profile of v3, /device:TPU:0, one launch (start us, length us, event | category | flops | bytes accessed | tf_op | source)
XLA Modules:
  0.0 574.8 jit_solution(17148445263157428984)
XLA Ops:
  0.7 4.1 convert_bitcast_fusion.refs_4_.refs_3_
  4.8 1.1 convert_bitcast_fusion.1.refs_5_
  5.9 0.8 convert_element_type.80.refs_0_
  6.7 0.6 pad.19.refs_7_
  7.3 0.7 convert_element_type.88.refs_6_
  8.0 0.7 convert_element_type.81.refs_1_
  9.4 150.0 %gather_weights.1 = (bf16[32,40,3840]{2,1,0:T(8,128)(2,1)}, bf16[32,40,1280]{2,1,0:T(8,128)(2,1)}, bf16[32,40,128]{2,1,0:T(8,128)(2,1)}, bf16[16,256,1280]{2,1,0...) custom-call(bf16[40,3840]{1,0:T(8,128)(2,1)} %convert_element_type.8, ...), custom_call_target="tpu_custom_call" | custom-call | tf_op jit(solution)/shard_map/gather_weights/pallas_call | solution.py:365
  159.3 1.1 copy.129
  160.5 0.6 pad_convert_fusion.gains.refs_4_
  161.1 0.8 broadcast_in_dim.50.seg_column.refs_3_
  162.5 14.4 %attention_forward.1 = (bf16[256,3840]{1,0:T(8,128)(2,1)}, bf16[256,1280]{1,0:T(8,128)(2,1)}, f32[256,1280]{1,0:T(8,128)}, bf16[256,1280]{1,0:T(8,128)(2,1)}) custom-call(bf16[256,1280]{1,0:T(8,128)(2,1)} %refs_0_.1, s32[8,256]{1,0:T(8,128)} %broadcast_in_dim.49.seg_row.refs_2_, s32[256,128]{1,0:T(8,128)} %broadcast_in_dim.50.seg_column.refs_3_, ...), custom_call_target="tpu_custom_call" | custom-call | tf_op jit(solution)/shard_map/attention_forward/pallas_call | solution.py:824
  177.1 0.6 maximum_bitcast_fusion.refs_1_
  177.8 158.9 %fused_experts.1 = (bf16[16,256,1280]{2,1,0:T(8,128)(2,1)}, f32[256,1280]{1,0:T(8,128)}, f32[3,448,1280]{2,1,0:T(8,128)}, bf16[3,448,1280]{2,1,0:T(8,128)(2,1)}) custom-call(bf16[256,1280]{1,0:T(8,128)(2,1)} %get-tuple-element.67.refs_0_.refs_10_, f32[32,256]{1,0:T(8,128)} %maximum_bitcast_fusion.refs_1_, bf16[16,256,1280]{2,1,0:T(8,128)(2,1)} %get-tuple-element.68.refs_2_, ...), custom_call_target="tpu_custom_call" | custom-call | tf_op jit(solution)/shard_map/fused_experts/pallas_call | solution.py:1539
  336.7 89.3 %dense_backward.1 = (f32[256,1280]{1,0:T(8,128)}, f32[256,1280]{1,0:T(8,128)}, f32[8,1280]{1,0:T(8,128)}, bf16[1280,3840]{1,0:T(8,128)(2,1)}, bf16[1280,1280]{1,...) custom-call(bf16[256,1280]{1,0:T(8,128)(2,1)} %refs_0_.1, ...), custom_call_target="tpu_custom_call" | custom-call | tf_op jit(solution)/shard_map/dense_backward/pallas_call | solution.py:1059
  426.0 7.7 %multiply_reduce_fusion = (f32[1280]{0:T(1024)S(1)}, f32[3,448,1280]{2,1,0:T(8,128)}) fusion(f32[3,448,1280]{2,1,0:T(8,128)} %get-tuple-element.89, bf16[1,3,448,1280]{3,2,1,0:T(8,128)(2,1)} %get-tuple-element.90), kind=kLoop, calls=%fused_computation.2 | loop fusion | flops 6880000 | bytes 17208320 | tf_op jit(solution)/shard_map/reduce_sum | solution.py:1682
  434.3 0.8 fusion.15
  435.4 0.8 pad.22.clone
  436.2 94.8 %scatter_weights_0.1 = (f32[40,3840]{1,0:T(8,128)}, f32[40,1280]{1,0:T(8,128)}, f32[40,128]{1,0:T(8,128)}, f32[40,1792]{1,0:T(8,128)}, f32[32,1280]{1,0:T(8,128)}) custom-call(bf16[32,40,3840]{2,1,0:T(8,128)(2,1)} %bitcast.56, bf16[32,40,1280]{2,1,0:T(8,128)(2,1)} %bitcast.60, bf16[32,40,128]{2,1,0:T(8,128)(2,1)} %bitcast.64, ...), custom_call_target="tpu_custom_call" | custom-call | tf_op jit(solution)/shard_map/scatter_weights_0/pallas_call | solution.py:697
  531.0 10.3 %sum_of_squares.1 = f32[8,128]{1,0:T(8,128)} custom-call(f32[40,3840]{1,0:T(8,128)} %get-tuple-element.84.refs_0_, f32[40,1280]{1,0:T(8,128)} %get-tuple-element.85.refs_1_, f32[40,128]{1,0:T(8,128)} %get-tuple-element.86.refs_2_, f32[40,1792]{1,0:T(8,128)} %get-tuple-element.87.refs_3_, f32[32,1280]{1,0:T(8,128)} %get-tuple-element.88.refs_4_, ...), custom_call_target="tpu_custom_call" | custom-call | tf_op jit(solution)/shard_map/sum_of_squares/pallas_call | solution.py:457
  541.3 1.3 reduce_sum.39
  543.6 0.7 sqrt_add_fusion
  544.7 0.6 copy.125
  547.2 8.0 %fusion.21 = (bf16[1,448,1280]{2,1,0:T(8,128)(2,1)}, f32[1,448,1280]{2,1,0:T(8,128)}, f32[1,448,1280]{2,1,0:T(8,128)}, f32[1,448,1280]{2,1,0:T(8,128)}) fusion(f32[1,448,1280]{2,1,0:T(8,128)S(1)} %copy-done, f32[]{:T(128)S(6)} %min.3, f32[3,448,1280]{2,1,0:T(8,128)} %get-tuple-element.248, f32[1,448,1280]{2,1,0:T(8,128)} %param.51, f32[1,448,1280]{2,1,0:T(8,128)} %param.52), kind=kLoop, calls=%fused_computation.61 | loop fusion | flops 9748480 | bytes 17203204 | tf_op jit(solution)/shard_map/convert_element_type | solution.py:1561
  555.2 1.1 slice-done.1
  556.4 9.4 %fusion.23 = (bf16[1,2,448,1280]{3,2,1,0:T(8,128)(2,1)}, f32[1,2,448,1280]{3,2,1,0:T(8,128)}, f32[1,2,448,1280]{3,2,1,0:T(8,128)}, f32[1,2,448,1280]{3,2,1,0:T(8,128)}) fusion(f32[1,2,448,1280]{3,2,1,0:T(8,128)S(1)} %bitcast.53, f32[]{:T(128)S(6)} %min.3, f32[3,448,1280]{2,1,0:T(8,128)S(1)} %bitcast.51, f32[1,2,448,1280]{3,2,1,0:T(8,128)} %param.48, ...), kind=kLoop, calls=%fused_computation.62 | loop fusion | flops 19496960 | bytes 34406404 | tf_op jit(solution)/shard_map/convert_element_type | solution.py:1561
  565.9 0.9 fusion.25
  566.8 1.1 fusion.27
  567.9 0.9 fusion.29
  568.9 1.6 fusion.31
  570.6 0.8 copy-done.4
  571.4 1.0 add_convert_fusion
  572.4 1.1 copy.132
  (87 shorter events, 5.0 us)
Async XLA Ops:
  0.7 4.1 copy-start
  4.7 1.2 copy-start.1
  4.7 1.9 copy-start.12
  4.7 2.6 copy-start.7
  4.8 3.2 copy-start.8
  4.8 3.9 copy-start.25
  8.6 152.5 %copy-start.24 = (s32[1,256]{1,0:T(1,128)S(1)}, s32[1,256]{1,0:T(1,128)}, u32[]{:S(2)}) copy-start(s32[1,256]{1,0:T(1,128)} %param.32) | copy-start | bytes 3076
  162.5 14.4 %copy-start.22 = (s32[256,7]{0,1:T(8,128)S(1)}, s32[256,7]{0,1:T(8,128)}, u32[]{:S(2)}) copy-start(s32[256,7]{0,1:T(8,128)} %param.33) | copy-start | bytes 21508
  162.5 14.4 %copy-start.23 = (f32[256,7]{0,1:T(8,128)S(1)}, f32[256,7]{0,1:T(8,128)}, u32[]{:S(2)}) copy-start(f32[256,7]{0,1:T(8,128)} %param.34) | copy-start | bytes 21508
  436.2 107.2 %copy-start.26 = (f32[2,40]{1,0:T(2,128)S(1)}, f32[2,40]{1,0:T(2,128)}, u32[]{:S(2)}) copy-start(f32[2,40]{1,0:T(2,128)} %param.54) | copy-start | bytes 964
  436.2 107.3 %copy-start.27 = (f32[2,40]{1,0:T(2,128)S(1)}, f32[2,40]{1,0:T(2,128)}, u32[]{:S(2)}) copy-start(f32[2,40]{1,0:T(2,128)} %param.55) | copy-start | bytes 964
  547.2 8.0 %slice-start = ((s8[6881280]{0:T(1024)(128)(4,1)}), s8[4194304]{0:T(1024)(128)(4,1)S(1)}, s32[]{:S(2)}) async-start(s8[6881280]{0:T(1024)(128)(4,1)} %bitcast.50), calls=%async_computation | async-start | bytes 8388608
  547.2 8.0 %slice-start.2 = ((s8[4587520]{0:T(1024)(128)(4,1)}), s8[4194304]{0:T(1024)(128)(4,1)S(1)}, s32[]{:S(2)}) async-start(s8[4587520]{0:T(1024)(128)(4,1)} %bitcast.52), calls=%async_computation.2 | async-start | bytes 8388608
  547.2 9.1 %slice-start.1 = ((s8[6881280]{0:T(1024)(128)(4,1)}), s8[2686976]{0:T(1024)(128)(4,1)S(1)}, s32[]{:S(2)}) async-start(s8[6881280]{0:T(1024)(128)(4,1)} %bitcast.50), calls=%async_computation.1 | async-start | bytes 5373952
  547.2 9.1 %slice-start.3 = ((s8[4587520]{0:T(1024)(128)(4,1)}), s8[393216]{0:T(1024)(128)(4,1)S(1)}, s32[]{:S(2)}) async-start(s8[4587520]{0:T(1024)(128)(4,1)} %bitcast.52), calls=%async_computation.3 | async-start | bytes 786432
  556.3 9.5 %copy-start.11 = (f32[32,1280]{1,0:T(8,128)S(1)}, f32[32,1280]{1,0:T(8,128)}, u32[]{:S(2)}) copy-start(f32[32,1280]{1,0:T(8,128)} %get-tuple-element.88.refs_4_) | copy-start | bytes 491524
  556.3 9.5 %copy-start.13 = (f32[28,1280]{1,0:T(8,128)S(1)}, f32[28,1280]{1,0:T(8,128)}, u32[]{:S(2)}) copy-start(f32[28,1280]{1,0:T(8,128)} %param.44) | copy-start | bytes 430084
  556.3 9.6 %copy-start.20 = (f32[28,1280]{1,0:T(8,128)S(1)}, f32[28,1280]{1,0:T(8,128)}, u32[]{:S(2)}) copy-start(f32[28,1280]{1,0:T(8,128)} %param.45) | copy-start | bytes 430084
  556.3 9.6 %copy-start.21 = (f32[28,1280]{1,0:T(8,128)S(1)}, f32[28,1280]{1,0:T(8,128)}, u32[]{:S(2)}) copy-start(f32[28,1280]{1,0:T(8,128)} %param.46) | copy-start | bytes 430084
  556.4 10.4 %copy-start.6 = (f32[40,1792]{1,0:T(8,128)S(1)}, f32[40,1792]{1,0:T(8,128)}, u32[]{:S(2)}) copy-start(f32[40,1792]{1,0:T(8,128)} %get-tuple-element.87.refs_3_) | copy-start | bytes 860164
  556.4 10.4 %copy-start.16 = (f32[40,1792]{1,0:T(8,128)S(1)}, f32[40,1792]{1,0:T(8,128)}, u32[]{:S(2)}) copy-start(f32[40,1792]{1,0:T(8,128)} %param.42) | copy-start | bytes 860164
  556.4 10.4 %copy-start.17 = (f32[40,1792]{1,0:T(8,128)S(1)}, f32[40,1792]{1,0:T(8,128)}, u32[]{:S(2)}) copy-start(f32[40,1792]{1,0:T(8,128)} %param.43) | copy-start | bytes 860164
  565.8 2.1 copy-start.9
  565.8 2.1 copy-start.10
  565.8 2.1 copy-start.18
  565.8 2.1 copy-start.19
  565.8 3.1 copy-start.2
  565.8 3.1 copy-start.14
  565.8 3.0 copy-start.15
  568.9 1.7 copy-start.3
  568.9 2.5 copy-start.4
  570.5 1.8 copy-start.5

commit v4 on v3

--- a/solution.py
+++ b/solution.py
@@ -301,13 +301,13 @@
 
 
 def gather_kernel(ep_count, tp_count, groups, *refs):
-    count = sum(n for _, n in groups)
+    count = sum(n for _, n, _ in groups)
     blocks, gathered, scratch = refs[:count], refs[count : 2 * count], refs[2 * count :]
     place = Place(ep_count, tp_count)
-    greet(place, longest(groups))
+    greet(place, longest([group[:2] for group in groups]))
     steps, ends, first = [], [], 0
     local, swaps = [], []
-    for order, n in groups:
+    for order, n, patience in groups:
         mine_in, mine_out = blocks[first : first + n], gathered[first : first + n]
         first += n
         if order == "t":
@@ -324,7 +324,7 @@
             finish += found[1]
         lines = by_core(place, order)[0][0]
         size = sum(block.shape[0] * block.shape[1] * (4 if block.dtype == jnp.float32 else 2) for block in mine_in)
-        steps += [(key * size, len(steps) + i, step) for i, (key, step) in enumerate(more)]
+        steps += [(key * size * patience, len(steps) + i, step) for i, (key, step) in enumerate(more)]
         ends += finish
         here = {name: place.own(name) for name, _ in place.dims(lines)}
         mine = place.index(here, place.core, len(lines) > 2)
@@ -347,7 +347,7 @@
 def gather(ep_count, tp_count, collective_id, name, groups):
     arrays, shapes, scratch = [], [], []
     place = Place(ep_count, tp_count)
-    for order, blocks in groups:
+    for order, blocks, _ in groups:
         lines = [line for line, _ in by_core(place, order)]
         total = ep_count * tp_count if len(lines[0]) > 2 else ep_count if order != "t" else tp_count - 1
         for block in blocks:
@@ -364,7 +364,10 @@
         ]
     return pl.pallas_call(
         functools.partial(
-            gather_kernel, ep_count, tp_count, tuple((order, len(blocks)) for order, blocks in groups)
+            gather_kernel,
+            ep_count,
+            tp_count,
+            tuple((order, len(blocks), patience) for order, blocks, patience in groups),
         ),
         out_shape=tuple(shapes),
         in_specs=[pl.BlockSpec(memory_space=pl.ANY)] * len(arrays),
@@ -639,11 +642,117 @@
     return scratch + [dma((count, slots))] * 3 + [dma((count, sends))] + [dma((count, wide)) for wide in lands]
 
 
-def scatter_kernel(ep_count, tp_count, groups, *refs):
+def greet_all(ep_count, tp_count):
+    devices = ep_count * tp_count
+    me = lax.axis_index("ep") * tp_count + lax.axis_index("tp")
+    barrier = pltpu.get_barrier_semaphore()
+
+    def signal(i, carry):
+        other = lax.rem(me + i, devices)
+        target = (other // tp_count, lax.rem(other, tp_count))
+        pl.semaphore_signal(barrier, inc=1, device_id=target, device_id_type=MESH)
+        return carry
+
+    lax.fori_loop(1, devices, signal, 0)
+    pl.semaphore_wait(barrier, devices - 1)
+
+
+def add_squares(total, ref):
+    def add(i, carry):
+        piece = ref[:, pl.ds(pl.multiple_of(i * 128, 128), 128)]
+        total[0:1, :] += jnp.sum(piece * piece, axis=0, keepdims=True)
+        return carry
+
+    lax.fori_loop(0, ref.shape[1] // 128, add, 0)
+
+
+def exchanged_pieces(own, others, summed, total, held, come, load_sems, save_sem):
+    pieces, parts = own.shape[0], others.shape[0]
+
+    def loads(q):
+        found = [pltpu.make_async_copy(own.at[q], held.at[q % 2], load_sems.at[q % 2, 0])]
+        for s in range(parts):
+            found.append(pltpu.make_async_copy(others.at[s, q], come.at[q % 2, s], load_sems.at[q % 2, s + 1]))
+        return found
+
+    def save(q):
+        return pltpu.make_async_copy(held.at[q % 2], summed.at[q], save_sem.at[q % 2])
+
+    def load(q):
+        if q >= 2:
+            save(q - 2).wait()
+        for copy in loads(q):
+            copy.start()
+
+    def piece(q):
+        for copy in loads(q):
+            copy.wait()
+        arrived = [come.at[q % 2, s] for s in range(parts)]
+        add_into(held.at[q % 2], [held.at[q % 2]] + arrived, jnp.float32)
+        add_squares(total, held.at[q % 2])
+        save(q).start()
+        if q + 2 < pieces:
+            load(q + 2)
+
+    def finish():
+        for q in range(max(0, pieces - 2), pieces):
+            save(q).wait()
+
+    for q in range(min(2, pieces)):
+        load(q)
+    return [functools.partial(piece, q) for q in range(pieces)] + [finish]
+
+
+def share_total(ep_count, tp_count, total, totals, send, recv, norm):
+    devices = ep_count * tp_count
+    me = lax.axis_index("ep") * tp_count + lax.axis_index("tp")
+
+    def share(i, carry):
+        other = lax.rem(me + i, devices)
+        pltpu.make_async_remote_copy(
+            src_ref=total,
+            dst_ref=totals.at[me],
+            send_sem=send.at[i],
+            recv_sem=recv.at[me],
+            device_id=(other // tp_count, lax.rem(other, tp_count)),
+            device_id_type=MESH,
+        ).start()
+        return carry
+
+    lax.fori_loop(1, devices, share, 0)
+    norm[...] = total[...]
+
+    def collect(i, carry):
+        other = lax.rem(me + i, devices)
+        pltpu.make_async_copy(totals.at[other], totals.at[other], recv.at[other]).wait()
+        norm[...] += totals[other]
+        return carry
+
+    lax.fori_loop(1, devices, collect, 0)
+    norm[...] = jnp.broadcast_to(jnp.sqrt(jnp.sum(norm[...], keepdims=True)), norm.shape)
+
+    def sent(i, carry):
+        pltpu.make_async_copy(total, total, send.at[i]).wait()
+        return carry
+
+    lax.fori_loop(1, devices, sent, 0)
+
+
+def scatter_kernel(ep_count, tp_count, groups, normed, *refs):
     count = sum(n for _, n in groups)
-    partials, outs, refs = refs[:count], refs[count : 2 * count], refs[2 * count :]
+    partials, refs = refs[:count], refs[count:]
+    if normed:
+        own, others, refs = refs[0], refs[1], refs[2:]
+    outs, refs = refs[:count], refs[count:]
+    if normed:
+        summed, norm, refs = refs[0], refs[1], refs[2:]
+        total, totals, held, come, load_sems, save_sem, send, recv = refs[:8]
+        refs = refs[8:]
     place = Place(ep_count, tp_count)
-    greet(place, longest(groups))
+    if normed:
+        greet_all(ep_count, tp_count)
+    else:
+        greet(place, longest(groups))
     starts, steps, ends, swaps, first = [], [], [], [], 0
     for order, n in groups:
         mine_in, mine_out = partials[first : first + n], outs[first : first + n]
@@ -664,9 +773,19 @@
         copy.start()
     for _, _, (on, start) in sorted(starts, key=lambda entry: entry[:2]):
         guarded(on, start)
-    for _, _, todo in sorted(steps, key=lambda entry: entry[:2]):
+    steps = [todo for _, _, todo in sorted(steps, key=lambda entry: entry[:2])]
+    if normed:
+        total[...] = jnp.zeros_like(total)
+        extras = exchanged_pieces(own, others, summed, total, held, come, load_sems, save_sem)
+        for i, act in enumerate(extras):
+            steps.insert((4 + i) * len(steps) // (5 + len(extras)), [(None, act)])
+    for todo in steps:
         for on, act in todo:
             guarded(on, act)
+    if normed:
+        for out in outs:
+            add_squares(total, out)
+        share_total(ep_count, tp_count, total, totals, send, recv, norm)
     for on, finish in ends:
         guarded(on, finish)
     for copy in swaps:
@@ -679,9 +798,10 @@
     return [(shift, way) for shift in spread for way in (-1, 1) if shift - way in spread and shift * way <= 0]
 
 
-def scatter_add(ep_count, tp_count, collective_id, name, groups):
+def scatter_add(ep_count, tp_count, collective_id, name, groups, grads=None):
     place = Place(ep_count, tp_count)
     arrays, shapes, scratch, specs = [], [], [], []
+    normed = grads is not None
     dma = pltpu.SemaphoreType.DMA
     for order, partials in groups:
         arrays += partials
@@ -694,9 +814,29 @@
         shapes += [jax.ShapeDtypeStruct(p.shape[1:], jnp.float32) for p in partials]
         specs += [pl.BlockSpec(memory_space=pltpu.VMEM)] * count
         scratch += scatter_scratch(place, order, partials)
+    if normed:
+        own, others = grads
+        arrays += [own, others]
+        devices, parts = ep_count * tp_count, others.shape[0]
+        shapes += [jax.ShapeDtypeStruct(own.shape, own.dtype), jax.ShapeDtypeStruct((8, 128), jnp.float32)]
+        specs += [pl.BlockSpec(memory_space=pl.ANY), pl.BlockSpec(memory_space=pltpu.VMEM)]
+        scratch = [
+            pltpu.VMEM((8, 128), jnp.float32),
+            pltpu.VMEM((devices, 8, 128), jnp.float32),
+            pltpu.VMEM((2,) + own.shape[1:], own.dtype),
+            pltpu.VMEM((2, parts) + own.shape[1:], others.dtype),
+            dma((2, parts + 1)),
+            dma((2,)),
+            dma((devices,)),
+            dma((devices,)),
+        ] + scratch
     return pl.pallas_call(
         functools.partial(
-            scatter_kernel, ep_count, tp_count, tuple((order, len(partials)) for order, partials in groups)
+            scatter_kernel,
+            ep_count,
+            tp_count,
+            tuple((order, len(partials)) for order, partials in groups),
+            normed,
         ),
         out_shape=tuple(shapes),
         in_specs=[pl.BlockSpec(memory_space=pl.ANY)] * len(arrays),
@@ -1193,6 +1333,113 @@
     return found[0], found[1], found[2], found[3:]
 
 
+def adam_rows(source, target, grad, clip, rate, decay):
+    weight, first, second = source
+    clipped = grad * clip
+    first_new = BETA_ONE * first + (1.0 - BETA_ONE) * clipped
+    second_new = BETA_TWO * second + (1.0 - BETA_TWO) * clipped * clipped
+    corr_one = 1.0 - BETA_ONE**STEP
+    corr_two = 1.0 - BETA_TWO**STEP
+    stepped = first_new * (1.0 / corr_one) / (jnp.sqrt(second_new * (1.0 / corr_two)) + ADAM_EPS)
+    weight_new = weight - rate * (stepped + decay * weight)
+    refs, window = target
+    for ref, value in zip(refs, (weight_new, first_new, second_new, weight_new)):
+        ref[window] = value.astype(ref.dtype)
+
+
+def adam_kernel(first_blocks, dense_blocks, *refs):
+    dense = len(dense_blocks)
+    norm, grads = refs[:2]
+    inside, outside = refs[2:5], refs[5:8]
+    refs = refs[8:]
+    dense_in, refs = refs[: 4 * dense], refs[4 * dense :]
+    inside_new, outside_new, dense_new = refs[:4], refs[4:8], refs[8:]
+    at = pl.program_id(0)
+    clip = jnp.minimum(1.0, CLIP_LEVEL / (norm[0:1, 0:1] + 1e-06))
+
+    def block(source, target):
+        def rows(i, carry):
+            window = (pl.ds(pl.multiple_of(i * 16, 16), 16), slice(None))
+            values = [ref[window] for ref in source]
+            adam_rows(values, (target, window), grads[window], clip, MATRIX_RATE, WEIGHT_DECAY)
+            return carry
+
+        lax.fori_loop(0, grads.shape[0] // 16, rows, 0)
+
+    pl.when(at < first_blocks)(lambda: block(inside, inside_new))
+    pl.when(at >= first_blocks)(lambda: block(outside, outside_new))
+
+    def one(k):
+        source, grad = dense_in[4 * k : 4 * k + 3], dense_in[4 * k + 3]
+        rows, width = source[0].shape
+        last = k == dense - 1
+        everything = (slice(None), slice(None))
+        adam_rows(
+            [ref[...] for ref in source],
+            (dense_new[4 * k : 4 * k + 4], everything),
+            grad[:rows, :width],
+            clip,
+            GAIN_RATE if last else MATRIX_RATE,
+            0.0 if last else WEIGHT_DECAY,
+        )
+
+    for k, count in enumerate(dense_blocks):
+        pl.when(at < count)(functools.partial(one, k))
+
+
+def adam_all(norm, grads, inside, outside, dense):
+    hidden, width = grads.shape[1:]
+    rows = hidden // 4 if hidden % 64 == 0 else hidden // 2
+    inner = 2 * hidden // rows
+    steps = 3 * hidden // rows
+
+    def blocks_of(columns):
+        return max(n for n in range(1, steps + 1) if columns % (128 * n) == 0 or n == 1)
+
+    counts = tuple(blocks_of(entry[0].shape[1]) for entry in dense)
+
+    def slab(array, count):
+        columns = array.shape[1] // count
+        return pl.BlockSpec((array.shape[0], columns), lambda i: (0, jnp.minimum(i, count - 1)))
+
+    first_spec = pl.BlockSpec((rows, width), lambda i: (jnp.minimum(i, inner - 1), 0))
+    second_spec = pl.BlockSpec((rows, width), lambda i: (jnp.maximum(i - inner, 0), 0))
+    flat = [a.reshape(2 * hidden, width) for a in inside] + [a.reshape(hidden, width) for a in outside]
+    low, full = jnp.bfloat16, jnp.float32
+    kinds = (full, full, full, low)
+    out_shape = [jax.ShapeDtypeStruct((2 * hidden, width), kind) for kind in kinds]
+    out_shape += [jax.ShapeDtypeStruct((hidden, width), kind) for kind in kinds]
+    out_specs = [first_spec] * 4 + [second_spec] * 4
+    in_specs = [pl.BlockSpec(norm.shape, lambda i: (0, 0)), pl.BlockSpec((rows, width), lambda i: (i, 0))]
+    in_specs += [first_spec] * 3 + [second_spec] * 3
+    more = []
+    for entry, count in zip(dense, counts):
+        more += entry
+        in_specs += [slab(array, count) for array in entry]
+        out_specs += [slab(entry[0], count)] * 4
+        out_shape += [jax.ShapeDtypeStruct(entry[0].shape, kind) for kind in kinds]
+    found = pl.pallas_call(
+        functools.partial(adam_kernel, inner, counts),
+        grid=(steps,),
+        in_specs=in_specs,
+        out_specs=out_specs,
+        out_shape=out_shape,
+        compiler_params=pltpu.CompilerParams(
+            dimension_semantics=("arbitrary",), vmem_limit_bytes=VMEM_MOST
+        ),
+        name="adam",
+    )(norm, grads.reshape(3 * hidden, width), *flat, *more)
+    first = [a.reshape(inside[0].shape) for a in found[:4]]
+    second = [a.reshape(outside[0].shape) for a in found[4:8]]
+    return first, second, [found[8 + 4 * k : 12 + 4 * k] for k in range(len(dense))]
+
+
+FROM_A = {1: (1, 0), 2: (2, 1), 3: (4, 1)}
+FROM_B = {0: (0, 2), 1: (2, 1), 2: (4, 1), 3: (6, 0)}
+TO_B = {1: (6, 1), 2: (5, 2), 3: (7, 2)}
+TO_A = {2: (6, 2)}
+
+
 def nearest(place):
     count = place.na
     table = [sorted(range(count), key=lambda other: abs(other - own)) for own in range(count)]
@@ -1283,8 +1530,8 @@
     start(loads)
 
     def chip_of(k):
-        side = lax.rem(k, 2)
-        return chip_at(k // 2) * 2 + jnp.where(side == 0, b, 1 - b)
+        near = (lax.rem(k, 2) == 0) == (k < 2 * na - 2)
+        return chip_at(k // 2) * 2 + jnp.where(near, b, 1 - b)
 
     def cot_copies(k):
         chip, buffer = chip_of(k), lax.rem(k, 2)
@@ -1377,6 +1624,17 @@
     def picks_of(source):
         return slots == infos[source, pl.ds(me, 1), :]
 
+    def turn(k, phase):
+        for r in range(1, na):
+            for far, spot in FROM_A.items():
+                if spot[1] == phase and (r + 1) // 2 <= far <= r:
+                    on = (k == spot[0]) & (jnp.abs(chip_at(r) - a) == far)
+                    pl.when(on)(functools.partial(from_a, r))
+        for act, spots in ((from_b, FROM_B), (to_b, TO_B), (to_a, TO_A)):
+            for r, spot in spots.items():
+                if spot[1] == phase:
+                    pl.when(k == spot[0])(functools.partial(act, r))
+
     def work(k, carry):
         chip, buffer = chip_of(k), lax.rem(k, 2)
 
@@ -1384,11 +1642,7 @@
         def _():
             start(cot_copies(k + 1))
 
-        for r in range(na):
-            if r == 1:
-                pl.when(k == 1)(functools.partial(from_a, r))
-            pl.when(k == 2 * r + 1)(functools.partial(from_b, r))
-        pl.when(k == 2 * na - 2)(functools.partial(to_b, 1))
+        turn(k, 0)
         arrived(chip * 2 + 1 - core)
         for copy in cot_copies(k):
             copy.wait()
@@ -1428,10 +1682,7 @@
                 sums[p][1, :, window] += mul(grad_up, rows_x[:, window], over_first)
                 sums[p][2, :, window] += mul(active, rows_g[:, window], over_first)
             if p == 0:
-                for r in range(2, na):
-                    pl.when(k == 2 * r - 2)(functools.partial(from_a, r))
-                    if r < na - 1:
-                        pl.when(k == 2 * na - 2)(functools.partial(to_b, r))
+                turn(k, 1)
 
         @pl.when(k > 0)
         def _():
@@ -1461,20 +1712,19 @@
             weighted = (gate_col[window, 0:1] * rounded).astype(jnp.bfloat16)
             res_stage[other] = mul(picks, weighted, over_first).astype(jnp.bfloat16)
             pltpu.make_async_copy(res_stage.at[other], result_ref.at[source], res_sem.at[other]).start()
+        turn(k, 2)
         return carry
 
     lax.fori_loop(0, 2 * na, work, 0)
-    to_b(na - 1)
+    to_a(1)
+    to_b(0)
     for p in range(1, parts):
         for q in range(3):
             if p > 1 or q > 0:
                 pltpu.make_async_copy(stage, stage, stage_sem.at[0]).wait()
             stage[...] = sums[p][q].astype(jnp.bfloat16)
             pltpu.make_async_copy(stage, sent[p - 1].at[q], stage_sem.at[0]).start()
-    for r in range(1, na):
-        if r == na - 1:
-            to_b(0)
-        to_a(r)
+    to_a(3)
     chip = a * 2 + b
     sib_wait(chip)
     b_wait(0)
@@ -1550,17 +1800,6 @@
     return found[0], found[1], found[2], found[3:]
 
 
-def adam_update(weight, gradient, first, second, clip_scale, rate, decay):
-    clipped = gradient * clip_scale
-    first_new = BETA_ONE * first + (1.0 - BETA_ONE) * clipped
-    second_new = BETA_TWO * second + (1.0 - BETA_TWO) * clipped * clipped
-    corr_one = 1.0 - BETA_ONE**STEP
-    corr_two = 1.0 - BETA_TWO**STEP
-    stepped = first_new / corr_one / (jnp.sqrt(second_new / corr_two) + ADAM_EPS)
-    weight_new = weight - rate * (stepped + decay * weight)
-    return (weight_new, first_new, second_new, weight_new.astype(jnp.bfloat16))
-
-
 def per_device(
     tokens,
     cotangent,
@@ -1609,10 +1848,10 @@
         1,
         "gather_weights",
         [
-            (("tab", "abt"), [qkv_weight.astype(low), out_weight.astype(low), gain_columns]),
-            (("ab", "ba"), [cotangent]),
-            ("t", [in_own, out_own]),
-            (("tab", "atb"), [shared_in.astype(low), shout_own]),
+            (("tab", "abt"), [qkv_weight.astype(low), out_weight.astype(low), gain_columns], 1.0),
+            (("ab", "ba"), [cotangent], 0.92),
+            ("t", [in_own, out_own], 1.0),
+            (("tab", "atb"), [shared_in.astype(low), shout_own], 2.9),
         ],
     )
     qkv_low = qkv_low.reshape(width, 3 * width)
@@ -1635,13 +1874,14 @@
     )
     chips = ep_count // 2
     held = tok_count * width * 2 * (ep_count + 3 * chips + 12) + 9 * tp_count * expert_in.size
-    if Place(ep_count, tp_count).nb == 2 and held <= VMEM_MOST * 9 // 10:
+    place = Place(ep_count, tp_count)
+    if (place.na, place.nb) == (4, 2) and held <= VMEM_MOST * 9 // 10:
         result_part, routed_grad, own_grad, sent_grads = fused_experts(
             ep_count, tp_count, 3, normed_two, info_own, cot_all, ins_low, outs_low, capacity
         )
     else:
         normed_all, info_all = gather(
-            ep_count, tp_count, 2, "gather_tokens", [("ab", [normed_two, info_own])]
+            ep_count, tp_count, 2, "gather_tokens", [("ab", [normed_two, info_own], 1.0)]
         )
         info = lax.dynamic_index_in_dim(
             info_all.reshape(ep_count, 2, ep_count, tok_count),
@@ -1660,111 +1900,52 @@
         routed_grad, qkv_low, out_low, shin_low, shout_low, ep_count, tp_count, 9, "ab",
         result_part if lean else None, sent,
     )
-    gain_rows = jnp.pad(gain_grads[:2].T.astype(low), ((0, 0), (0, 126)))
+    own_gains = norm_gains.shape[1]
+    gain_rows = gain_grads[:2].astype(low).reshape(2, devices, own_gains).transpose(1, 0, 2)
+    gain_rows = jnp.pad(gain_rows, ((0, 0), (0, 14), (0, 128 - own_gains)))
 
     def by_owner(grad):
         return grad.reshape(devices, -1, grad.shape[1])
 
     scattered = [
-        (("abt", "tab"), [by_owner(qkv_grad), by_owner(out_grad), by_owner(gain_rows)]),
+        (("abt", "tab"), [by_owner(qkv_grad), by_owner(out_grad), gain_rows]),
         (("abt", "bta"), [by_owner(shin_grad), by_owner(shout_grad)]),
     ]
-    if not lean:
+    if lean:
+        routed, others = carried
+        qkv_part, out_part, gains_part, shin_part, shout_part, own_grad, norm = scatter_add(
+            ep_count, tp_count, 4, "scatter_weights", scattered, (own_grad, others)
+        )
+    else:
         scattered += [("ab", [result_part]), ("t", [sent])]
-    qkv_part, out_part, gains_part, shin_part, shout_part, *more = scatter_all(
-        ep_count, tp_count, (4, 6, 7, 8), "scatter_weights", scattered
-    )
-    routed, others = carried or more
-    for shift in range(tp_count - 1):
-        own_grad = own_grad + others[shift].astype(jnp.float32)
-    block_out = (base + routed).astype(low)
-    exin_part, exout_part = own_grad[None, :2], own_grad[2:]
-    extra = jnp.sum(own_grad * own_grad, axis=(0, 1))[None, :]
-    grad_norm = jnp.sqrt(
-        sum_of_squares(
+        qkv_part, out_part, gains_part, shin_part, shout_part, routed, others = scatter_all(
+            ep_count, tp_count, (4, 6, 7, 8), "scatter_weights", scattered
+        )
+        for shift in range(tp_count - 1):
+            own_grad = own_grad + others[shift].astype(jnp.float32)
+        extra = jnp.sum(own_grad * own_grad, axis=(0, 1))[None, :]
+        norm = sum_of_squares(
             ep_count, tp_count, 5, [qkv_part, out_part, gains_part, shin_part, shout_part], extra
         )
+        norm = jnp.broadcast_to(jnp.sqrt(norm), (8, 128))
+    grad_norm = norm[0, 0]
+    block_out = (base + routed).astype(low)
+    exin, exout, dense = adam_all(
+        norm,
+        own_grad,
+        (expert_in, expert_in_first, expert_in_second),
+        (expert_out, expert_out_first, expert_out_second),
+        [
+            (qkv_weight, qkv_first, qkv_second, qkv_part),
+            (out_weight, out_first, out_second, out_part),
+            (shared_in, shared_in_first, shared_in_second, shin_part),
+            (shared_out, shared_out_first, shared_out_second, shout_part),
+            (norm_gains, gains_first, gains_second, gains_part),
+        ],
     )
-    shout_part = shout_part[:group]
-    gains_part = gains_part[:, :2].T
-    clip_scale = jnp.minimum(1.0, CLIP_LEVEL / (grad_norm + 1e-06))
-    qkv_new, qkv_first_new, qkv_second_new, qkv_copy = adam_update(
-        qkv_weight, qkv_part, qkv_first, qkv_second, clip_scale, MATRIX_RATE, WEIGHT_DECAY
-    )
-    out_new, out_first_new, out_second_new, out_copy = adam_update(
-        out_weight, out_part, out_first, out_second, clip_scale, MATRIX_RATE, WEIGHT_DECAY
-    )
-    shin_new, shin_first_new, shin_second_new, shin_copy = adam_update(
-        shared_in,
-        shin_part,
-        shared_in_first,
-        shared_in_second,
-        clip_scale,
-        MATRIX_RATE,
-        WEIGHT_DECAY,
-    )
-    shout_new, shout_first_new, shout_second_new, shout_copy = adam_update(
-        shared_out,
-        shout_part,
-        shared_out_first,
-        shared_out_second,
-        clip_scale,
-        MATRIX_RATE,
-        WEIGHT_DECAY,
-    )
-    exin_new, exin_first_new, exin_second_new, exin_copy = adam_update(
-        expert_in,
-        exin_part,
-        expert_in_first,
-        expert_in_second,
-        clip_scale,
-        MATRIX_RATE,
-        WEIGHT_DECAY,
-    )
-    exout_new, exout_first_new, exout_second_new, exout_copy = adam_update(
-        expert_out,
-        exout_part,
-        expert_out_first,
-        expert_out_second,
-        clip_scale,
-        MATRIX_RATE,
-        WEIGHT_DECAY,
-    )
-    gains_new, gains_first_new, gains_second_new, gains_copy = adam_update(
-        norm_gains, gains_part, gains_first, gains_second, clip_scale, GAIN_RATE, 0.0
-    )
+    qkv_all, out_all, shin_all, shout_all, gains_all = dense
     return (
-        block_out,
-        tokens_grad,
-        grad_norm,
-        qkv_new,
-        qkv_first_new,
-        qkv_second_new,
-        qkv_copy,
-        out_new,
-        out_first_new,
-        out_second_new,
-        out_copy,
-        shin_new,
-        shin_first_new,
-        shin_second_new,
-        shin_copy,
-        shout_new,
-        shout_first_new,
-        shout_second_new,
-        shout_copy,
-        exin_new,
-        exin_first_new,
-        exin_second_new,
-        exin_copy,
-        exout_new,
-        exout_first_new,
-        exout_second_new,
-        exout_copy,
-        gains_new,
-        gains_first_new,
-        gains_second_new,
-        gains_copy,
+        block_out, tokens_grad, grad_norm, *qkv_all, *out_all, *shin_all, *shout_all, *exin, *exout, *gains_all
     )
 
 

time: 581 us -> 556 us (0.957)
  other arithmetic: 41.3 us -> 15.9 us
    convert_element_type x7 -> x0, other arithmetic: 22 us -> none  [adam_update(): return (weight_new, first_new, second_new, weight_new.astype(jnp.bfloat16))]
    pallas_call x1, Pallas kernels: 10.3 us -> 27.2 us  [adam_all(): pl.pallas_call(functools.partial(adam_kernel, inner, counts), grid=(steps...]
    pallas_call x1, Pallas kernels: 159 us -> 146 us  [fused_experts(): pl.pallas_call(functools.partial(fused_kernel, parts, ep_count, tp_count,...]
    reduce_sum x2 -> x0, other arithmetic: 8.98 us -> none  [the longest x1 7.69 us: per_device(): extra = jnp.sum(own_grad * own_grad, axis=(0, 1))[None, :]]
    pallas_call x1, Pallas kernels: 94.8 us -> 103 us  [scatter_add(): pl.pallas_call(functools.partial(scatter_kernel, ep_count, tp_count, tupl...]
    pallas_call x1, Pallas kernels: 150 us -> 144 us  [gather(): pl.pallas_call(functools.partial(gather_kernel, ep_count, tp_count, tuple...]
where the time goes in v4:
time: 556 us; the launch traced here: 549 us
  Pallas kernels  523 us (94%)
  other arithmetic  15.9 us (3%)
  local copies, waits for them, and re-layouts  9.02 us (2%)
    pallas_call x1, Pallas kernels, fused_experts(): pl.pallas_call(functools.partial(fused_kernel, parts, ep_count, tp_count,...  146 us
    pallas_call x1, Pallas kernels, gather(): pl.pallas_call(functools.partial(gather_kernel, ep_count, tp_count, tuple...  144 us
    pallas_call x1, Pallas kernels, scatter_add(): pl.pallas_call(functools.partial(scatter_kernel, ep_count, tp_count, tupl...  103 us
    pallas_call x1, Pallas kernels, dense_backward(): pl.pallas_call(functools.partial(backward_kernel, group, step, carried),...  88.6 us
    pallas_call x1, Pallas kernels, adam_all(): pl.pallas_call(functools.partial(adam_kernel, inner, counts), grid=(steps...  27.2 us
    pallas_call x1, Pallas kernels, attention_forward(): pl.pallas_call(forward_kernel, grid=(pairs,), in_specs=[whole(length, wid...  14.4 us

profile of v4, /device:TPU:0, one launch (start us, length us, event | category | flops | bytes accessed | tf_op | source)
XLA Modules:
  0.0 548.9 jit_solution(2416804297292106537)
XLA Ops:
  0.7 0.7 convert_element_type.50
  1.4 1.3 broadcast_in_dim.45.seg_row.refs_2_
  2.6 0.1 copy.70
  2.7 0.6 pad.18.refs_2_
  3.3 0.7 convert_reduce_fusion
  4.1 0.2 convolution_select_fusion
  4.3 0.6 maximum_bitcast_fusion.refs_1_
  5.0 0.9 convert_element_type.56
  5.9 0.6 pad.19.refs_7_
  6.5 1.6 convert_element_type.49.refs_1_
  8.1 1.4 broadcast_in_dim.46.seg_column.refs_3_
  9.6 0.0 copy-start
  9.6 1.8 convert_element_type.55.refs_6_
  11.3 1.8 convert_element_type.48.refs_0_
  13.2 2.8 bitcast_convert_fusion.refs_5_
  15.9 0.0 copy-done
  15.9 1.6 convert_bitcast_fusion.refs_4_.refs_3_
  17.5 143.5 %gather_weights.1 = (bf16[32,40,3840]{2,1,0:T(8,128)(2,1)}, bf16[32,40,1280]{2,1,0:T(8,128)(2,1)}, bf16[32,40,128]{2,1,0:T(8,128)(2,1)}, bf16[16,256,1280]{2,1,0...) custom-call(bf16[40,3840]{1,0:T(8,128)(2,1)} %convert_element_type.4, ...), custom_call_target="tpu_custom_call" | custom-call | tf_op jit(solution)/shard_map/gather_weights/pallas_call | solution.py:365
  161.1 1.1 copy.73
  162.2 0.6 pad_convert_fusion.gains.refs_4_
  162.8 14.4 %attention_forward.1 = (bf16[256,3840]{1,0:T(8,128)(2,1)}, bf16[256,1280]{1,0:T(8,128)(2,1)}, f32[256,1280]{1,0:T(8,128)}, bf16[256,1280]{1,0:T(8,128)(2,1)}) custom-call(bf16[256,1280]{1,0:T(8,128)(2,1)} %refs_0_.1, s32[8,256]{1,0:T(8,128)} %broadcast_in_dim.45.seg_row.refs_2_, s32[256,128]{1,0:T(8,128)} %broadcast_in_dim.46.seg_column.refs_3_, ...), custom_call_target="tpu_custom_call" | custom-call | tf_op jit(solution)/shard_map/attention_forward/pallas_call | solution.py:964
  177.2 146.2 %fused_experts.1 = (bf16[16,256,1280]{2,1,0:T(8,128)(2,1)}, f32[256,1280]{1,0:T(8,128)}, f32[3,448,1280]{2,1,0:T(8,128)}, bf16[3,448,1280]{2,1,0:T(8,128)(2,1)}) custom-call(bf16[256,1280]{1,0:T(8,128)(2,1)} %get-tuple-element.97.refs_0_.refs_10_, f32[32,256]{1,0:T(8,128)} %maximum_bitcast_fusion.refs_1_, bf16[16,256,1280]{2,1,0:T(8,128)(2,1)} %get-tuple-element.98.refs_2_, ...), custom_call_target="tpu_custom_call" | custom-call | tf_op jit(solution)/shard_map/fused_experts/pallas_call | solution.py:1789
  323.4 88.6 %dense_backward.1 = (f32[256,1280]{1,0:T(8,128)}, f32[256,1280]{1,0:T(8,128)}, f32[8,1280]{1,0:T(8,128)}, bf16[1280,3840]{1,0:T(8,128)(2,1)}, bf16[1280,1280]{1,...) custom-call(bf16[256,1280]{1,0:T(8,128)(2,1)} %refs_0_.1, ...), custom_call_target="tpu_custom_call" | custom-call | tf_op jit(solution)/shard_map/dense_backward/pallas_call | solution.py:1199
  412.0 2.7 add_convert_fusion
  414.7 0.8 slice.16
  415.5 0.1 reshape.146
  415.6 0.7 pad.22.refs_2_
  416.3 102.9 %scatter_weights.1 = (f32[40,3840]{1,0:T(8,128)}, f32[40,1280]{1,0:T(8,128)}, f32[16,128]{1,0:T(8,128)}, f32[40,1792]{1,0:T(8,128)}, f32[32,1280]{1,0:T(8,128)},...) custom-call(bf16[32,40,3840]{2,1,0:T(8,128)(2,1)} %bitcast.49, bf16[32,40,1280]{2,1,0:T(8,128)(2,1)} %bitcast.57, ...), custom_call_target="tpu_custom_call" | custom-call | tf_op jit(solution)/shard_map/scatter_weights/pallas_call | solution.py:833
  519.2 1.2 slice.12
  520.4 27.2 %adam.1 = (f32[896,1280]{1,0:T(8,128)}, f32[896,1280]{1,0:T(8,128)}, f32[896,1280]{1,0:T(8,128)}, bf16[896,1280]{1,0:T(8,128)(2,1)}, f32[448,1280]{1,0:T(8,128)}...) custom-call(f32[8,128]{1,0:T(8,128)} %get-tuple-element.116.refs_0_,, ...), custom_call_target="tpu_custom_call" | custom-call | tf_op jit(solution)/shard_map/adam/pallas_call | solution.py:1421
  547.6 0.0 copy-done.1
  547.6 1.1 copy.77
  (3 shorter events, 0.0 us)
Async XLA Ops:
  9.6 6.4 %copy-start = (f32[1,2,448,1280]{3,2,1,0:T(8,128)S(1)}, f32[1,2,448,1280]{3,2,1,0:T(8,128)}, u32[]{:S(2)}) copy-start(f32[1,2,448,1280]{3,2,1,0:T(8,128)} %param.47) | copy-start | bytes 13762564
  520.4 27.2 %copy-start.1 = (f32[256,1280]{1,0:T(8,128)S(1)}, f32[256,1280]{1,0:T(8,128)}, u32[]{:S(2)}) copy-start(f32[256,1280]{1,0:T(8,128)} %get-tuple-element.185) | copy-start | bytes 3932164

commit v5 on v4

--- a/solution.py
+++ b/solution.py
@@ -1347,91 +1347,41 @@
         ref[window] = value.astype(ref.dtype)
 
 
-def adam_kernel(first_blocks, dense_blocks, *refs):
-    dense = len(dense_blocks)
-    norm, grads = refs[:2]
-    inside, outside = refs[2:5], refs[5:8]
-    refs = refs[8:]
-    dense_in, refs = refs[: 4 * dense], refs[4 * dense :]
-    inside_new, outside_new, dense_new = refs[:4], refs[4:8], refs[8:]
-    at = pl.program_id(0)
+def adam_dense_kernel(count, norm, *refs):
     clip = jnp.minimum(1.0, CLIP_LEVEL / (norm[0:1, 0:1] + 1e-06))
-
-    def block(source, target):
-        def rows(i, carry):
-            window = (pl.ds(pl.multiple_of(i * 16, 16), 16), slice(None))
-            values = [ref[window] for ref in source]
-            adam_rows(values, (target, window), grads[window], clip, MATRIX_RATE, WEIGHT_DECAY)
+    for k in range(count):
+        source, grad = refs[4 * k : 4 * k + 3], refs[4 * k + 3]
+        target = refs[4 * (count + k) : 4 * (count + k) + 4]
+        rows, width = source[0].shape
+        if k == count - 1:
+            values = [ref[...] for ref in source]
+            window = (slice(None), slice(None))
+            adam_rows(values, (target, window), grad[:rows, :width], clip, GAIN_RATE, 0.0)
+            continue
+
+        def columns(i, carry, source=source, grad=grad, target=target, rows=rows):
+            some = pl.ds(pl.multiple_of(i * 256, 256), 256)
+            values = [ref[:, some] for ref in source]
+            adam_rows(values, (target, (slice(None), some)), grad[:rows, some], clip, MATRIX_RATE, WEIGHT_DECAY)
             return carry
 
-        lax.fori_loop(0, grads.shape[0] // 16, rows, 0)
-
-    pl.when(at < first_blocks)(lambda: block(inside, inside_new))
-    pl.when(at >= first_blocks)(lambda: block(outside, outside_new))
-
-    def one(k):
-        source, grad = dense_in[4 * k : 4 * k + 3], dense_in[4 * k + 3]
-        rows, width = source[0].shape
-        last = k == dense - 1
-        everything = (slice(None), slice(None))
-        adam_rows(
-            [ref[...] for ref in source],
-            (dense_new[4 * k : 4 * k + 4], everything),
-            grad[:rows, :width],
-            clip,
-            GAIN_RATE if last else MATRIX_RATE,
-            0.0 if last else WEIGHT_DECAY,
-        )
-
-    for k, count in enumerate(dense_blocks):
-        pl.when(at < count)(functools.partial(one, k))
-
-
-def adam_all(norm, grads, inside, outside, dense):
-    hidden, width = grads.shape[1:]
-    rows = hidden // 4 if hidden % 64 == 0 else hidden // 2
-    inner = 2 * hidden // rows
-    steps = 3 * hidden // rows
-
-    def blocks_of(columns):
-        return max(n for n in range(1, steps + 1) if columns % (128 * n) == 0 or n == 1)
-
-    counts = tuple(blocks_of(entry[0].shape[1]) for entry in dense)
-
-    def slab(array, count):
-        columns = array.shape[1] // count
-        return pl.BlockSpec((array.shape[0], columns), lambda i: (0, jnp.minimum(i, count - 1)))
-
-    first_spec = pl.BlockSpec((rows, width), lambda i: (jnp.minimum(i, inner - 1), 0))
-    second_spec = pl.BlockSpec((rows, width), lambda i: (jnp.maximum(i - inner, 0), 0))
-    flat = [a.reshape(2 * hidden, width) for a in inside] + [a.reshape(hidden, width) for a in outside]
+        lax.fori_loop(0, width // 256, columns, 0)
+
+
+def adam_dense(norm, dense):
     low, full = jnp.bfloat16, jnp.float32
-    kinds = (full, full, full, low)
-    out_shape = [jax.ShapeDtypeStruct((2 * hidden, width), kind) for kind in kinds]
-    out_shape += [jax.ShapeDtypeStruct((hidden, width), kind) for kind in kinds]
-    out_specs = [first_spec] * 4 + [second_spec] * 4
-    in_specs = [pl.BlockSpec(norm.shape, lambda i: (0, 0)), pl.BlockSpec((rows, width), lambda i: (i, 0))]
-    in_specs += [first_spec] * 3 + [second_spec] * 3
-    more = []
-    for entry, count in zip(dense, counts):
-        more += entry
-        in_specs += [slab(array, count) for array in entry]
-        out_specs += [slab(entry[0], count)] * 4
-        out_shape += [jax.ShapeDtypeStruct(entry[0].shape, kind) for kind in kinds]
+    more = [array for entry in dense for array in entry]
+    out_shape = [jax.ShapeDtypeStruct(e[0].shape, kind) for e in dense for kind in (full, full, full, low)]
+    inside = pl.BlockSpec(memory_space=pltpu.VMEM)
     found = pl.pallas_call(
-        functools.partial(adam_kernel, inner, counts),
-        grid=(steps,),
-        in_specs=in_specs,
-        out_specs=out_specs,
+        functools.partial(adam_dense_kernel, len(dense)),
+        in_specs=[inside] * (1 + len(more)),
+        out_specs=[inside] * len(out_shape),
         out_shape=out_shape,
-        compiler_params=pltpu.CompilerParams(
-            dimension_semantics=("arbitrary",), vmem_limit_bytes=VMEM_MOST
-        ),
-        name="adam",
-    )(norm, grads.reshape(3 * hidden, width), *flat, *more)
-    first = [a.reshape(inside[0].shape) for a in found[:4]]
-    second = [a.reshape(outside[0].shape) for a in found[4:8]]
-    return first, second, [found[8 + 4 * k : 12 + 4 * k] for k in range(len(dense))]
+        compiler_params=pltpu.CompilerParams(vmem_limit_bytes=VMEM_MOST),
+        name="adam_dense",
+    )(norm, *more)
+    return [found[4 * k : 4 * k + 4] for k in range(len(dense))]
 
 
 FROM_A = {1: (1, 0), 2: (2, 1), 3: (4, 1)}
@@ -1798,6 +1748,17 @@
         name="fused_experts",
     )(normed, info, cot_all, *ins, *outs_w)
     return found[0], found[1], found[2], found[3:]
+
+
+def adam_update(weight, gradient, first, second, clip_scale, rate, decay):
+    clipped = gradient * clip_scale
+    first_new = BETA_ONE * first + (1.0 - BETA_ONE) * clipped
+    second_new = BETA_TWO * second + (1.0 - BETA_TWO) * clipped * clipped
+    corr_one = 1.0 - BETA_ONE**STEP
+    corr_two = 1.0 - BETA_TWO**STEP
+    stepped = first_new / corr_one / (jnp.sqrt(second_new / corr_two) + ADAM_EPS)
+    weight_new = weight - rate * (stepped + decay * weight)
+    return (weight_new, first_new, second_new, weight_new.astype(jnp.bfloat16))
 
 
 def per_device(
@@ -1930,11 +1891,15 @@
         norm = jnp.broadcast_to(jnp.sqrt(norm), (8, 128))
     grad_norm = norm[0, 0]
     block_out = (base + routed).astype(low)
-    exin, exout, dense = adam_all(
+    clip_scale = jnp.minimum(1.0, CLIP_LEVEL / (grad_norm + 1e-06))
+    exin = adam_update(
+        expert_in, own_grad[None, :2], expert_in_first, expert_in_second, clip_scale, MATRIX_RATE, WEIGHT_DECAY
+    )
+    exout = adam_update(
+        expert_out, own_grad[2:], expert_out_first, expert_out_second, clip_scale, MATRIX_RATE, WEIGHT_DECAY
+    )
+    dense = adam_dense(
         norm,
-        own_grad,
-        (expert_in, expert_in_first, expert_in_second),
-        (expert_out, expert_out_first, expert_out_second),
         [
             (qkv_weight, qkv_first, qkv_second, qkv_part),
             (out_weight, out_first, out_second, out_part),

time: 556 us -> 554 us (level)
  Pallas kernels: 523 us -> 502 us
  other arithmetic: 15.9 us -> 33.2 us
    pallas_call x1, Pallas kernels: 27.2 us -> 6.58 us  [adam_dense(): pl.pallas_call(functools.partial(adam_dense_kernel, len(dense)), in_specs...]
    convert_element_type x0 -> x2, other arithmetic: none -> 17.4 us  [adam_update(): return (weight_new, first_new, second_new, weight_new.astype(jnp.bfloat16))]
where the time goes in v5:
time: 554 us; the launch traced here: 548 us
  Pallas kernels  502 us (91%)
  other arithmetic  33.2 us (6%)
  local copies, waits for them, and re-layouts  10.3 us (2%)
    pallas_call x1, Pallas kernels, fused_experts(): pl.pallas_call(functools.partial(fused_kernel, parts, ep_count, tp_count,...  146 us
    pallas_call x1, Pallas kernels, gather(): pl.pallas_call(functools.partial(gather_kernel, ep_count, tp_count, tuple...  144 us
    pallas_call x1, Pallas kernels, scatter_add(): pl.pallas_call(functools.partial(scatter_kernel, ep_count, tp_count, tupl...  103 us
    pallas_call x1, Pallas kernels, dense_backward(): pl.pallas_call(functools.partial(backward_kernel, group, step, carried),...  88.5 us
    convert_element_type x2, other arithmetic, adam_update(): return (weight_new, first_new, second_new, weight_new.astype(jnp.bfloat16))  17.4 us
    pallas_call x1, Pallas kernels, attention_forward(): pl.pallas_call(forward_kernel, grid=(pairs,), in_specs=[whole(length, wid...  14.4 us

profile of v5, /device:TPU:0, one launch (start us, length us, event | category | flops | bytes accessed | tf_op | source)
XLA Modules:
  0.0 547.5 jit_solution(3743724518571789744)
XLA Ops:
  0.7 0.7 convert_element_type.58
  1.4 1.3 broadcast_in_dim.46.seg_row.refs_2_
  2.6 0.1 copy.70
  2.7 0.6 pad.18.refs_2_
  3.3 0.7 convert_reduce_fusion
  4.1 0.2 convolution_select_fusion
  4.3 0.6 maximum_bitcast_fusion.refs_1_
  5.0 0.9 convert_element_type.65
  5.9 0.6 pad.19.refs_7_
  6.5 1.6 convert_element_type.57.refs_1_
  8.1 1.4 broadcast_in_dim.47.seg_column.refs_3_
  9.6 1.8 convert_element_type.64.refs_6_
  11.3 1.8 convert_element_type.56.refs_0_
  13.2 2.8 convert_bitcast_fusion.1.refs_5_
  15.9 1.6 convert_bitcast_fusion.refs_4_.refs_3_
  17.5 143.5 %gather_weights.1 = (bf16[32,40,3840]{2,1,0:T(8,128)(2,1)}, bf16[32,40,1280]{2,1,0:T(8,128)(2,1)}, bf16[32,40,128]{2,1,0:T(8,128)(2,1)}, bf16[16,256,1280]{2,1,0...) custom-call(bf16[40,3840]{1,0:T(8,128)(2,1)} %convert_element_type.5, ...), custom_call_target="tpu_custom_call" | custom-call | tf_op jit(solution)/shard_map/gather_weights/pallas_call | solution.py:365
  161.1 1.1 copy.73
  162.2 0.6 pad_convert_fusion.gains.refs_4_
  162.8 14.4 %attention_forward.1 = (bf16[256,3840]{1,0:T(8,128)(2,1)}, bf16[256,1280]{1,0:T(8,128)(2,1)}, f32[256,1280]{1,0:T(8,128)}, bf16[256,1280]{1,0:T(8,128)(2,1)}) custom-call(bf16[256,1280]{1,0:T(8,128)(2,1)} %refs_0_.2, s32[8,256]{1,0:T(8,128)} %broadcast_in_dim.46.seg_row.refs_2_, s32[256,128]{1,0:T(8,128)} %broadcast_in_dim.47.seg_column.refs_3_, ...), custom_call_target="tpu_custom_call" | custom-call | tf_op jit(solution)/shard_map/attention_forward/pallas_call | solution.py:964
  177.2 146.2 %fused_experts.1 = (bf16[16,256,1280]{2,1,0:T(8,128)(2,1)}, f32[256,1280]{1,0:T(8,128)}, f32[3,448,1280]{2,1,0:T(8,128)}, bf16[3,448,1280]{2,1,0:T(8,128)(2,1)}) custom-call(bf16[256,1280]{1,0:T(8,128)(2,1)} %get-tuple-element.89.refs_0_.refs_10_, f32[32,256]{1,0:T(8,128)} %maximum_bitcast_fusion.refs_1_, bf16[16,256,1280]{2,1,0:T(8,128)(2,1)} %get-tuple-element.90.refs_2_, ...), custom_call_target="tpu_custom_call" | custom-call | tf_op jit(solution)/shard_map/fused_experts/pallas_call | solution.py:1739
  323.4 88.5 %dense_backward.1 = (f32[256,1280]{1,0:T(8,128)}, f32[256,1280]{1,0:T(8,128)}, f32[8,1280]{1,0:T(8,128)}, bf16[1280,3840]{1,0:T(8,128)(2,1)}, bf16[1280,1280]{1,...) custom-call(bf16[256,1280]{1,0:T(8,128)(2,1)} %refs_0_.2, ...), custom_call_target="tpu_custom_call" | custom-call | tf_op jit(solution)/shard_map/dense_backward/pallas_call | solution.py:1199
  411.9 2.7 add_convert_fusion
  414.6 0.8 slice.34
  415.4 0.1 reshape.108
  415.5 0.7 pad.22.refs_2_
  416.2 102.9 %scatter_weights.1 = (f32[40,3840]{1,0:T(8,128)}, f32[40,1280]{1,0:T(8,128)}, f32[16,128]{1,0:T(8,128)}, f32[40,1792]{1,0:T(8,128)}, f32[32,1280]{1,0:T(8,128)},...) custom-call(bf16[32,40,3840]{2,1,0:T(8,128)(2,1)} %bitcast.44, bf16[32,40,1280]{2,1,0:T(8,128)(2,1)} %bitcast.50, ...), custom_call_target="tpu_custom_call" | custom-call | tf_op jit(solution)/shard_map/scatter_weights/pallas_call | solution.py:833
  519.1 1.2 slice.18
  521.0 6.6 %adam_dense.1 = (f32[40,3840]{1,0:T(8,128)}, f32[40,3840]{1,0:T(8,128)}, f32[40,3840]{1,0:T(8,128)}, bf16[40,3840]{1,0:T(8,128)(2,1)}, f32[40,1280]{1,0:T(8,128)...) custom-call(f32[8,128]{1,0:T(8,128)} %get-tuple-element.108.norm, ...), custom_call_target="tpu_custom_call" | custom-call | tf_op jit(solution)/shard_map/adam_dense/pallas_call | solution.py:1376
  527.6 8.0 %fusion.11 = (bf16[1,448,1280]{2,1,0:T(8,128)(2,1)}, f32[1,448,1280]{2,1,0:T(8,128)}, f32[1,448,1280]{2,1,0:T(8,128)}, f32[1,448,1280]{2,1,0:T(8,128)}) fusion(f32[1,448,1280]{2,1,0:T(8,128)S(1)} %copy-done.1, f32[]{:T(128)S(6)} %min.3, f32[3,448,1280]{2,1,0:T(8,128)} %get-tuple-element.130, f32[1,448,1280]{2,1,0:T(8,128)} %param.51, f32[1,448,1280]{2,1,0:T(8,128)} %param.52), kind=kLoop, calls=%fused_computation.31 | loop fusion | flops 9748480 | bytes 17203204 | tf_op jit(solution)/shard_map/convert_element_type | solution.py:1761
  535.6 1.2 slice-done.3
  536.8 9.4 %fusion.13 = (bf16[1,2,448,1280]{3,2,1,0:T(8,128)(2,1)}, f32[1,2,448,1280]{3,2,1,0:T(8,128)}, f32[1,2,448,1280]{3,2,1,0:T(8,128)}, f32[1,2,448,1280]{3,2,1,0:T(8,128)}) fusion(f32[1,2,448,1280]{3,2,1,0:T(8,128)S(1)} %bitcast.41, f32[]{:T(128)S(6)} %min.3, f32[3,448,1280]{2,1,0:T(8,128)S(1)} %bitcast.46, f32[1,2,448,1280]{3,2,1,0:T(8,128)} %param.48, ...), kind=kLoop, calls=%fused_computation.32 | loop fusion | flops 19496960 | bytes 34406404 | tf_op jit(solution)/shard_map/convert_element_type | solution.py:1761
  546.2 1.1 copy.77
  (17 shorter events, 0.1 us)
Async XLA Ops:
  9.6 6.4 %copy-start = (f32[1,2,448,1280]{3,2,1,0:T(8,128)S(1)}, f32[1,2,448,1280]{3,2,1,0:T(8,128)}, u32[]{:S(2)}) copy-start(f32[1,2,448,1280]{3,2,1,0:T(8,128)} %param.47) | copy-start | bytes 13762564
  521.0 6.6 %copy-start.1 = (f32[1,448,1280]{2,1,0:T(8,128)S(1)}, f32[1,448,1280]{2,1,0:T(8,128)}, u32[]{:S(2)}) copy-start(f32[1,448,1280]{2,1,0:T(8,128)} %param.50) | copy-start | bytes 6881284
  527.6 8.0 %slice-start = ((s8[4587520]{0:T(1024)(128)(4,1)}), s8[4194304]{0:T(1024)(128)(4,1)S(1)}, s32[]{:S(2)}) async-start(s8[4587520]{0:T(1024)(128)(4,1)} %bitcast.40), calls=%async_computation | async-start | bytes 8388608
  527.6 8.0 %slice-start.2 = ((s8[6881280]{0:T(1024)(128)(4,1)}), s8[4194304]{0:T(1024)(128)(4,1)S(1)}, s32[]{:S(2)}) async-start(s8[6881280]{0:T(1024)(128)(4,1)} %bitcast.45), calls=%async_computation.2 | async-start | bytes 8388608
  527.6 8.0 %slice-start.1 = ((s8[4587520]{0:T(1024)(128)(4,1)}), s8[393216]{0:T(1024)(128)(4,1)S(1)}, s32[]{:S(2)}) async-start(s8[4587520]{0:T(1024)(128)(4,1)} %bitcast.40), calls=%async_computation.1 | async-start | bytes 786432
  527.6 9.2 %slice-start.3 = ((s8[6881280]{0:T(1024)(128)(4,1)}), s8[2686976]{0:T(1024)(128)(4,1)S(1)}, s32[]{:S(2)}) async-start(s8[6881280]{0:T(1024)(128)(4,1)} %bitcast.45), calls=%async_computation.3 | async-start | bytes 5373952
  536.8 9.4 %copy-start.2 = (f32[256,1280]{1,0:T(8,128)S(1)}, f32[256,1280]{1,0:T(8,128)}, u32[]{:S(2)}) copy-start(f32[256,1280]{1,0:T(8,128)} %get-tuple-element.177) | copy-start | bytes 3932164
